TPU v7x, 256 devices: a whole 4x4x8 slice. The times are simulated.
256 devices in a mesh: seq: 64 (over y_hi, x, z), head: 4 (over y_lo, core).
Axes of the slice: x: 4, y: 4 (y_hi: 2, y_lo: 2; y = y_hi * 2 + y_lo), z: 8, core: 2. Of those that a mesh axis runs over, the one named last changes fastest.
Arguments:
- queries: bfloat16 [16384, 1024], P('seq', 'head'), may hold values from -40 to 40
- keys: bfloat16 [16384, 1024], P('seq', 'head'), may hold values from -12 to 12
- values: bfloat16 [16384, 1024], P('seq', 'head'), may hold values from -6 to 6
- residual: bfloat16 [16384, 1024], P('seq', 'head'), may hold values from -3 to 3
- reg_weight: bfloat16 [1024, 1024], P('head'), may hold values from -0.1875 to 0.1875
- targets: bfloat16 [256, 16, 1024], P('seq'), may hold values from -3 to 3
- block_track: int32 [128], replicated, may hold values from 0 to 255
- row_count: int32 [128], P('seq'), may hold values from 1 to 128, 12288 in all
- pool_slot: int32 [128, 128], P('seq'), may hold values from 0 to 15
Outputs:
- grad_reg: bfloat16 [1024, 1024], P('head')
- context_grad: bfloat16 [16384, 1024], P('seq', 'head')
All inputs are finite; a program needn't handle non-finite values. No bound on the sum of `row_count` on one device may be relied on, other than what follows from the above.
Results may differ from a plain program's by a relative error of at most 0.019.
Values may be sent and summed in bfloat16 or wider, within the bound.
No kernel may reach another device: no remote copies, remote signals or barrier semaphores. Data moves between devices by JAX's collectives and lax.ppermute only.
A program may use at most 128 MiB of HBM per device.

v0:
```python
import jax
import jax.numpy as jnp
from jax import lax
from jax.sharding import PartitionSpec as P

HEAD_DIM = 64
BLK = 128
POOL = 16


def make_advance(query_heads, scale):

    def advance(state, block):
        run_max, run_total, run_sum = state
        key_rows, value_rows = block
        scores = (
            jnp.einsum("qhd,khd->hqk", query_heads, key_rows, preferred_element_type=jnp.float32)
            * scale
        )
        new_max = jnp.maximum(run_max, jnp.max(scores, axis=2))
        shrink = jnp.exp(run_max - new_max)
        exp_terms = jnp.exp(scores - new_max[:, :, None])
        run_total = run_total * shrink + jnp.sum(exp_terms, axis=2)
        weighted = jnp.einsum(
            "hqk,khd->hqd",
            exp_terms.astype(jnp.bfloat16),
            value_rows,
            preferred_element_type=jnp.float32,
        )
        run_sum = run_sum * shrink[:, :, None] + weighted
        return ((new_max, run_total, run_sum), None)

    return advance


def local(queries, keys, values, residual, reg_weight, targets, block_track, row_count, pool_slot):
    tok_rows, width = queries.shape
    head_count = width // HEAD_DIM
    query_heads = queries.reshape(tok_rows, head_count, HEAD_DIM)
    advance = make_advance(query_heads, HEAD_DIM ** (-0.5))
    initial = (
        jnp.full((head_count, tok_rows), -1e30, jnp.float32),
        jnp.zeros((head_count, tok_rows), jnp.float32),
        jnp.zeros((head_count, tok_rows, HEAD_DIM), jnp.float32),
    )
    state = initial
    key_piece = lax.all_gather(keys, "seq", axis=0, tiled=True)
    value_piece = lax.all_gather(values, "seq", axis=0, tiled=True)
    key_count = key_piece.shape[0]
    key_heads = key_piece.reshape(key_count, head_count, HEAD_DIM)
    value_heads = value_piece.reshape(key_count, head_count, HEAD_DIM)
    block_count = key_count // 512
    blocks = (
        key_heads.reshape(block_count, 512, head_count, HEAD_DIM),
        value_heads.reshape(block_count, 512, head_count, HEAD_DIM),
    )
    state, unused = lax.scan(advance, state, blocks)
    run_max, run_total, run_sum = state
    context = (
        (run_sum / run_total[:, :, None])
        .transpose(1, 0, 2)
        .reshape(tok_rows, width)
        .astype(jnp.bfloat16)
    )
    stream = (residual.astype(jnp.float32) + context.astype(jnp.float32)).astype(jnp.bfloat16)
    block_here = tok_rows // BLK
    owned = 2 * block_here
    seq_count = lax.axis_size("seq")
    tracks_all = owned * seq_count
    seq_index = lax.axis_index("seq")
    stream_blocks = stream.reshape(block_here, BLK, width)
    valid = jnp.arange(BLK, dtype=jnp.int32)[None, :] < row_count[:, None]
    match = pool_slot[:, None, :] == jnp.arange(POOL, dtype=jnp.int32)[None, :, None]
    selector = jnp.where(match & valid[:, None, :], 1.0, 0.0).astype(jnp.bfloat16)
    pooled = jnp.einsum("bpr,brc->bpc", selector, stream_blocks, preferred_element_type=jnp.float32)
    slot_rows = jnp.sum(selector.astype(jnp.float32), axis=2)
    own_track = lax.dynamic_slice_in_dim(block_track, seq_index * block_here, block_here)
    track_select = jnp.where(
        own_track[:, None] == jnp.arange(tracks_all, dtype=jnp.int32)[None, :], 1.0, 0.0
    ).astype(jnp.float32)
    dense_sums = jnp.einsum("bt,bpc->tpc", track_select, pooled, precision=lax.Precision.HIGHEST)
    dense_counts = jnp.einsum("bt,bp->tp", track_select, slot_rows, precision=lax.Precision.HIGHEST)
    sums, counts = (
        lax.psum_scatter(dense_sums, "seq", scatter_dimension=0, tiled=True),
        lax.psum_scatter(dense_counts, "seq", scatter_dimension=0, tiled=True),
    )
    divisor = jnp.maximum(counts, 1.0)
    mean = (sums / divisor[:, :, None]).astype(jnp.bfloat16).reshape(owned * POOL, width)
    partial_pred = jnp.dot(mean, reg_weight, preferred_element_type=jnp.float32)
    prediction = lax.psum(partial_pred.astype(jnp.bfloat16), "head").astype(jnp.float32)
    error = (prediction - targets.reshape(owned * POOL, -1).astype(jnp.float32)).astype(
        jnp.bfloat16
    )
    reg_part = lax.dot_general(
        mean, error, (((0,), (0,)), ((), ())), preferred_element_type=jnp.float32
    )
    mean_grad = lax.dot_general(
        error, reg_weight, (((1,), (1,)), ((), ())), preferred_element_type=jnp.float32
    )
    track_grad = (mean_grad.reshape(owned, POOL, width) / divisor[:, :, None]).astype(jnp.bfloat16)
    every_grad = lax.all_gather(track_grad, "seq", axis=0, tiled=True)
    grad_select = jnp.where(
        own_track[:, None] == jnp.arange(tracks_all, dtype=jnp.int32)[None, :], 1.0, 0.0
    ).astype(jnp.bfloat16)
    pooled_grad = jnp.einsum(
        "bt,tpc->bpc", grad_select, every_grad, preferred_element_type=jnp.float32
    ).astype(jnp.bfloat16)
    row_grad = jnp.einsum("bpr,bpc->brc", selector, pooled_grad, preferred_element_type=jnp.float32)
    context_grad = row_grad.reshape(tok_rows, width).astype(jnp.bfloat16)
    grad_reg = lax.psum(reg_part, "seq").astype(jnp.bfloat16)
    return (grad_reg, context_grad)


def solution(mesh):
    return jax.shard_map(
        local,
        mesh=mesh,
        in_specs=(
            P("seq", "head"),
            P("seq", "head"),
            P("seq", "head"),
            P("seq", "head"),
            P("head", None),
            P("seq", None, None),
            P(),
            P("seq"),
            P("seq", None),
        ),
        out_specs=(P("head", None), P("seq", "head")),
        check_vma=False,
    )
```

profile of v0, /device:TPU:2, one launch (start us, length us, event | category | flops | bytes accessed | tf_op | source)
XLA Modules:
  0.0 1237.1 jit_solution(4644142932304192094)
XLA Ops:
  11.2 150.7 %all-gather.4.cloned.1.call-done = bf16[16384,256]{1,0:T(8,128)(2,1)} async-done(((bf16[256,256]{1,0:T(8,128)(2,1)}), bf16[16384,256]{1,0:T(8,128)(2,1)}) %all-gather.4.cloned.1.call-update) | async-done | bytes 8388624 | tf_op jit(solution)/shard_map/all_gather | solution.py:47
  161.9 24.5 %reshape.56 = bf16[32,512,4,64]{3,2,1,0:T(4,128)(2,1)} reshape(bf16[16384,256]{1,0:T(8,128)(2,1)} %all-gather.4.cloned.1.call-done) | data formatting | bytes 16777216 | tf_op jit(solution)/shard_map/reshape;reshape | solution.py:54
  186.4 24.2 %copy.29 = bf16[32,512,4,64]{1,3,2,0:T(8,128)(2,1)} copy(bf16[32,512,4,64]{3,2,1,0:T(4,128)(2,1)} %reshape.56) | data formatting | bytes 16777216
  210.6 99.0 %all-gather.6.cloned.1.call-done = bf16[16384,256]{1,0:T(8,128)(2,1)} async-done(((bf16[256,256]{1,0:T(8,128)(2,1)}), bf16[16384,256]{1,0:T(8,128)(2,1)}) %all-gather.6.cloned.1.call-update) | async-done | bytes 8388624 | tf_op jit(solution)/shard_map/all_gather | solution.py:48
  309.6 24.5 %reshape.57 = bf16[32,512,4,64]{3,2,1,0:T(4,128)(2,1)} reshape(bf16[16384,256]{1,0:T(8,128)(2,1)} %all-gather.6.cloned.1.call-done) | data formatting | bytes 16777216 | tf_op jit(solution)/shard_map/reshape;reshape | solution.py:55
  334.1 24.2 %copy.30 = bf16[32,512,4,64]{1,3,2,0:T(8,128)(2,1)} copy(bf16[32,512,4,64]{3,2,1,0:T(4,128)(2,1)} %reshape.57) | data formatting | bytes 16777216
  358.3 107.5 %while.15 = (s32[]{:T(128)}, f32[4,256]{1,0:T(4,128)S(1)}, f32[4,256]{1,0:T(4,128)S(1)}, f32[4,256,64]{1,2,0:T(8,128)S(1)}, bf16[32,512,4,64]{1,3,2,0:T(8,128)(2...) while((s32[]{:T(128)}, f32[4,256]{1,0:T(4,128)S(1)}, ...), condition=%wide.region_3.4_spmd.clone, body=%wide.region_0.3_spmd.clone.sunk | while | flops 138613760 | bytes 7537769 | solution.py:57
  358.3 1.5 bitcast_reduce_fusion.2
  360.2 1.5 convolution_add_fusion.2
  363.6 1.5 convolution_add_fusion.2
  367.0 1.5 convolution_add_fusion.2
  370.3 1.5 convolution_add_fusion.2
  373.7 1.5 convolution_add_fusion.2
  377.0 1.5 convolution_add_fusion.2
  380.4 1.5 convolution_add_fusion.2
  383.8 1.5 convolution_add_fusion.2
  387.1 1.5 convolution_add_fusion.2
  390.5 1.5 convolution_add_fusion.2
  393.8 1.5 convolution_add_fusion.2
  397.2 1.5 convolution_add_fusion.2
  400.6 1.5 convolution_add_fusion.2
  403.9 1.5 convolution_add_fusion.2
  407.3 1.5 convolution_add_fusion.2
  410.6 1.5 convolution_add_fusion.2
  414.0 1.5 convolution_add_fusion.2
  466.3 3.8 fusion.22
  470.0 4.4 copy.33
  476.8 333.4 %all-reduce = f32[256,16]{1,0:T(8,128)S(1)} all-reduce(f32[256,16]{1,0:T(8,128)S(1)} %fusion.37), channel_id=3, replica_groups=mesh['seq'=64,'head'=4] {'seq'}, use_global_device_ids=true, to_apply=%region_6.7.clone | all-reduce | flops 4096 | bytes 32768
  810.2 10.1 reduce-scatter.2.cloned.1.call-done
  822.1 56.1 %all-reduce.4.cloned.1.call-done = bf16[64,1024]{1,0:T(8,128)(2,1)} async-done(((bf16[64,1024]{1,0:T(8,128)(2,1)}), bf16[64,1024]{1,0:T(8,128)(2,1)}) %all-reduce.4.cloned.1.call-update) | async-done | bytes 131088 | tf_op jit(solution)/shard_map/psum | solution.py:90
  880.5 347.0 %all-reduce.5 = bf16[256,1024]{1,0:T(8,128)(2,1)} all-reduce(f32[256,1024]{1,0:T(8,128)S(1)} %fusion.59), channel_id=1, replica_groups=mesh['seq'=64,'head'=4] {'seq'}, use_global_device_ids=true, to_apply=%region_8.9 | all-reduce | flops 262144 | bytes 1572864 | tf_op jit(solution)/shard_map/psum | solution.py:110
  1227.4 2.3 fusion.17
  (216 shorter events, 90.6 us)
Async XLA Ops:
  7.2 814.0 %copy-start = (bf16[256,1024]{1,0:T(8,128)(2,1)S(1)}, bf16[256,1024]{1,0:T(8,128)(2,1)}, u32[]{:S(2)}) copy-start(bf16[256,1024]{1,0:T(8,128)(2,1)} %param.15) | copy-start | bytes 1572868
  7.2 154.7 %all-gather.4.cloned.1.call-start = ((), (), s32[]{:S(2)}) async-start(), calls=%async_computation.1 | async-start | bytes 8519680 | tf_op jit(solution)/shard_map/all_gather | solution.py:47
  7.9 301.7 %all-gather.6.cloned.1.call-start = ((), (), s32[]{:S(2)}) async-start(), calls=%async_computation.2 | async-start | bytes 8519680 | tf_op jit(solution)/shard_map/all_gather | solution.py:48
  8.7 811.6 %reduce-scatter.2.cloned.1.call-start = ((), (), s32[]{:S(2)}) async-start(), calls=%async_computation.3 | async-start | bytes 4259840 | tf_op jit(solution)/shard_map/reduce_scatter | solution.py:84
  358.3 107.7 %copy-start.2 = (bf16[256,256]{1,0:T(8,128)(2,1)S(1)}, bf16[256,256]{1,0:T(8,128)(2,1)}, u32[]{:S(2)}) copy-start(bf16[256,256]{1,0:T(8,128)(2,1)} %param.14) | copy-start | bytes 393220
  358.3 107.8 %copy-start.3 = (s32[2,128]{1,0:T(2,128)S(1)}, s32[2,128]{1,0:T(2,128)}, u32[]{:S(2)}) copy-start(s32[2,128]{1,0:T(2,128)} %param.19) | copy-start | bytes 3076
  474.4 0.7 copy-start.4
  474.4 403.8 %copy-start.1 = (bf16[4,16,1024]{2,1,0:T(8,128)(2,1)S(1)}, bf16[4,16,1024]{2,1,0:T(8,128)(2,1)}, u32[]{:S(2)}) copy-start(bf16[4,16,1024]{2,1,0:T(8,128)(2,1)} %param.16) | copy-start | bytes 393220
  474.4 403.8 %all-reduce.4.cloned.1.call-start = ((), (), s32[]{:S(2)}) async-start(), calls=%async_computation.4 | async-start | bytes 262144 | tf_op jit(solution)/shard_map/psum | solution.py:90
  822.1 405.4 %all-gather.8.cloned.1.call-start = ((), (), s32[]{:S(2)}) async-start(), calls=%async_computation.5 | async-start | bytes 2129920 | tf_op jit(solution)/shard_map/all_gather | solution.py:101
Sparse Core Ops, SparseCore 0:
  11.7 150.1 all-gather.3
  165.5 144.0 all-gather.5
  474.5 345.6 reduce-scatter.1
  823.5 54.7 all-reduce.3
  882.4 118.9 all-gather.7
where the time goes:
time: 1260 us; the launch traced here: 1240 us
  blocking collectives  680 us (54%)
  waiting for transfers between devices  317 us (25%)
  local copies, waits for them, and re-layouts  105 us (8%)
  matrix products  102 us (8%)
  other arithmetic  15.8 us (1%)
  between operations  14.6 us (1%)
    psum x1, blocking collectives, local(): grad_reg = lax.psum(reg_part, 'seq').astype(jnp.bfloat16)  347 us
    unnamed x1, blocking collectives  333 us
    all_gather x1, waiting for transfers between devices, local(): key_piece = lax.all_gather(keys, 'seq', axis=0, tiled=True)  151 us
    all_gather x1, waiting for transfers between devices, local(): value_piece = lax.all_gather(values, 'seq', axis=0, tiled=True)  99 us
    psum x1, waiting for transfers between devices, local(): lax.psum(partial_pred.astype(jnp.bfloat16), 'head').astype(jnp.float32)  56.1 us
    unnamed x14, local copies, waits for them, and re-layouts  50.6 us
    dot_general x32, matrix products, advance(): jnp.einsum('hqk,khd->hqd', exp_terms.astype(jnp.bfloat16), value_rows, pr...  46.9 us
    dot_general x32, matrix products, advance(): jnp.einsum('qhd,khd->hqk', query_heads, key_rows, preferred_element_type=...  46.6 us
  transfers between devices with their start and end apart: 5, of which 4 were waited for; matrix products, arithmetic and copies ran while one was open for 4% of the time, Pallas kernels for 0%

commit v1 on v0

v1 whole, which is shorter than its diff:
```python
import jax
import jax.numpy as jnp
from jax import lax
from jax.experimental import pallas as pl
from jax.experimental.pallas import tpu as pltpu
from jax.sharding import PartitionSpec as P

HEAD_DIM = 64
BLK = 128
POOL = 16
SIDE = 8
LOG2E = 1.4426950408889634
STAT = 16

GROUP_Z = [[g * SIDE + i for i in range(SIDE)] for g in range(SIDE)]
GROUP_YX = [[g * SIDE + i for g in range(SIDE)] for i in range(SIDE)]


def spread(x, groups):
    wide = jnp.broadcast_to(x[None], (SIDE, *x.shape))
    return lax.all_to_all(wide, "seq", 0, 0, axis_index_groups=groups)


def attend_kernel(q_ref, k_ref, v_ref, o_ref, k_own, v_own):
    rows = q_ref.shape[0]
    lane = lax.broadcasted_iota(jnp.int32, (1, 128), 1)
    first = lane < HEAD_DIM

    @pl.when(pl.program_id(1) == 0)
    def _():
        zero = jnp.zeros((), jnp.bfloat16)
        one = jnp.ones((), jnp.bfloat16)
        k = k_ref[...]
        v = v_ref[...]
        k_own[0] = jnp.where(first, k, zero)
        k_own[1] = jnp.where(first, zero, k)
        v_own[0] = jnp.where(first, v, one)
        v_own[1] = jnp.where(first, one, v)

    scale = LOG2E * HEAD_DIM ** (-0.5)
    q = q_ref[...]
    tops, sums = [], []
    for h in range(2):
        s = lax.dot_general(
            q, k_own[h], (((1,), (1,)), ((), ())), preferred_element_type=jnp.float32
        )
        top = jnp.max(s, axis=1, keepdims=True)
        p = jnp.exp2((s - top) * scale).astype(jnp.bfloat16)
        sums.append(jnp.dot(p, v_own[h], preferred_element_type=jnp.float32))
        tops.append(top * scale)
    num = jnp.where(first, sums[0], sums[1])
    den_other = jnp.where(first, sums[1], sums[0])
    den = pltpu.roll(den_other, HEAD_DIM, 1)
    o_ref[0, :rows] = (num / den).astype(jnp.bfloat16)
    lse = jnp.where(first, tops[1], tops[0]) + jnp.log2(den_other)
    turned = lse.T
    left = jnp.concatenate([turned[HEAD_DIM : HEAD_DIM + 1], turned[0:1]], axis=0)
    left = jnp.concatenate([left[:, :128], left[:, 128:]], axis=0)
    hi = left.astype(jnp.bfloat16)
    rest = left - hi.astype(jnp.float32)
    mid = rest.astype(jnp.bfloat16)
    rest = rest - mid.astype(jnp.float32)
    pad = jnp.zeros_like(left)
    o_ref[0, rows:] = jnp.concatenate(
        [hi.astype(jnp.float32), mid.astype(jnp.float32), rest, pad], axis=0
    ).astype(jnp.bfloat16)


def attend(queries, keys, values):
    n, width = queries.shape
    rows = n // SIDE
    keys_n = keys.shape[0]
    pairs = width // 128
    return pl.pallas_call(
        attend_kernel,
        grid=(pairs, SIDE),
        in_specs=[
            pl.BlockSpec((rows, 128), lambda p, i: (i, p)),
            pl.BlockSpec((keys_n, 128), lambda p, i: (0, p)),
            pl.BlockSpec((keys_n, 128), lambda p, i: (0, p)),
        ],
        out_specs=pl.BlockSpec((1, rows + STAT, 128), lambda p, i: (i, 0, p)),
        out_shape=jax.ShapeDtypeStruct((SIDE, rows + STAT, width), jnp.bfloat16),
        scratch_shapes=[
            pltpu.VMEM((2, keys_n, 128), jnp.bfloat16),
            pltpu.VMEM((2, keys_n, 128), jnp.bfloat16),
        ],
        compiler_params=pltpu.CompilerParams(vmem_limit_bytes=40 * 1024 * 1024),
        name="attend",
    )(queries, keys, values)


def merge_kernel(part_ref, residual_ref, sel_ref, out_ref):
    rows, width = residual_ref.shape
    heads = width // HEAD_DIM
    stats = part_ref[:, rows:, :].astype(jnp.float32)
    merged = stats[:, 0:4] + stats[:, 4:8] + stats[:, 8:12]
    per_head = []
    for p in range(heads // 2):
        cols = slice(p * 128, p * 128 + 128)
        for h in range(2):
            per_head.append(
                jnp.concatenate([merged[:, h, cols], merged[:, 2 + h, cols]], axis=1)
            )
    scaled = []
    for x in per_head:
        w = jnp.exp2(x - jnp.max(x, axis=0, keepdims=True))
        scaled.append(w / jnp.sum(w, axis=0, keepdims=True))
    weights = jnp.concatenate(scaled, axis=0)
    weights = jnp.concatenate(
        [weights, jnp.zeros((128 - weights.shape[0], rows), jnp.float32)], axis=0
    ).T
    lane = lax.broadcasted_iota(jnp.int32, (1, 128), 1)
    first = lane < HEAD_DIM
    streams = []
    for p in range(heads // 2):
        cols = slice(p * 128, p * 128 + 128)
        total = jnp.zeros((rows, 128), jnp.float32)
        for j in range(SIDE):
            a = (2 * p) * SIDE + j
            b = (2 * p + 1) * SIDE + j
            w = jnp.where(first, weights[:, a : a + 1], weights[:, b : b + 1])
            total = total + w * part_ref[j, :rows, cols].astype(jnp.float32)
        context = total.astype(jnp.bfloat16).astype(jnp.float32)
        streams.append(
            (residual_ref[:, cols].astype(jnp.float32) + context).astype(jnp.bfloat16)
        )
    streams.append(jnp.ones((rows, 128), jnp.bfloat16))
    stream = jnp.concatenate(streams, axis=1)
    out_ref[...] = jnp.dot(sel_ref[...], stream, preferred_element_type=jnp.float32).astype(
        jnp.bfloat16
    )


def merge(parts, residual, sel):
    rows, width = residual.shape
    return pl.pallas_call(
        merge_kernel,
        out_shape=jax.ShapeDtypeStruct((sel.shape[0], width + 128), jnp.bfloat16),
        compiler_params=pltpu.CompilerParams(vmem_limit_bytes=40 * 1024 * 1024),
        name="merge",
    )(parts, residual, sel)


def local(queries, keys, values, residual, reg_weight, targets, block_track, row_count, pool_slot):
    tok_rows, width = queries.shape
    here = tok_rows // BLK
    seq_count = lax.axis_size("seq")
    head_count = lax.axis_size("head")
    seq_index = lax.axis_index("seq")
    head_index = lax.axis_index("head")
    blocks = here * seq_count
    target_d = reg_weight.shape[1]
    chunk = target_d // seq_count
    quarter = target_d // head_count
    chunks_per_quarter = quarter // chunk

    target_part = lax.dynamic_slice_in_dim(targets, head_index * quarter, quarter, axis=2)
    every_target = lax.all_gather(target_part, "seq", axis=0, tiled=True)

    query_all = spread(queries, GROUP_Z).reshape(SIDE * tok_rows, width)
    pair = spread(jnp.stack([keys, values]), GROUP_YX)
    key_all = pair[:, 0].reshape(SIDE * tok_rows, width)
    value_all = pair[:, 1].reshape(SIDE * tok_rows, width)
    parts = attend(query_all, key_all, value_all)
    parts = lax.all_to_all(parts, "seq", 0, 0, axis_index_groups=GROUP_Z)

    valid = jnp.arange(BLK, dtype=jnp.int32)[None, :] < row_count[:, None]
    match = pool_slot[:, None, :] == jnp.arange(POOL, dtype=jnp.int32)[None, :, None]
    sel = match & valid[:, None, :]
    same_block = jnp.arange(here)[:, None] == jnp.arange(here)[None, :]
    selector = (
        jnp.where(sel[:, :, None, :] & same_block[:, None, :, None], 1.0, 0.0)
        .astype(jnp.bfloat16)
        .reshape(here * POOL, tok_rows)
    )
    pooled = merge(parts, residual, selector)

    every = spread(spread(pooled, GROUP_Z), GROUP_YX).reshape(blocks, POOL, width + 128)
    same = block_track[:, None] == block_track[None, :]
    same_track = jnp.where(same, 1.0, 0.0).astype(jnp.bfloat16)
    sums = jnp.einsum("ab,bpc->apc", same_track, every, preferred_element_type=jnp.float32)
    divisor = jnp.maximum(sums[:, :, width : width + 1], 1.0)
    mean = (sums[:, :, :width] / divisor).astype(jnp.bfloat16)
    earlier = jnp.arange(blocks)[None, :] < jnp.arange(blocks)[:, None]
    leader = ~jnp.any(same & earlier, axis=1)

    block_start = seq_index * here
    own_track = lax.dynamic_slice_in_dim(block_track, block_start, here)
    own_mean = lax.dynamic_slice_in_dim(mean, block_start, here, axis=0).reshape(here * POOL, width)
    own_divisor = lax.dynamic_slice_in_dim(divisor, block_start, here, axis=0).reshape(
        here * POOL, 1
    )
    own_target = jnp.concatenate(
        [lax.dynamic_slice_in_dim(every_target, own_track[b], 1, axis=0) for b in range(here)]
    ).reshape(here * POOL, quarter)
    weight_groups = reg_weight.reshape(width, head_count, quarter)
    own_part = jnp.einsum(
        "rc,cgn->grn", own_mean, weight_groups, preferred_element_type=jnp.float32
    )
    mine = jnp.arange(head_count)[:, None, None] == head_index
    own_part = own_part - jnp.where(mine, own_target[None].astype(jnp.float32), 0.0)
    own_part = own_part.astype(jnp.bfloat16).reshape(head_count * here * POOL, quarter)

    chunk_weight = lax.dynamic_slice_in_dim(reg_weight, seq_index * chunk, chunk, axis=1)
    mean_groups = mean.reshape(SIDE, blocks * POOL // SIDE, width)
    chunk_part = jnp.einsum(
        "cn,grc->gnr", chunk_weight, mean_groups, preferred_element_type=jnp.float32
    )
    chunk_home = seq_index // chunks_per_quarter == head_index
    chunk_target = lax.dynamic_slice_in_dim(
        every_target, lax.rem(seq_index, chunks_per_quarter) * chunk, chunk, axis=2
    )
    track_of = block_track[:, None] == jnp.arange(targets.shape[0] * seq_count)[None, :]
    chunk_target = jnp.einsum(
        "bt,tpn->bpn", jnp.where(track_of, 1.0, 0.0).astype(jnp.bfloat16), chunk_target
    ).reshape(SIDE, blocks * POOL // SIDE, chunk)
    chunk_part = chunk_part - jnp.where(
        chunk_home, chunk_target.transpose(0, 2, 1).astype(jnp.float32), 0.0
    )
    chunk_part = chunk_part.astype(jnp.bfloat16).reshape(SIDE * chunk, blocks * POOL // SIDE)

    both = jnp.concatenate([own_part, chunk_part], axis=0)
    both = lax.all_to_all(
        jnp.broadcast_to(both[None], (head_count, *both.shape)), "head", 0, 0
    )
    error = jnp.sum(both.astype(jnp.float32), axis=0).astype(jnp.bfloat16)
    own_error = error[: own_part.shape[0]].reshape(head_count, here * POOL, quarter)
    chunk_error = error[own_part.shape[0] :].reshape(chunk_part.shape).reshape(
        SIDE, chunk, blocks * POOL // SIDE
    )

    counted = jnp.where(leader[:, None, None], mean, jnp.zeros((), jnp.bfloat16)).reshape(
        SIDE, blocks * POOL // SIDE, width
    )
    grad_chunk = jnp.einsum(
        "gnr,grc->nc", chunk_error, counted, preferred_element_type=jnp.float32
    ).astype(jnp.bfloat16)
    grad_turned = spread(spread(grad_chunk, GROUP_Z), GROUP_YX).reshape(target_d, width)
    grad_reg = grad_turned.T

    mean_grad = jnp.einsum(
        "grn,cgn->rc", own_error, weight_groups, preferred_element_type=jnp.float32
    )
    track_grad = (mean_grad / own_divisor).astype(jnp.bfloat16)
    context_grad = lax.dot_general(
        selector, track_grad, (((0,), (0,)), ((), ())), preferred_element_type=jnp.float32
    ).astype(jnp.bfloat16)
    return (grad_reg, context_grad)


def solution(mesh):
    return jax.shard_map(
        local,
        mesh=mesh,
        in_specs=(
            P("seq", "head"),
            P("seq", "head"),
            P("seq", "head"),
            P("seq", "head"),
            P("head", None),
            P("seq", None, None),
            P(),
            P("seq"),
            P("seq", None),
        ),
        out_specs=(P("head", None), P("seq", "head")),
        check_vma=False,
    )
```

time: 1260 us -> 246 us (0.20); the launches traced: 1240 us -> 245 us
  blocking collectives: 680 us -> 46.2 us
  waiting for transfers between devices: 317 us -> 93.4 us
  matrix products: 102 us -> 2.94 us
  local copies, waits for them, and re-layouts: 105 us -> 15.5 us
  starting transfers between devices: 0.2 us -> 34.4 us
  Pallas kernels: 0 us -> 31.3 us
  other arithmetic: 15.8 us -> 3.08 us
    psum x1 -> x0, blocking collectives: 347 us -> none  [local(): grad_reg = lax.psum(reg_part, 'seq').astype(jnp.bfloat16)]
    unnamed x1 -> x0, blocking collectives: 333 us -> none
    all_gather x3 -> x1, waiting for transfers between devices: 250 us -> 9.68 us  [local(): every_target = lax.all_gather(target_part, 'seq', axis=0, tiled=True)]
    dot_general x72 -> x5, matrix products: 102 us -> 2.69 us  [the longest x1 1.17 us: local(): lax.dot_general(selector, track_grad, (((0,), (0,)), ((), ())), preferred...]
    all_to_all x0 -> x6, waiting for transfers between devices: none -> 83.6 us  [the longest x4 46.7 us: spread(): return lax.all_to_all(wide, 'seq', 0, 0, axis_index_groups=groups)]
    psum x1 -> x0, waiting for transfers between devices: 56.1 us -> none  [local(): lax.psum(partial_pred.astype(jnp.bfloat16), 'head').astype(jnp.float32)]
    another operation x2 -> x0, local copies, waits for them, and re-layouts: 49 us -> none  [the longest x1 24.5 us: local(): key_heads.reshape(block_count, 512, head_count, HEAD_DIM)]
    unnamed x14 -> x17, local copies, waits for them, and re-layouts: 50.6 us -> 2.26 us
  transfers between devices with their start and end apart: 5 -> 7, of which waited for: 4 -> 7; matrix products, arithmetic and copies ran while one was open for 4% -> 5% of each run, Pallas kernels for 0% -> 13%
where the time goes in v1:
time: 246 us; the launch traced here: 245 us
  waiting for transfers between devices  93.4 us (38%)
  blocking collectives  46.2 us (19%)
  starting transfers between devices  34.4 us (14%)
  Pallas kernels  31.3 us (13%)
  between operations  17.9 us (7%)
  local copies, waits for them, and re-layouts  15.5 us (6%)
  other arithmetic  3.08 us (1%)
  matrix products  2.94 us (1%)
    all_to_all x4, waiting for transfers between devices, spread(): return lax.all_to_all(wide, 'seq', 0, 0, axis_index_groups=groups)  46.7 us
    all_to_all x2, blocking collectives, spread(): return lax.all_to_all(wide, 'seq', 0, 0, axis_index_groups=groups)  46.2 us
    pallas_call x1, Pallas kernels, attend(): pl.pallas_call(attend_kernel, grid=(pairs, SIDE), in_specs=[pl.BlockSpec(...  29.7 us
    all_to_all x1, waiting for transfers between devices, local(): parts = lax.all_to_all(parts, 'seq', 0, 0, axis_index_groups=GROUP_Z)  28.8 us
    all_to_all x4, starting transfers between devices, spread(): return lax.all_to_all(wide, 'seq', 0, 0, axis_index_groups=groups)  27.2 us
    all_gather x1, waiting for transfers between devices, local(): every_target = lax.all_gather(target_part, 'seq', axis=0, tiled=True)  9.68 us
    all_to_all x1, waiting for transfers between devices, local(): lax.all_to_all(jnp.broadcast_to(both[None], (head_count, *both.shape)), '...  8.22 us
  transfers between devices with their start and end apart: 7, of which 7 were waited for; matrix products, arithmetic and copies ran while one was open for 5% of the time, Pallas kernels for 13%

profile of v1, /device:TPU:2, one launch (start us, length us, event | category | flops | bytes accessed | tf_op | source)
XLA Modules:
  0.0 244.7 jit_solution(3637330977925885660)
XLA Ops:
  7.2 1.0 pad_maximum_fusion
  8.4 35.0 %all_to_all.40 = bf16[8,2,256,256]{3,2,1,0:T(8,128)(2,1)} all-to-all(bf16[8,2,256,256]{3,2,1,0:T(8,128)(2,1)S(1)} %broadcast_in_dim.77), channel_id=1, replica_groups={{0,32,64,96,128,160,192,224},{4,36,68,100,132,164,196,228},{8,40,72,104..., dimensions={0} | all-to-all | bytes 4194304 | tf_op jit(solution)/shard_map/all_to_all | solution.py:21
  43.5 1.0 broadcast_in_dim.76
  44.5 8.5 %all-to-all-start = ((bf16[8,256,256]{2,1,0:T(8,128)(2,1)}), bf16[8,256,256]{2,1,0:T(8,128)(2,1)S(1)}, u32[]{:S(2)}, u32[]{:S(2)}) async-start(bf16[8,256,256]{2,1,0:T(8,128)(2,1)} %broadcast_in_dim.76), calls=%async_computation | async-start | bytes 2097152 | tf_op jit(solution)/shard_map/all_to_all | solution.py:21
  53.0 0.6 constant_dynamic-slice_fusion.4
  53.7 1.7 fusion.39
  55.4 25.3 %all-to-all-done = bf16[8,256,256]{2,1,0:T(8,128)(2,1)S(1)} async-done(((bf16[8,256,256]{2,1,0:T(8,128)(2,1)}), bf16[8,256,256]{2,1,0:T(8,128)(2,1)S(1)}, u32[]{:S(2)}, u32[]{:S(2)}) %all-to-all-start) | async-done | bytes 1048608 | tf_op jit(solution)/shard_map/all_to_all | solution.py:21
  80.7 29.7 %attend.1 = bf16[8,272,256]{2,1,0:T(8,128)(2,1)} custom-call(bf16[2048,256]{1,0:T(8,128)(2,1)S(1)} %bitcast.75, bf16[2048,256]{1,0:T(8,128)(2,1)S(1)} %bitcast.77, bf16[2048,256]{1,0:T(8,128)(2,1)S(1)} %bitcast.76), custom_call_target="tpu_custom_call" | custom-call | tf_op jit(solution)/shard_map/attend/pallas_call | solution.py:74
  110.4 3.7 %all-to-all-start.2 = ((bf16[8,272,256]{2,1,0:T(8,128)(2,1)}), bf16[8,272,256]{2,1,0:T(8,128)(2,1)S(1)}, u32[]{:S(2)}, u32[]{:S(2)}) async-start(bf16[8,272,256]{2,1,0:T(8,128)(2,1)} %attend.1), calls=%async_computation.2 | async-start | bytes 2228224 | tf_op jit(solution)/shard_map/all_to_all | solution.py:166
  114.4 28.8 %all-to-all-done.2.part_ref = bf16[8,272,256]{2,1,0:T(8,128)(2,1)S(1)} async-done(((bf16[8,272,256]{2,1,0:T(8,128)(2,1)}), bf16[8,272,256]{2,1,0:T(8,128)(2,1)S(1)}, u32[]{:S(2)}, u32[]{:S(2)}) %all-to-all-start.2) | async-done | bytes 1114144 | tf_op jit(solution)/shard_map/all_to_all | solution.py:166
  143.1 1.5 merge.1
  144.7 0.7 broadcast_in_dim.80
  145.4 4.4 %all-to-all-start.3 = ((bf16[8,32,384]{2,1,0:T(8,128)(2,1)}), bf16[8,32,384]{2,1,0:T(8,128)(2,1)S(1)}, u32[]{:S(2)}, u32[]{:S(2)}) async-start(bf16[8,32,384]{2,1,0:T(8,128)(2,1)} %broadcast_in_dim.80), calls=%async_computation.3 | async-start | bytes 393216 | tf_op jit(solution)/shard_map/all_to_all | solution.py:21
  149.8 11.7 %all-to-all-done.3 = bf16[8,32,384]{2,1,0:T(8,128)(2,1)S(1)} async-done(((bf16[8,32,384]{2,1,0:T(8,128)(2,1)}), bf16[8,32,384]{2,1,0:T(8,128)(2,1)S(1)}, u32[]{:S(2)}, u32[]{:S(2)}) %all-to-all-start.3) | async-done | bytes 196640 | tf_op jit(solution)/shard_map/all_to_all | solution.py:21
  161.5 1.3 broadcast_in_dim.126
  162.8 5.2 %all-to-all-start.4 = ((bf16[8,8,32,384]{3,2,1,0:T(8,128)(2,1)}), bf16[8,8,32,384]{3,2,1,0:T(8,128)(2,1)S(1)}, u32[]{:S(2)}, u32[]{:S(2)}) async-start(bf16[8,8,32,384]{3,2,1,0:T(8,128)(2,1)} %broadcast_in_dim.126), calls=%async_computation.4 | async-start | bytes 3145728 | tf_op jit(solution)/shard_map/all_to_all | solution.py:21
  172.4 9.7 %all-gather.2.cloned.1.call-done = bf16[256,16,256]{2,1,0:T(8,128)(2,1)} async-done(((bf16[4,16,256]{2,1,0:T(8,128)(2,1)}), bf16[256,16,256]{2,1,0:T(8,128)(2,1)}) %all-gather.2.cloned.1.call-update) | async-done | bytes 2097168 | tf_op jit(solution)/shard_map/all_gather | solution.py:159
  182.1 1.6 constant_dynamic-slice_fusion.1
  183.7 0.8 copy.53
  185.6 0.7 constant_dynamic-slice_fusion.3
  186.3 2.8 %all-to-all-done.4 = bf16[8,8,32,384]{3,2,1,0:T(8,128)(2,1)S(1)} async-done(((bf16[8,8,32,384]{3,2,1,0:T(8,128)(2,1)}), bf16[8,8,32,384]{3,2,1,0:T(8,128)(2,1)S(1)}, u32[]{:S(2)}, u32[]{:S(2)}) %all-to-all-start.4) | async-done | bytes 1572896 | tf_op jit(solution)/shard_map/all_to_all | solution.py:21
  189.7 1.2 slice_maximum_fusion
  193.0 0.8 broadcast_in_dim.133
  193.9 3.5 %all-to-all-start.5 = ((bf16[4,256,256]{2,1,0:T(8,128)(2,1)}), bf16[4,256,256]{2,1,0:T(8,128)(2,1)S(1)}, u32[]{:S(2)}, u32[]{:S(2)}) async-start(bf16[4,256,256]{2,1,0:T(8,128)(2,1)} %broadcast_in_dim.133), calls=%async_computation.5 | async-start | bytes 1048576 | tf_op jit(solution)/shard_map/all_to_all | solution.py:224
  197.9 8.2 %all-to-all-done.5 = bf16[4,256,256]{2,1,0:T(8,128)(2,1)S(1)} async-done(((bf16[4,256,256]{2,1,0:T(8,128)(2,1)}), bf16[4,256,256]{2,1,0:T(8,128)(2,1)S(1)}, u32[]{:S(2)}, u32[]{:S(2)}) %all-to-all-start.5) | async-done | bytes 524320 | tf_op jit(solution)/shard_map/all_to_all | solution.py:224
  206.5 11.1 %all_to_all.41 = bf16[8,16,256]{2,1,0:T(8,128)(2,1)S(1)} all-to-all(bf16[8,16,256]{2,1,0:T(8,128)(2,1)S(1)} %broadcast_in_dim.136), channel_id=1, replica_groups={{0,4,8,12,16,20,24,28},{32,36,40,44,48,52,56,60},{64,68,72,76,80,84,88,..., dimensions={0} | all-to-all | bytes 131072 | tf_op jit(solution)/shard_map/all_to_all | solution.py:21
  217.7 0.8 broadcast_in_dim.137
  218.5 9.2 %all-to-all-start.7 = ((bf16[8,8,16,256]{3,2,1,0:T(8,128)(2,1)}), bf16[8,8,16,256]{3,2,1,0:T(8,128)(2,1)S(1)}, u32[]{:S(2)}, u32[]{:S(2)}) async-start(bf16[8,8,16,256]{3,2,1,0:T(8,128)(2,1)} %broadcast_in_dim.137), calls=%async_computation.7 | async-start | bytes 1048576 | tf_op jit(solution)/shard_map/all_to_all | solution.py:21
  227.7 0.8 constant_dynamic-slice_fusion
  228.8 1.2 convolution_convert_fusion
  229.9 6.9 %all-to-all-done.7 = bf16[8,8,16,256]{3,2,1,0:T(8,128)(2,1)S(1)} async-done(((bf16[8,8,16,256]{3,2,1,0:T(8,128)(2,1)}), bf16[8,8,16,256]{3,2,1,0:T(8,128)(2,1)S(1)}, u32[]{:S(2)}, u32[]{:S(2)}) %all-to-all-start.7) | async-done | bytes 524320 | tf_op jit(solution)/shard_map/all_to_all | solution.py:21
  236.8 1.0 copy.51
  (48 shorter events, 6.2 us)
Async XLA Ops:
  7.2 45.9 %copy-start = (bf16[4,16,1024]{2,1,0:T(8,128)(2,1)S(1)}, bf16[4,16,1024]{2,1,0:T(8,128)(2,1)}, u32[]{:S(2)}) copy-start(bf16[4,16,1024]{2,1,0:T(8,128)(2,1)} %param.14) | copy-start | bytes 393220
  8.4 35.0 %copy-start.2 = (bf16[256,256]{1,0:T(8,128)(2,1)S(1)}, bf16[256,256]{1,0:T(8,128)(2,1)}, u32[]{:S(2)}) copy-start(bf16[256,256]{1,0:T(8,128)(2,1)} %param.9) | copy-start | bytes 393220
  44.5 36.2 %all-to-all-start = ((bf16[8,256,256]{2,1,0:T(8,128)(2,1)}), bf16[8,256,256]{2,1,0:T(8,128)(2,1)S(1)}, u32[]{:S(2)}, u32[]{:S(2)}) async-start(bf16[8,256,256]{2,1,0:T(8,128)(2,1)} %broadcast_in_dim.76), calls=%async_computation | async-start | bytes 2097152 | tf_op jit(solution)/shard_map/all_to_all | solution.py:21
  53.0 129.1 %all-gather.2.cloned.1.call-start = ((), (), s32[]{:S(2)}) async-start(), calls=%async_computation.8 | async-start | bytes 2129920 | tf_op jit(solution)/shard_map/all_gather | solution.py:159
  110.4 3.7 %copy-start.6 = (s32[2]{0:T(128)S(1)}, s32[2]{0:T(128)}, u32[]{:S(2)}) copy-start(s32[2]{0:T(128)} %param.16) | copy-start | bytes 28
  110.4 3.8 %copy-start.5 = (s32[2,128]{1,0:T(2,128)S(1)}, s32[2,128]{1,0:T(2,128)}, u32[]{:S(2)}) copy-start(s32[2,128]{1,0:T(2,128)} %param.17) | copy-start | bytes 3076
  110.4 32.7 %copy-start.1 = (bf16[256,256]{1,0:T(8,128)(2,1)S(1)}, bf16[256,256]{1,0:T(8,128)(2,1)}, u32[]{:S(2)}) copy-start(bf16[256,256]{1,0:T(8,128)(2,1)} %residual_ref.1) | copy-start | bytes 393220
  110.4 39.3 %copy-start.4 = (s32[128]{0:T(128)S(1)}, s32[128]{0:T(128)}, u32[]{:S(2)}) copy-start(s32[128]{0:T(128)} %param.15) | copy-start | bytes 1540
  110.4 32.7 %all-to-all-start.2 = ((bf16[8,272,256]{2,1,0:T(8,128)(2,1)}), bf16[8,272,256]{2,1,0:T(8,128)(2,1)S(1)}, u32[]{:S(2)}, u32[]{:S(2)}) async-start(bf16[8,272,256]{2,1,0:T(8,128)(2,1)} %attend.1), calls=%async_computation.2 | async-start | bytes 2228224 | tf_op jit(solution)/shard_map/all_to_all | solution.py:166
  145.4 16.1 %all-to-all-start.3 = ((bf16[8,32,384]{2,1,0:T(8,128)(2,1)}), bf16[8,32,384]{2,1,0:T(8,128)(2,1)S(1)}, u32[]{:S(2)}, u32[]{:S(2)}) async-start(bf16[8,32,384]{2,1,0:T(8,128)(2,1)} %broadcast_in_dim.80), calls=%async_computation.3 | async-start | bytes 393216 | tf_op jit(solution)/shard_map/all_to_all | solution.py:21
  162.8 26.3 %all-to-all-start.4 = ((bf16[8,8,32,384]{3,2,1,0:T(8,128)(2,1)}), bf16[8,8,32,384]{3,2,1,0:T(8,128)(2,1)S(1)}, u32[]{:S(2)}, u32[]{:S(2)}) async-start(bf16[8,8,32,384]{3,2,1,0:T(8,128)(2,1)} %broadcast_in_dim.126), calls=%async_computation.4 | async-start | bytes 3145728 | tf_op jit(solution)/shard_map/all_to_all | solution.py:21
  191.3 1.0 copy-start.3
  193.9 12.3 %all-to-all-start.5 = ((bf16[4,256,256]{2,1,0:T(8,128)(2,1)}), bf16[4,256,256]{2,1,0:T(8,128)(2,1)S(1)}, u32[]{:S(2)}, u32[]{:S(2)}) async-start(bf16[4,256,256]{2,1,0:T(8,128)(2,1)} %broadcast_in_dim.133), calls=%async_computation.5 | async-start | bytes 1048576 | tf_op jit(solution)/shard_map/all_to_all | solution.py:224
  218.5 18.3 %all-to-all-start.7 = ((bf16[8,8,16,256]{3,2,1,0:T(8,128)(2,1)}), bf16[8,8,16,256]{3,2,1,0:T(8,128)(2,1)S(1)}, u32[]{:S(2)}, u32[]{:S(2)}) async-start(bf16[8,8,16,256]{3,2,1,0:T(8,128)(2,1)} %broadcast_in_dim.137), calls=%async_computation.7 | async-start | bytes 1048576 | tf_op jit(solution)/shard_map/all_to_all | solution.py:21
Sparse Core Ops, SparseCore 0:
  58.1 123.9 all-gather.1

commit v2 on v1

v2 whole, which is shorter than its diff:
```python
import jax
import jax.numpy as jnp
from jax import lax
from jax.experimental import pallas as pl
from jax.experimental.pallas import tpu as pltpu
from jax.sharding import PartitionSpec as P

HEAD_DIM = 64
BLK = 128
POOL = 16
SIDE = 8
LOG2E = 1.4426950408889634
STAT = 16

GROUP_Z = [[g * SIDE + i for i in range(SIDE)] for g in range(SIDE)]
GROUP_YX = [[g * SIDE + i for g in range(SIDE)] for i in range(SIDE)]


def spread(x, groups):
    wide = jnp.broadcast_to(x[None], (SIDE, *x.shape))
    return lax.all_to_all(wide, "seq", 0, 0, axis_index_groups=groups)


def shift(seq_count, dg):
    dy, dx = dg // 4, dg % 4
    pairs = []
    for g in range(seq_count // SIDE):
        to = (g // 4 + dy) % 2 * 4 + (g % 4 + dx) % 4
        pairs += [(g * SIDE + i, to * SIDE + i) for i in range(SIDE)]
    return pairs


def attend_kernel(q_ref, *refs):
    kv_refs, (o_ref, k_own, v_own) = refs[:-3], refs[-3:]
    rows = q_ref.shape[0]
    lane = lax.broadcasted_iota(jnp.int32, (1, 128), 1)
    first = lane < HEAD_DIM

    @pl.when(pl.program_id(0) == 0)
    def _():
        zero = jnp.zeros((), jnp.bfloat16)
        one = jnp.ones((), jnp.bfloat16)
        for i, kv_ref in enumerate(kv_refs):
            n = kv_ref.shape[0] // 2
            span = pl.ds(i * n, n)
            k = kv_ref[:n]
            v = kv_ref[n:]
            k_own[0, span] = jnp.where(first, k, zero)
            k_own[1, span] = jnp.where(first, zero, k)
            v_own[0, span] = jnp.where(first, v, one)
            v_own[1, span] = jnp.where(first, one, v)

    scale = LOG2E * HEAD_DIM ** (-0.5)
    q = q_ref[...]
    tops, sums = [], []
    for h in range(2):
        s = lax.dot_general(
            q, k_own[h], (((1,), (1,)), ((), ())), preferred_element_type=jnp.float32
        )
        top = jnp.max(s, axis=1, keepdims=True)
        p = jnp.exp2((s - top) * scale).astype(jnp.bfloat16)
        sums.append(jnp.dot(p, v_own[h], preferred_element_type=jnp.float32))
        tops.append(top * scale)
    num = jnp.where(first, sums[0], sums[1])
    den_other = jnp.where(first, sums[1], sums[0])
    den = pltpu.roll(den_other, HEAD_DIM, 1)
    o_ref[0, :rows] = (num / den).astype(jnp.bfloat16)
    lse = jnp.where(first, tops[1], tops[0]) + jnp.log2(den_other)
    turned = lse.T
    left = jnp.concatenate([turned[HEAD_DIM : HEAD_DIM + 1], turned[0:1]], axis=0)
    left = jnp.concatenate([left[:, :128], left[:, 128:]], axis=0)
    hi = left.astype(jnp.bfloat16)
    rest = left - hi.astype(jnp.float32)
    mid = rest.astype(jnp.bfloat16)
    rest = rest - mid.astype(jnp.float32)
    pad = jnp.zeros_like(left)
    o_ref[0, rows:] = jnp.concatenate(
        [hi.astype(jnp.float32), mid.astype(jnp.float32), rest, pad], axis=0
    ).astype(jnp.bfloat16)


def attend(queries, pieces, pair):
    n = queries.shape[0]
    rows = n // SIDE
    keys_n = sum(x.shape[0] for x in pieces) // 2
    return pl.pallas_call(
        attend_kernel,
        grid=(SIDE,),
        in_specs=[pl.BlockSpec((rows, 128), lambda i: (i, pair))]
        + [pl.BlockSpec((x.shape[0], 128), lambda i: (0, pair)) for x in pieces],
        out_specs=pl.BlockSpec((1, rows + STAT, 128), lambda i: (i, 0, 0)),
        out_shape=jax.ShapeDtypeStruct((SIDE, rows + STAT, 128), jnp.bfloat16),
        scratch_shapes=[
            pltpu.VMEM((2, keys_n, 128), jnp.bfloat16),
            pltpu.VMEM((2, keys_n, 128), jnp.bfloat16),
        ],
        compiler_params=pltpu.CompilerParams(vmem_limit_bytes=40 * 1024 * 1024),
        cost_estimate=pl.CostEstimate(
            flops=2 * 2 * 2 * n * keys_n * 256,
            bytes_accessed=8 * n * 128,
            transcendentals=2 * n * keys_n,
        ),
        name="attend",
    )(queries, *pieces)


def merge_kernel(*refs):
    part_refs, (residual_ref, sel_ref, out_ref) = refs[:-3], refs[-3:]
    rows = residual_ref.shape[0]
    lane = lax.broadcasted_iota(jnp.int32, (1, 128), 1)
    first = lane < HEAD_DIM
    scaled = []
    for part_ref in part_refs:
        stats = part_ref[:, rows:, :].astype(jnp.float32)
        merged = stats[:, 0:4] + stats[:, 4:8] + stats[:, 8:12]
        for h in range(2):
            x = jnp.concatenate([merged[:, h], merged[:, 2 + h]], axis=1)
            w = jnp.exp2(x - jnp.max(x, axis=0, keepdims=True))
            scaled.append(w / jnp.sum(w, axis=0, keepdims=True))
    weights = jnp.concatenate(scaled, axis=0)
    weights = jnp.concatenate(
        [weights, jnp.zeros((128 - weights.shape[0], rows), jnp.float32)], axis=0
    ).T
    streams = []
    for p, part_ref in enumerate(part_refs):
        cols = slice(p * 128, p * 128 + 128)
        total = jnp.zeros((rows, 128), jnp.float32)
        for j in range(SIDE):
            a = (2 * p) * SIDE + j
            b = (2 * p + 1) * SIDE + j
            w = jnp.where(first, weights[:, a : a + 1], weights[:, b : b + 1])
            total = total + w * part_ref[j, :rows].astype(jnp.float32)
        context = total.astype(jnp.bfloat16).astype(jnp.float32)
        streams.append(
            (residual_ref[:, cols].astype(jnp.float32) + context).astype(jnp.bfloat16)
        )
    stream = jnp.concatenate(streams, axis=1)
    out_ref[...] = jnp.dot(sel_ref[...], stream, preferred_element_type=jnp.float32).astype(
        jnp.bfloat16
    )


def merge(parts, residual, sel):
    return pl.pallas_call(
        merge_kernel,
        out_shape=jax.ShapeDtypeStruct((sel.shape[0], residual.shape[1]), jnp.bfloat16),
        compiler_params=pltpu.CompilerParams(vmem_limit_bytes=40 * 1024 * 1024),
        name="merge",
    )(*parts, residual, sel)


def track_kernel(id_col_ref, id_row_ref, every_ref, divisor_ref, weight_ref, mean_ref, part_ref):
    match = jnp.where(id_col_ref[...] == id_row_ref[...], 1.0, 0.0).astype(jnp.bfloat16)
    sums = jnp.dot(match, every_ref[...], preferred_element_type=jnp.float32)
    mean = (sums / divisor_ref[...]).astype(jnp.bfloat16)
    mean_ref[...] = mean
    part = lax.dot_general(
        weight_ref[...], mean, (((1,), (1,)), ((), ())), preferred_element_type=jnp.float32
    ).astype(jnp.bfloat16)
    for h in range(part_ref.shape[0]):
        part_ref[h] = part


def track_means(ids, every, divisor, weight, head_count):
    rows, width = every.shape
    chunk = weight.shape[0]
    step = rows // SIDE
    return pl.pallas_call(
        track_kernel,
        grid=(SIDE,),
        in_specs=[
            pl.BlockSpec((step, 1), lambda i: (i, 0)),
            pl.BlockSpec((1, rows), lambda i: (0, 0)),
            pl.BlockSpec((rows, width), lambda i: (0, 0)),
            pl.BlockSpec((step, 1), lambda i: (i, 0)),
            pl.BlockSpec((chunk, width), lambda i: (0, 0)),
        ],
        out_specs=[
            pl.BlockSpec((step, width), lambda i: (i, 0)),
            pl.BlockSpec((head_count, chunk, step), lambda i: (0, 0, i)),
        ],
        out_shape=[
            jax.ShapeDtypeStruct((rows, width), jnp.bfloat16),
            jax.ShapeDtypeStruct((head_count, chunk, rows), jnp.bfloat16),
        ],
        compiler_params=pltpu.CompilerParams(vmem_limit_bytes=40 * 1024 * 1024),
        name="track_means",
    )(ids.reshape(rows, 1), ids.reshape(1, rows), every, divisor, weight)


def error_kernel(part_ref, target_ref, leader_ref, mean_ref, out_ref):
    back = part_ref.shape[2] // out_ref.shape[0]
    width = mean_ref.shape[1]
    total = part_ref[0].astype(jnp.float32)
    for h in range(1, part_ref.shape[0]):
        total = total + part_ref[h].astype(jnp.float32)
    error = (total - target_ref[...]).astype(jnp.bfloat16).astype(jnp.float32)
    grad = jnp.dot(
        (error * leader_ref[...]).astype(jnp.bfloat16),
        mean_ref[...],
        preferred_element_type=jnp.float32,
    ).astype(jnp.bfloat16)
    per = 128 // back
    for s in range(out_ref.shape[0]):
        tile = error[:, s // per * 128 : s // per * 128 + 128]
        turn = s % per * back
        rows = pltpu.roll(tile, 128 - turn, 1) if turn else tile
        out_ref[s, :, :width] = grad
        out_ref[s, :, width:] = rows.astype(jnp.bfloat16)


def error_messages(partial, target, leader, mean, seq_count):
    chunk = partial.shape[1]
    return pl.pallas_call(
        error_kernel,
        out_shape=jax.ShapeDtypeStruct((seq_count, chunk, mean.shape[1] + 128), jnp.bfloat16),
        compiler_params=pltpu.CompilerParams(vmem_limit_bytes=40 * 1024 * 1024),
        name="error_messages",
    )(partial, target, leader, mean)


def local(queries, keys, values, residual, reg_weight, targets, block_track, row_count, pool_slot):
    tok_rows, width = queries.shape
    here = tok_rows // BLK
    seq_count = lax.axis_size("seq")
    head_count = lax.axis_size("head")
    seq_index = lax.axis_index("seq")
    blocks = here * seq_count
    target_d = reg_weight.shape[1]
    chunk = target_d // seq_count
    owned = targets.shape[0]
    tracks = owned * seq_count

    own_kv = jnp.concatenate([keys, values], axis=0)
    pieces = [own_kv] + [
        lax.ppermute(own_kv, "seq", shift(seq_count, d)) for d in (6, 5, 7, 2, 4, 1, 3)
    ]
    query_all = spread(queries, GROUP_Z).reshape(SIDE * tok_rows, width)

    valid = jnp.arange(BLK, dtype=jnp.int32)[None, :] < row_count[:, None]
    match = pool_slot[:, None, :] == jnp.arange(POOL, dtype=jnp.int32)[None, :, None]
    sel = match & valid[:, None, :]
    same_block = jnp.arange(here)[:, None] == jnp.arange(here)[None, :]
    selector = (
        jnp.where(sel[:, :, None, :] & same_block[:, None, :, None], 1.0, 0.0)
        .astype(jnp.bfloat16)
        .reshape(here * POOL, tok_rows)
    )
    slot_rows = jnp.sum(jnp.where(sel, 1.0, 0.0), axis=2).astype(jnp.bfloat16)
    turned = targets.reshape(owned * POOL, target_d).T.reshape(seq_count, chunk, owned * POOL)
    extra = jnp.concatenate(
        [slot_rows.T, jnp.zeros((POOL, 128 - owned * POOL - here), jnp.bfloat16)], axis=1
    )
    early = jnp.concatenate(
        [turned, jnp.broadcast_to(extra[None], (seq_count, *extra.shape))], axis=2
    )
    early, query_all = lax.optimization_barrier((early, query_all))
    early = lax.all_to_all(early, "seq", 0, 0)

    parts = []
    for pair in range(width // 128):
        part = attend(query_all, pieces, pair)
        if pair == 0:
            early, part = lax.optimization_barrier((early, part))
        parts.append(lax.all_to_all(part, "seq", 0, 0, axis_index_groups=GROUP_Z))

    same = block_track[:, None] == block_track[None, :]
    same_track = jnp.where(same, 1.0, 0.0).astype(jnp.bfloat16)
    earlier = jnp.arange(blocks)[None, :] < jnp.arange(blocks)[:, None]
    leader = jnp.where(jnp.any(same & earlier, axis=1), 0.0, 1.0)
    leader = jnp.repeat(leader, POOL).reshape(1, blocks * POOL)
    ids = (
        block_track[:, None] * POOL + jnp.arange(POOL, dtype=jnp.int32)[None, :]
    ).reshape(blocks * POOL)
    every_count = (
        early[:, :, owned * POOL : owned * POOL + here].transpose(0, 2, 1).reshape(blocks, POOL)
    )
    counts = jnp.dot(same_track, every_count, preferred_element_type=jnp.float32)
    divisor = jnp.maximum(counts, 1.0)
    track_of = block_track[:, None] == jnp.arange(tracks, dtype=jnp.int32)[None, :]
    track_of = jnp.where(track_of, 1.0, 0.0).astype(jnp.bfloat16)
    chunk_target = (
        early[:, :, : owned * POOL]
        .reshape(seq_count, chunk, owned, POOL)
        .transpose(1, 0, 2, 3)
        .reshape(chunk, tracks, POOL)
    )
    chunk_target = jnp.einsum(
        "bt,ntp->nbp", track_of, chunk_target, preferred_element_type=jnp.float32
    ).reshape(chunk, blocks * POOL)
    rows_divisor = divisor.reshape(blocks * POOL, 1)
    chunk_weight = lax.dynamic_slice_in_dim(reg_weight, seq_index * chunk, chunk, axis=1).T
    own_divisor = lax.dynamic_slice_in_dim(divisor, seq_index * here, here, axis=0).reshape(
        here * POOL, 1
    )

    pooled = merge(parts, residual, selector)
    chunk_target, rows_divisor, leader, ids, chunk_weight, own_divisor, pooled = (
        lax.optimization_barrier(
            (chunk_target, rows_divisor, leader, ids, chunk_weight, own_divisor, pooled)
        )
    )
    every = spread(spread(pooled, GROUP_Z), GROUP_YX).reshape(blocks * POOL, width)
    mean, partial = track_means(ids, every, rows_divisor, chunk_weight, head_count)
    partial = lax.all_to_all(partial, "head", 0, 0)
    back = here * POOL
    final = error_messages(partial, chunk_target, leader, mean, seq_count)
    final = lax.all_to_all(final, "seq", 0, 0).reshape(target_d, width + 128)
    grad_reg = final[:, :width].T
    mean_grad = lax.dot_general(
        final[:, width : width + back],
        reg_weight,
        (((0,), (1,)), ((), ())),
        preferred_element_type=jnp.float32,
    )
    track_grad = (mean_grad / own_divisor).astype(jnp.bfloat16)
    context_grad = lax.dot_general(
        selector, track_grad, (((0,), (0,)), ((), ())), preferred_element_type=jnp.float32
    ).astype(jnp.bfloat16)
    return (grad_reg, context_grad)


def solution(mesh):
    return jax.shard_map(
        local,
        mesh=mesh,
        in_specs=(
            P("seq", "head"),
            P("seq", "head"),
            P("seq", "head"),
            P("seq", "head"),
            P("head", None),
            P("seq", None, None),
            P(),
            P("seq"),
            P("seq", None),
        ),
        out_specs=(P("head", None), P("seq", "head")),
        check_vma=False,
    )
```

time: 246 us -> 196 us (0.80)
  waiting for transfers between devices: 93.4 us -> 24.2 us
  starting transfers between devices: 34.4 us -> 56.4 us
  between operations: 17.9 us -> 0.92 us
  Pallas kernels: 31.3 us -> 38.8 us
  local copies, waits for them, and re-layouts: 15.5 us -> 20.6 us
    all_to_all x0 -> x2, blocking collectives: none -> 36.2 us  [the longest x1 27.8 us: local(): final = lax.all_to_all(final, 'seq', 0, 0).reshape(target_d, width + 128)]
    all_to_all x2 -> x1, blocking collectives: 46.2 us -> 11.5 us  [spread(): return lax.all_to_all(wide, 'seq', 0, 0, axis_index_groups=groups)]
    all_to_all x2 -> x3, waiting for transfers between devices: 37 us -> 5.86 us  [the longest x2 5.86 us: local(): parts.append(lax.all_to_all(part, 'seq', 0, 0, axis_index_groups=GROUP_Z))]
    all_to_all x4 -> x2, waiting for transfers between devices: 46.7 us -> 18.3 us  [spread(): return lax.all_to_all(wide, 'seq', 0, 0, axis_index_groups=groups)]
    ppermute x0 -> x7, starting transfers between devices: none -> 18.3 us  [local(): lax.ppermute(own_kv, 'seq', shift(seq_count, d))]
    all_to_all x2 -> x3, starting transfers between devices: 7.18 us -> 22.1 us  [the longest x2 13.9 us: local(): parts.append(lax.all_to_all(part, 'seq', 0, 0, axis_index_groups=GROUP_Z))]
    all_to_all x4 -> x2, starting transfers between devices: 27.2 us -> 16 us  [spread(): return lax.all_to_all(wide, 'seq', 0, 0, axis_index_groups=groups)]
    all_gather x1 -> x0, waiting for transfers between devices: 9.68 us -> none  [local(): every_target = lax.all_gather(target_part, 'seq', axis=0, tiled=True)]
  transfers between devices with their start and end apart: 7 -> 12, of which waited for: 7 -> 3; matrix products, arithmetic and copies ran while one was open for 5% -> 8% of each run, Pallas kernels for 13% -> 17%
where the time goes in v2:
time: 196 us; the launch traced here: 193 us
  starting transfers between devices  56.4 us (29%)
  blocking collectives  47.7 us (24%)
  Pallas kernels  38.8 us (20%)
  waiting for transfers between devices  24.2 us (12%)
  local copies, waits for them, and re-layouts  20.6 us (11%)
  matrix products  3.04 us (2%)
    pallas_call x2, Pallas kernels, attend(): pl.pallas_call(attend_kernel, grid=(SIDE,), in_specs=[pl.BlockSpec((rows,...  32.1 us
    all_to_all x1, blocking collectives, local(): final = lax.all_to_all(final, 'seq', 0, 0).reshape(target_d, width + 128)  27.8 us
    all_to_all x2, waiting for transfers between devices, spread(): return lax.all_to_all(wide, 'seq', 0, 0, axis_index_groups=groups)  18.3 us
    ppermute x7, starting transfers between devices, local(): lax.ppermute(own_kv, 'seq', shift(seq_count, d))  18.3 us
    all_to_all x2, starting transfers between devices, spread(): return lax.all_to_all(wide, 'seq', 0, 0, axis_index_groups=groups)  16 us
    all_to_all x2, starting transfers between devices, local(): parts.append(lax.all_to_all(part, 'seq', 0, 0, axis_index_groups=GROUP_Z))  13.9 us
    all_to_all x1, blocking collectives, spread(): return lax.all_to_all(wide, 'seq', 0, 0, axis_index_groups=groups)  11.5 us
    all_to_all x1, blocking collectives, local(): partial = lax.all_to_all(partial, 'head', 0, 0)  8.42 us
  transfers between devices with their start and end apart: 12, of which 3 were waited for; matrix products, arithmetic and copies ran while one was open for 8% of the time, Pallas kernels for 17%

profile of v2, /device:TPU:2, one launch (start us, length us, event | category | flops | bytes accessed | tf_op | source)
XLA Modules:
  0.0 193.0 jit_solution(3332375509952704702)
XLA Ops:
  0.6 2.0 %broadcast_in_dim.53 = bf16[8,256,256]{2,1,0:T(8,128)(2,1)} broadcast(bf16[256,256]{1,0:T(8,128)(2,1)} %param.9), dimensions={1,2} | broadcast | bytes 1179648 | tf_op jit(solution)/shard_map/broadcast_in_dim | solution.py:20
  2.7 8.6 %all-to-all-start = ((bf16[8,256,256]{2,1,0:T(8,128)(2,1)}), bf16[8,256,256]{2,1,0:T(8,128)(2,1)S(1)}, u32[]{:S(2)}, u32[]{:S(2)}) async-start(bf16[8,256,256]{2,1,0:T(8,128)(2,1)} %broadcast_in_dim.53), calls=%async_computation | async-start | bytes 2097152 | tf_op jit(solution)/shard_map/all_to_all | solution.py:21
  12.8 1.5 collective-permute-start.5
  14.3 3.2 %collective-permute-start.4 = (bf16[512,256]{1,0:T(8,128)(2,1)S(1)}, bf16[512,256]{1,0:T(8,128)(2,1)S(1)}, u32[]{:S(2)}, u32[]{:S(2)}) collective-permute-start(bf16[512,256]{1,0:T(8,128)(2,1)S(1)} %constant_dynamic-update-slice_fusion.refs_0_), channel_id=1, source_target_pairs={{0,128},{4,132},{8,136},{12,140},{16,144},{20,148},{24,152},{28,15... | collective-permute-start | bytes 786440 | tf_op jit(solution)/shard_map/ppermute | solution.py:236
  17.5 3.3 %collective-permute-start.3 = (bf16[512,256]{1,0:T(8,128)(2,1)S(1)}, bf16[512,256]{1,0:T(8,128)(2,1)S(1)}, u32[]{:S(2)}, u32[]{:S(2)}) collective-permute-start(bf16[512,256]{1,0:T(8,128)(2,1)S(1)} %constant_dynamic-update-slice_fusion.refs_0_), channel_id=1, source_target_pairs={{0,64},{4,68},{8,72},{12,76},{16,80},{20,84},{24,88},{28,92},{32,9... | collective-permute-start | bytes 786440 | tf_op jit(solution)/shard_map/ppermute | solution.py:236
  21.1 1.1 copy.53
  23.3 4.5 %collective-permute-start.1 = (bf16[512,256]{1,0:T(8,128)(2,1)S(1)}, bf16[512,256]{1,0:T(8,128)(2,1)S(1)}, u32[]{:S(2)}, u32[]{:S(2)}) collective-permute-start(bf16[512,256]{1,0:T(8,128)(2,1)S(1)} %constant_dynamic-update-slice_fusion.refs_0_), channel_id=1, source_target_pairs={{0,160},{4,164},{8,168},{12,172},{16,176},{20,180},{24,184},{28,18... | collective-permute-start | bytes 786440 | tf_op jit(solution)/shard_map/ppermute | solution.py:236
  27.8 5.1 %collective-permute-start = (bf16[512,256]{1,0:T(8,128)(2,1)S(1)}, bf16[512,256]{1,0:T(8,128)(2,1)}, u32[]{:S(2)}, u32[]{:S(2)}) collective-permute-start(bf16[512,256]{1,0:T(8,128)(2,1)S(1)} %constant_dynamic-update-slice_fusion.refs_0_), channel_id=1, source_target_pairs={{0,192},{4,196},{8,200},{12,204},{16,208},{20,212},{24,216},{28,22... | collective-permute-start | bytes 786440 | tf_op jit(solution)/shard_map/ppermute | solution.py:236
  33.0 6.9 %all-to-all-done = bf16[8,256,256]{2,1,0:T(8,128)(2,1)S(1)} async-done(((bf16[8,256,256]{2,1,0:T(8,128)(2,1)}), bf16[8,256,256]{2,1,0:T(8,128)(2,1)S(1)}, u32[]{:S(2)}, u32[]{:S(2)}) %all-to-all-start) | async-done | bytes 1048608 | tf_op jit(solution)/shard_map/all_to_all | solution.py:21
  40.0 8.2 %all-to-all-start.1 = ((bf16[64,16,128]{2,1,0:T(8,128)(2,1)}), bf16[64,16,128]{2,1,0:T(8,128)(2,1)}, u32[]{:S(2)}, u32[]{:S(2)}) async-start(bf16[64,16,128]{2,1,0:T(8,128)(2,1)} %pad_maximum_fusion), calls=%async_computation.1 | async-start | bytes 524288 | tf_op jit(solution)/shard_map/all_to_all | solution.py:258
  48.3 16.1 %attend.3 = bf16[8,272,128]{2,1,0:T(8,128)(2,1)} custom-call(bf16[2048,256]{1,0:T(8,128)(2,1)S(1)} %bitcast.37, bf16[512,256]{1,0:T(8,128)(2,1)S(1)} %constant_dynamic-update-slice_fusion.refs_0_, bf16[512,256]{1,0:T(8,128)(2,1)} %collective-permute-done.refs_1_, bf16[512,256]{1,0:T(8,128)(2,1)S(1)} %collective-permute-done.1.refs_2_, ...), custom_call_target="tpu_custom_call" | custom-call | flops 8589934592 | bytes 2097152 | tf_op jit(solution)/shard_map/attend/pallas_call | solution.py:86
  64.4 6.7 %all-to-all-start.3 = ((bf16[8,272,128]{2,1,0:T(8,128)(2,1)}), bf16[8,272,128]{2,1,0:T(8,128)(2,1)S(1)}, u32[]{:S(2)}, u32[]{:S(2)}) async-start(bf16[8,272,128]{2,1,0:T(8,128)(2,1)} %attend.3), calls=%async_computation.3 | async-start | bytes 1114112 | tf_op jit(solution)/shard_map/all_to_all | solution.py:265
  73.0 16.0 %attend.2 = bf16[8,272,128]{2,1,0:T(8,128)(2,1)} custom-call(bf16[2048,256]{1,0:T(8,128)(2,1)S(1)} %bitcast.38, bf16[512,256]{1,0:T(8,128)(2,1)S(1)} %constant_dynamic-update-slice_fusion.refs_0_, bf16[512,256]{1,0:T(8,128)(2,1)} %collective-permute-done.refs_1_, bf16[512,256]{1,0:T(8,128)(2,1)S(1)} %copy-done.6, bf16[512,256]{1,0:T(8,128)(2,1)S(1)} %copy-done.4, ...), custom_call_target="tpu_custom_call" | custom-call | flops 8589934592 | bytes 2097152 | tf_op jit(solution)/shard_map/attend/pallas_call | solution.py:86
  89.0 7.2 %all-to-all-start.2 = ((bf16[8,272,128]{2,1,0:T(8,128)(2,1)}), bf16[8,272,128]{2,1,0:T(8,128)(2,1)S(1)}, u32[]{:S(2)}, u32[]{:S(2)}) async-start(bf16[8,272,128]{2,1,0:T(8,128)(2,1)} %attend.2), calls=%async_computation.2 | async-start | bytes 1114112 | tf_op jit(solution)/shard_map/all_to_all | solution.py:265
  96.7 1.2 copy.55
  97.9 1.1 slice_bitcast_fusion
  100.2 2.6 %copy.56 = bf16[16,64,4,16]{3,0,2,1:T(8,128)(2,1)} copy(bf16[16,64,4,16]{1,3,2,0:T(8,128)(2,1)S(1)} %bitcast.46) | data formatting | bytes 262144 | tf_op jit(solution)/shard_map/transpose | solution.py:285
  102.7 1.7 convolution_bitcast_fusion
  104.4 1.4 copy.58
  105.8 1.9 reshape.102.target_ref
  107.6 5.9 %all-to-all-done.2.refs_0_ = bf16[8,272,128]{2,1,0:T(8,128)(2,1)S(1)} async-done(((bf16[8,272,128]{2,1,0:T(8,128)(2,1)}), bf16[8,272,128]{2,1,0:T(8,128)(2,1)S(1)}, u32[]{:S(2)}, u32[]{:S(2)}) %all-to-all-start.2) | async-done | bytes 557088 | tf_op jit(solution)/shard_map/all_to_all | solution.py:265
  113.5 1.5 merge.1
  115.0 11.5 %all_to_all.40 = bf16[8,32,256]{2,1,0:T(8,128)(2,1)S(1)} all-to-all(bf16[8,32,256]{2,1,0:T(8,128)(2,1)S(1)} %broadcast_in_dim.98), channel_id=1, replica_groups={{0,4,8,12,16,20,24,28},{32,36,40,44,48,52,56,60},{64,68,72,76,80,84,88,..., dimensions={0} | all-to-all | bytes 262144 | tf_op jit(solution)/shard_map/all_to_all | solution.py:21
  126.5 1.1 broadcast_in_dim.99
  127.6 7.4 %all-to-all-start.5 = ((bf16[8,8,32,256]{3,2,1,0:T(8,128)(2,1)}), bf16[8,8,32,256]{3,2,1,0:T(8,128)(2,1)S(1)}, u32[]{:S(2)}, u32[]{:S(2)}) async-start(bf16[8,8,32,256]{3,2,1,0:T(8,128)(2,1)} %broadcast_in_dim.99), calls=%async_computation.5 | async-start | bytes 2097152 | tf_op jit(solution)/shard_map/all_to_all | solution.py:21
  135.4 1.4 copy.63.id_col_ref
  136.8 11.4 %all-to-all-done.5 = bf16[8,8,32,256]{3,2,1,0:T(8,128)(2,1)S(1)} async-done(((bf16[8,8,32,256]{3,2,1,0:T(8,128)(2,1)}), bf16[8,8,32,256]{3,2,1,0:T(8,128)(2,1)S(1)}, u32[]{:S(2)}, u32[]{:S(2)}) %all-to-all-start.5) | async-done | bytes 1048608 | tf_op jit(solution)/shard_map/all_to_all | solution.py:21
  148.2 1.2 copy-done.1
  149.4 4.9 %track_means.1 = (bf16[2048,256]{1,0:T(8,128)(2,1)S(1)}, bf16[4,16,2048]{2,1,0:T(8,128)(2,1)S(1)}) custom-call(s32[2048,1]{1,0:T(8,128)S(1)} %copy-done.1, s32[1,2048]{1,0:T(1,128)S(1)} %bitcast.40, bf16[2048,256]{1,0:T(8,128)(2,1)S(1)} %bitcast.36, f32[2048,1]{1,0:T(8,128)S(1)} %copy.64.divisor_ref, bf16[16,256]{1,0:T(8,128)(2,1)S(1)} %bitcast.42), custom_call_target="tpu_custom_call" | custom-call | tf_op jit(solution)/shard_map/track_means/pallas_call | solution.py:168
  154.3 8.4 %all_to_all.41.part_ref = bf16[4,16,2048]{2,1,0:T(8,128)(2,1)S(1)} all-to-all(bf16[4,16,2048]{2,1,0:T(8,128)(2,1)S(1)} %get-tuple-element.23), channel_id=1, replica_groups=mesh['seq'=64,'head'=4] {'head'}, dimensions={0} | all-to-all | bytes 524288 | tf_op jit(solution)/shard_map/all_to_all | solution.py:305
  163.0 27.8 %all_to_all.42 = bf16[64,16,384]{2,1,0:T(8,128)(2,1)S(1)} all-to-all(bf16[64,16,384]{2,1,0:T(8,128)(2,1)S(1)} %error_messages.1), channel_id=1, replica_groups=mesh['seq'=64,'head'=4] {'seq'}, dimensions={0} | all-to-all | bytes 1572864 | tf_op jit(solution)/shard_map/all_to_all | solution.py:308
  190.9 1.2 convolution_convert_fusion
  (67 shorter events, 8.2 us)
Async XLA Ops:
  0.6 95.9 %copy-start = (bf16[256,1024]{1,0:T(8,128)(2,1)S(1)}, bf16[256,1024]{1,0:T(8,128)(2,1)}, u32[]{:S(2)}) copy-start(bf16[256,1024]{1,0:T(8,128)(2,1)} %param.13) | copy-start | bytes 1572868
  2.7 8.6 %copy-start.7 = (bf16[256,256]{1,0:T(8,128)(2,1)S(1)}, bf16[256,256]{1,0:T(8,128)(2,1)}, u32[]{:S(2)}) copy-start(bf16[256,256]{1,0:T(8,128)(2,1)} %param.10) | copy-start | bytes 393220
  2.7 37.3 %all-to-all-start = ((bf16[8,256,256]{2,1,0:T(8,128)(2,1)}), bf16[8,256,256]{2,1,0:T(8,128)(2,1)S(1)}, u32[]{:S(2)}, u32[]{:S(2)}) async-start(bf16[8,256,256]{2,1,0:T(8,128)(2,1)} %broadcast_in_dim.53), calls=%async_computation | async-start | bytes 2097152 | tf_op jit(solution)/shard_map/all_to_all | solution.py:21
  11.3 0.9 copy-start.8
  12.2 8.7 %copy-start.10 = (s32[2]{0:T(128)S(1)}, s32[2]{0:T(128)}, u32[]{:S(2)}) copy-start(s32[2]{0:T(128)} %param.16) | copy-start | bytes 28
  12.2 8.7 %copy-start.9 = (s32[2,128]{1,0:T(2,128)S(1)}, s32[2,128]{1,0:T(2,128)}, u32[]{:S(2)}) copy-start(s32[2,128]{1,0:T(2,128)} %param.17) | copy-start | bytes 3076
  12.2 11.1 %collective-permute-start.6 = (bf16[512,256]{1,0:T(8,128)(2,1)S(1)}, bf16[512,256]{1,0:T(8,128)(2,1)S(1)}, u32[]{:S(2)}, u32[]{:S(2)}) collective-permute-start(bf16[512,256]{1,0:T(8,128)(2,1)S(1)} %constant_dynamic-update-slice_fusion.refs_0_), channel_id=1, source_target_pairs={{0,96},{4,100},{8,104},{12,108},{16,112},{20,116},{24,120},{28,124... | collective-permute-start | bytes 786440 | tf_op jit(solution)/shard_map/ppermute | solution.py:236
  12.8 15.0 %collective-permute-start.5 = (bf16[512,256]{1,0:T(8,128)(2,1)S(1)}, bf16[512,256]{1,0:T(8,128)(2,1)S(1)}, u32[]{:S(2)}, u32[]{:S(2)}) collective-permute-start(bf16[512,256]{1,0:T(8,128)(2,1)S(1)} %constant_dynamic-update-slice_fusion.refs_0_), channel_id=1, source_target_pairs={{0,32},{4,36},{8,40},{12,44},{16,48},{20,52},{24,56},{28,60},{32,6... | collective-permute-start | bytes 786440 | tf_op jit(solution)/shard_map/ppermute | solution.py:236
  14.3 33.9 %collective-permute-start.4 = (bf16[512,256]{1,0:T(8,128)(2,1)S(1)}, bf16[512,256]{1,0:T(8,128)(2,1)S(1)}, u32[]{:S(2)}, u32[]{:S(2)}) collective-permute-start(bf16[512,256]{1,0:T(8,128)(2,1)S(1)} %constant_dynamic-update-slice_fusion.refs_0_), channel_id=1, source_target_pairs={{0,128},{4,132},{8,136},{12,140},{16,144},{20,148},{24,152},{28,15... | collective-permute-start | bytes 786440 | tf_op jit(solution)/shard_map/ppermute | solution.py:236
  17.5 30.7 %collective-permute-start.3 = (bf16[512,256]{1,0:T(8,128)(2,1)S(1)}, bf16[512,256]{1,0:T(8,128)(2,1)S(1)}, u32[]{:S(2)}, u32[]{:S(2)}) collective-permute-start(bf16[512,256]{1,0:T(8,128)(2,1)S(1)} %constant_dynamic-update-slice_fusion.refs_0_), channel_id=1, source_target_pairs={{0,64},{4,68},{8,72},{12,76},{16,80},{20,84},{24,88},{28,92},{32,9... | collective-permute-start | bytes 786440 | tf_op jit(solution)/shard_map/ppermute | solution.py:236
  20.8 27.4 %collective-permute-start.2 = (bf16[512,256]{1,0:T(8,128)(2,1)S(1)}, bf16[512,256]{1,0:T(8,128)(2,1)S(1)}, u32[]{:S(2)}, u32[]{:S(2)}) collective-permute-start(bf16[512,256]{1,0:T(8,128)(2,1)S(1)} %constant_dynamic-update-slice_fusion.refs_0_), channel_id=1, source_target_pairs={{0,224},{4,228},{8,232},{12,236},{16,240},{20,244},{24,248},{28,25... | collective-permute-start | bytes 786440 | tf_op jit(solution)/shard_map/ppermute | solution.py:236
  22.2 0.9 copy-start.11
  23.3 24.9 %collective-permute-start.1 = (bf16[512,256]{1,0:T(8,128)(2,1)S(1)}, bf16[512,256]{1,0:T(8,128)(2,1)S(1)}, u32[]{:S(2)}, u32[]{:S(2)}) collective-permute-start(bf16[512,256]{1,0:T(8,128)(2,1)S(1)} %constant_dynamic-update-slice_fusion.refs_0_), channel_id=1, source_target_pairs={{0,160},{4,164},{8,168},{12,172},{16,176},{20,180},{24,184},{28,18... | collective-permute-start | bytes 786440 | tf_op jit(solution)/shard_map/ppermute | solution.py:236
  27.8 20.5 %collective-permute-start = (bf16[512,256]{1,0:T(8,128)(2,1)S(1)}, bf16[512,256]{1,0:T(8,128)(2,1)}, u32[]{:S(2)}, u32[]{:S(2)}) collective-permute-start(bf16[512,256]{1,0:T(8,128)(2,1)S(1)} %constant_dynamic-update-slice_fusion.refs_0_), channel_id=1, source_target_pairs={{0,192},{4,196},{8,200},{12,204},{16,208},{20,212},{24,216},{28,22... | collective-permute-start | bytes 786440 | tf_op jit(solution)/shard_map/ppermute | solution.py:236
  40.0 24.4 %all-to-all-start.1 = ((bf16[64,16,128]{2,1,0:T(8,128)(2,1)}), bf16[64,16,128]{2,1,0:T(8,128)(2,1)}, u32[]{:S(2)}, u32[]{:S(2)}) async-start(bf16[64,16,128]{2,1,0:T(8,128)(2,1)} %pad_maximum_fusion), calls=%async_computation.1 | async-start | bytes 524288 | tf_op jit(solution)/shard_map/all_to_all | solution.py:258
  48.2 16.1 %copy-start.3 = (bf16[512,256]{1,0:T(8,128)(2,1)}, bf16[512,256]{1,0:T(8,128)(2,1)S(1)}, u32[]{:S(2)}) copy-start(bf16[512,256]{1,0:T(8,128)(2,1)S(1)} %collective-permute-done.2.refs_3_) | copy-start | bytes 786436
  48.3 16.1 %copy-start.5 = (bf16[512,256]{1,0:T(8,128)(2,1)}, bf16[512,256]{1,0:T(8,128)(2,1)S(1)}, u32[]{:S(2)}) copy-start(bf16[512,256]{1,0:T(8,128)(2,1)S(1)} %collective-permute-done.1.refs_2_) | copy-start | bytes 786436
  64.4 24.6 %all-to-all-start.3 = ((bf16[8,272,128]{2,1,0:T(8,128)(2,1)}), bf16[8,272,128]{2,1,0:T(8,128)(2,1)S(1)}, u32[]{:S(2)}, u32[]{:S(2)}) async-start(bf16[8,272,128]{2,1,0:T(8,128)(2,1)} %attend.3), calls=%async_computation.3 | async-start | bytes 1114112 | tf_op jit(solution)/shard_map/all_to_all | solution.py:265
  71.1 1.0 copy-start.4
  72.1 0.9 copy-start.6
  89.0 24.5 %all-to-all-start.2 = ((bf16[8,272,128]{2,1,0:T(8,128)(2,1)}), bf16[8,272,128]{2,1,0:T(8,128)(2,1)S(1)}, u32[]{:S(2)}, u32[]{:S(2)}) async-start(bf16[8,272,128]{2,1,0:T(8,128)(2,1)} %attend.2), calls=%async_computation.2 | async-start | bytes 1114112 | tf_op jit(solution)/shard_map/all_to_all | solution.py:265
  105.7 7.7 %copy-start.2 = (bf16[256,256]{1,0:T(8,128)(2,1)S(1)}, bf16[256,256]{1,0:T(8,128)(2,1)}, u32[]{:S(2)}) copy-start(bf16[256,256]{1,0:T(8,128)(2,1)} %refs_2_.1) | copy-start | bytes 393220
  127.6 20.6 %all-to-all-start.5 = ((bf16[8,8,32,256]{3,2,1,0:T(8,128)(2,1)}), bf16[8,8,32,256]{3,2,1,0:T(8,128)(2,1)S(1)}, u32[]{:S(2)}, u32[]{:S(2)}) async-start(bf16[8,8,32,256]{3,2,1,0:T(8,128)(2,1)} %broadcast_in_dim.99), calls=%async_computation.5 | async-start | bytes 2097152 | tf_op jit(solution)/shard_map/all_to_all | solution.py:21
  148.2 1.2 copy-start.1

commit v3 on v2

v3 whole, which is shorter than its diff:
```python
import functools

import jax
import jax.numpy as jnp
from jax import lax
from jax.experimental import pallas as pl
from jax.experimental.pallas import tpu as pltpu
from jax.sharding import PartitionSpec as P

HEAD_DIM = 64
BLK = 128
POOL = 16
SIDE = 8
LOG2E = 1.4426950408889634
STAT = 16
VMEM_BYTES = 24 * 1024 * 1024

GROUP_Z = [[g * SIDE + i for i in range(SIDE)] for g in range(SIDE)]
GROUP_YX = [[g * SIDE + i for g in range(SIDE)] for i in range(SIDE)]


def spread(x, groups):
    wide = jnp.broadcast_to(x[None], (SIDE, *x.shape))
    return lax.all_to_all(wide, "seq", 0, 0, axis_index_groups=groups)


def shift(seq_count, dg):
    dy, dx = dg // 4, dg % 4
    pairs = []
    for g in range(seq_count // SIDE):
        to = (g // 4 + dy) % 2 * 4 + (g % 4 + dx) % 4
        pairs += [(g * SIDE + i, to * SIDE + i) for i in range(SIDE)]
    return pairs


def attend_kernel(riders, q_ref, *refs):
    extra_refs, kv_refs, (o_ref, k_own, v_own) = refs[:riders], refs[riders:-3], refs[-3:]
    rows = q_ref.shape[0]
    lane = lax.broadcasted_iota(jnp.int32, (1, 128), 1)
    first = lane < HEAD_DIM

    @pl.when(pl.program_id(0) == 0)
    def _():
        zero = jnp.zeros((), jnp.bfloat16)
        one = jnp.ones((), jnp.bfloat16)
        for i, kv_ref in enumerate(kv_refs):
            n = kv_ref.shape[0] // 2
            span = pl.ds(i * n, n)
            k = kv_ref[:n]
            v = kv_ref[n:]
            k_own[0, span] = jnp.where(first, k, zero)
            k_own[1, span] = jnp.where(first, zero, k)
            v_own[0, span] = jnp.where(first, v, one)
            v_own[1, span] = jnp.where(first, one, v)

    scale = LOG2E * HEAD_DIM ** (-0.5)
    q = q_ref[...]
    tops, sums = [], []
    for h in range(2):
        s = lax.dot_general(
            q, k_own[h], (((1,), (1,)), ((), ())), preferred_element_type=jnp.float32
        )
        top = jnp.max(s, axis=1, keepdims=True)
        p = jnp.exp2((s - top) * scale).astype(jnp.bfloat16)
        sums.append(jnp.dot(p, v_own[h], preferred_element_type=jnp.float32))
        tops.append(top * scale)
    num = jnp.where(first, sums[0], sums[1])
    den_other = jnp.where(first, sums[1], sums[0])
    den = pltpu.roll(den_other, HEAD_DIM, 1)
    o_ref[0, :rows] = (num / den).astype(jnp.bfloat16)
    lse = jnp.where(first, tops[1], tops[0]) + jnp.log2(den_other)
    turned = lse.T
    left = jnp.concatenate([turned[HEAD_DIM : HEAD_DIM + 1], turned[0:1]], axis=0)
    left = jnp.concatenate([left[:, :128], left[:, 128:]], axis=0)
    hi = left.astype(jnp.bfloat16)
    rest = left - hi.astype(jnp.float32)
    mid = rest.astype(jnp.bfloat16)
    rest = rest - mid.astype(jnp.float32)
    pad = jnp.zeros_like(left)
    if riders:
        piece_ref, count_ref = extra_refs
        pad = jnp.concatenate([count_ref[...], pad[1:]], axis=0)
        o_ref[0, rows + STAT :] = piece_ref[0]
    o_ref[0, rows : rows + STAT] = jnp.concatenate(
        [hi.astype(jnp.float32), mid.astype(jnp.float32), rest, pad], axis=0
    ).astype(jnp.bfloat16)


def attend(queries, pieces, pair, riders):
    n = queries.shape[0]
    rows = n // SIDE
    keys_n = sum(x.shape[0] for x in pieces) // 2
    out_rows = rows + STAT
    rider_specs = []
    if riders:
        rider_specs = [
            pl.BlockSpec((1, *riders[0].shape[1:]), lambda i: (i, 0, 0)),
            pl.BlockSpec(riders[1].shape, lambda i: (0, 0)),
        ]
        out_rows = out_rows + riders[0].shape[1]
    return pl.pallas_call(
        functools.partial(attend_kernel, len(riders)),
        grid=(SIDE,),
        in_specs=[pl.BlockSpec((rows, 128), lambda i: (i, pair))]
        + rider_specs
        + [pl.BlockSpec((x.shape[0], 128), lambda i: (0, pair)) for x in pieces],
        out_specs=pl.BlockSpec((1, out_rows, 128), lambda i: (i, 0, 0)),
        out_shape=jax.ShapeDtypeStruct((SIDE, out_rows, 128), jnp.bfloat16),
        scratch_shapes=[
            pltpu.VMEM((2, keys_n, 128), jnp.bfloat16),
            pltpu.VMEM((2, keys_n, 128), jnp.bfloat16),
        ],
        compiler_params=pltpu.CompilerParams(vmem_limit_bytes=VMEM_BYTES),
        cost_estimate=pl.CostEstimate(
            flops=2 * 2 * 2 * n * keys_n * 256,
            bytes_accessed=8 * n * 128,
            transcendentals=2 * n * keys_n,
        ),
        name="attend",
    )(queries, *riders, *pieces)


def merge_kernel(*refs):
    part_refs, (residual_ref, sel_ref, out_ref, rider_ref) = refs[:-4], refs[-4:]
    rows = residual_ref.shape[0]
    lane = lax.broadcasted_iota(jnp.int32, (1, 128), 1)
    first = lane < HEAD_DIM
    scaled = []
    for part_ref in part_refs:
        stats = part_ref[:, rows : rows + STAT, :].astype(jnp.float32)
        merged = stats[:, 0:4] + stats[:, 4:8] + stats[:, 8:12]
        for h in range(2):
            x = jnp.concatenate([merged[:, h], merged[:, 2 + h]], axis=1)
            w = jnp.exp2(x - jnp.max(x, axis=0, keepdims=True))
            scaled.append(w / jnp.sum(w, axis=0, keepdims=True))
    weights = jnp.concatenate(scaled, axis=0)
    weights = jnp.concatenate(
        [weights, jnp.zeros((128 - weights.shape[0], rows), jnp.float32)], axis=0
    ).T
    streams = []
    for p, part_ref in enumerate(part_refs):
        cols = slice(p * 128, p * 128 + 128)
        total = jnp.zeros((rows, 128), jnp.float32)
        for j in range(SIDE):
            a = (2 * p) * SIDE + j
            b = (2 * p + 1) * SIDE + j
            w = jnp.where(first, weights[:, a : a + 1], weights[:, b : b + 1])
            total = total + w * part_ref[j, :rows].astype(jnp.float32)
        context = total.astype(jnp.bfloat16).astype(jnp.float32)
        streams.append(
            (residual_ref[:, cols].astype(jnp.float32) + context).astype(jnp.bfloat16)
        )
    stream = jnp.concatenate(streams, axis=1)
    pooled = jnp.dot(sel_ref[...], stream, preferred_element_type=jnp.float32).astype(jnp.bfloat16)
    for j in range(SIDE):
        out_ref[j] = pooled

    carried = part_refs[0][:, rows + STAT :].astype(jnp.float32)
    counts = part_refs[0][:, rows : rows + STAT].astype(jnp.float32)[:, 12:13]
    back = sel_ref.shape[0]
    per = 128 // back
    count_tiles = []
    for half in range(SIDE // per):
        tile = jnp.zeros((1, 128), jnp.float32)
        for q in range(per):
            row = counts[half * per + q]
            row = pltpu.roll(row, q * back, 1) if q else row
            tile = jnp.where(lane // back == q, row, tile)
        count_tiles.append(tile)
    count_row = jnp.concatenate(count_tiles, axis=1)
    tail = jnp.concatenate([count_row, jnp.zeros((15, count_row.shape[1]), jnp.float32)], axis=0)
    for g in range(SIDE):
        span = slice(g * 8, g * 8 + 8)
        halves = [
            jnp.concatenate([carried[half * 4 + q, span] for q in range(4)], axis=0)
            for half in range(2)
        ]
        rider_ref[g] = jnp.concatenate(
            [jnp.concatenate(halves, axis=1), tail], axis=0
        ).astype(jnp.bfloat16)


def merge(parts, residual, sel):
    back, width = sel.shape[0], residual.shape[1]
    return pl.pallas_call(
        merge_kernel,
        out_shape=[
            jax.ShapeDtypeStruct((SIDE, back, width), jnp.bfloat16),
            jax.ShapeDtypeStruct((SIDE, 48, 256), jnp.bfloat16),
        ],
        compiler_params=pltpu.CompilerParams(vmem_limit_bytes=VMEM_BYTES),
        name="merge",
    )(*parts, residual, sel)


def column(row):
    return jnp.broadcast_to(row, (128, row.shape[1])).T[:, :1]


def track_kernel(ids_here_ref, ids_ref, every_ref, weight_ref, mean_ref, part_ref, divisor_ref):
    step = mean_ref.shape[0]
    here = column(ids_here_ref[...])
    sums = jnp.zeros(mean_ref.shape, jnp.float32)
    counts = jnp.zeros((step, step), jnp.float32)
    for g in range(SIDE):
        match = here == ids_ref[:, g * step : g * step + step]
        sums = sums + jnp.dot(
            jnp.where(match, 1.0, 0.0).astype(jnp.bfloat16),
            every_ref[g, :step],
            preferred_element_type=jnp.float32,
        )
        count_row = every_ref[g, step + 32 :].astype(jnp.float32)[:1]
        counts = counts + jnp.where(match, count_row, 0.0)
    divisor = jnp.maximum(jnp.sum(counts, axis=1, keepdims=True), 1.0)
    divisor_ref[...] = jnp.broadcast_to(divisor, divisor_ref.shape)
    mean = (sums / divisor).astype(jnp.bfloat16)
    mean_ref[...] = mean
    part = lax.dot_general(
        weight_ref[...], mean, (((1,), (1,)), ((), ())), preferred_element_type=jnp.float32
    ).astype(jnp.bfloat16)
    for h in range(part_ref.shape[0]):
        part_ref[h] = part


def track_means(ids, every, weight, head_count):
    width = every.shape[2]
    rows = ids.shape[1]
    chunk = weight.shape[0]
    step = rows // SIDE
    return pl.pallas_call(
        track_kernel,
        grid=(SIDE,),
        in_specs=[
            pl.BlockSpec((1, step), lambda i: (0, i)),
            pl.BlockSpec((1, rows), lambda i: (0, 0)),
            pl.BlockSpec(every.shape, lambda i: (0, 0, 0)),
            pl.BlockSpec((chunk, width), lambda i: (0, 0)),
        ],
        out_specs=[
            pl.BlockSpec((step, width), lambda i: (i, 0)),
            pl.BlockSpec((head_count, chunk, step), lambda i: (0, 0, i)),
            pl.BlockSpec((step, 128), lambda i: (i, 0)),
        ],
        out_shape=[
            jax.ShapeDtypeStruct((rows, width), jnp.bfloat16),
            jax.ShapeDtypeStruct((head_count, chunk, rows), jnp.bfloat16),
            jax.ShapeDtypeStruct((rows, 128), jnp.float32),
        ],
        compiler_params=pltpu.CompilerParams(vmem_limit_bytes=VMEM_BYTES),
        name="track_means",
    )(ids, ids, every, weight)


def error_kernel(track_ref, part_ref, every_ref, leader_ref, mean_ref, out_ref, target_buf):
    back = part_ref.shape[2] // out_ref.shape[0]
    width = mean_ref.shape[1]
    step = part_ref.shape[2] // SIDE
    for g in range(SIDE):
        carried = every_ref[g, step : step + 32].astype(jnp.float32)
        for z in range(SIDE):
            target_buf[g * SIDE + z] = carried[
                z % 4 * 8 : z % 4 * 8 + 8, z // 4 * 128 : z // 4 * 128 + 128
            ]
    lane = lax.broadcasted_iota(jnp.int32, (8, 128), 1)
    tiles = []
    for group in range(part_ref.shape[2] // 128):
        low = jnp.zeros((8, 128), jnp.float32)
        high = jnp.zeros((8, 128), jnp.float32)
        for j in range(8):
            track = track_ref[group * 8 + j]
            tile = target_buf[track // 4]
            turn = j * POOL + 128 - track % 4 * POOL
            here = lane // POOL == j
            low = jnp.where(here, pltpu.roll(tile, lax.rem(turn, 128), 1), low)
            high = jnp.where(here, pltpu.roll(tile, lax.rem(turn + 64, 128), 1), high)
        tiles.append(jnp.concatenate([low, high], axis=0))
    target = jnp.concatenate(tiles, axis=1)
    total = part_ref[0].astype(jnp.float32)
    for h in range(1, part_ref.shape[0]):
        total = total + part_ref[h].astype(jnp.float32)
    error = (total - target).astype(jnp.bfloat16).astype(jnp.float32)
    grad = jnp.dot(
        (error * leader_ref[...]).astype(jnp.bfloat16),
        mean_ref[...],
        preferred_element_type=jnp.float32,
    ).astype(jnp.bfloat16)
    per = 128 // back
    for s in range(out_ref.shape[0]):
        tile = error[:, s // per * 128 : s // per * 128 + 128]
        turn = s % per * back
        rows = pltpu.roll(tile, 128 - turn, 1) if turn else tile
        out_ref[s, :, :width] = grad
        out_ref[s, :, width:] = rows.astype(jnp.bfloat16)


def error_messages(tracks, partial, every, leader, mean, seq_count):
    chunk = partial.shape[1]
    vmem = pl.BlockSpec(memory_space=pltpu.VMEM)
    return pl.pallas_call(
        error_kernel,
        in_specs=[pl.BlockSpec(memory_space=pltpu.SMEM), vmem, vmem, vmem, vmem],
        out_shape=jax.ShapeDtypeStruct((seq_count, chunk, mean.shape[1] + 128), jnp.bfloat16),
        scratch_shapes=[pltpu.VMEM((seq_count, 8, 128), jnp.float32)],
        compiler_params=pltpu.CompilerParams(vmem_limit_bytes=VMEM_BYTES),
        name="error_messages",
    )(tracks, partial, every, leader, mean)


def finish_kernel(index_ref, final_ref, weight_ref, sel_ref, divisor_ref, grad_ref, context_ref):
    width = weight_ref.shape[0]
    back = sel_ref.shape[0]
    for i in range(final_ref.shape[0] // width):
        span = slice(i * width, i * width + width)
        grad_ref[:, span] = final_ref[span, :width].T
    mean_grad = jnp.dot(
        weight_ref[...], final_ref[:, width:], preferred_element_type=jnp.float32
    ).T[:back]
    track_grad = (mean_grad / divisor_ref[:, :1]).astype(jnp.bfloat16)
    context_ref[...] = lax.dot_general(
        sel_ref[...], track_grad, (((0,), (0,)), ((), ())), preferred_element_type=jnp.float32
    ).astype(jnp.bfloat16)


def finish(index, final, weight, sel, divisor):
    width, target_d = weight.shape
    back, tok_rows = sel.shape
    whole = lambda *shape: pl.BlockSpec(shape, lambda i, at: (0, 0))
    return pl.pallas_call(
        finish_kernel,
        grid_spec=pltpu.PrefetchScalarGridSpec(
            num_scalar_prefetch=1,
            grid=(1,),
            in_specs=[
                whole(*final.shape),
                whole(*weight.shape),
                whole(*sel.shape),
                pl.BlockSpec((back, 128), lambda i, at: (at[0], 0)),
            ],
            out_specs=[whole(width, target_d), whole(tok_rows, width)],
        ),
        out_shape=[
            jax.ShapeDtypeStruct((width, target_d), jnp.bfloat16),
            jax.ShapeDtypeStruct((tok_rows, width), jnp.bfloat16),
        ],
        compiler_params=pltpu.CompilerParams(vmem_limit_bytes=VMEM_BYTES),
        name="finish",
    )(index.reshape(1).astype(jnp.int32), final, weight, sel, divisor)


def local(queries, keys, values, residual, reg_weight, targets, block_track, row_count, pool_slot):
    tok_rows, width = queries.shape
    here = tok_rows // BLK
    seq_count = lax.axis_size("seq")
    head_count = lax.axis_size("head")
    seq_index = lax.axis_index("seq")
    blocks = here * seq_count
    target_d = reg_weight.shape[1]
    chunk = target_d // seq_count
    owned = targets.shape[0]

    own_kv = jnp.concatenate([keys, values], axis=0)
    pieces = [own_kv] + [
        lax.ppermute(own_kv, "seq", shift(seq_count, d)) for d in (6, 5, 7, 2, 4, 1, 3)
    ]
    query_all = spread(queries, GROUP_Z).reshape(SIDE * tok_rows, width)

    valid = jnp.arange(BLK, dtype=jnp.int32)[None, :] < row_count[:, None]
    match = pool_slot[:, None, :] == jnp.arange(POOL, dtype=jnp.int32)[None, :, None]
    sel = match & valid[:, None, :]
    same_block = jnp.arange(here)[:, None] == jnp.arange(here)[None, :]
    selector = (
        jnp.where(sel[:, :, None, :] & same_block[:, None, :, None], 1.0, 0.0)
        .astype(jnp.bfloat16)
        .reshape(here * POOL, tok_rows)
    )
    slot_rows = jnp.sum(jnp.where(sel, 1.0, 0.0), axis=2).reshape(1, here * POOL)
    slot_rows = jnp.pad(slot_rows, ((0, 0), (0, 128 - here * POOL)))
    turned = targets.reshape(owned * POOL, target_d).T
    turned = turned.reshape(SIDE, SIDE, 2, chunk // 2, owned * POOL).transpose(1, 0, 2, 3, 4)
    carried = jnp.concatenate([turned[:, :, 0], turned[:, :, 1]], axis=3)
    carried = carried.reshape(SIDE, SIDE * chunk // 2, 128)
    same = block_track[:, None] == block_track[None, :]
    earlier = jnp.arange(blocks)[None, :] < jnp.arange(blocks)[:, None]
    leader = jnp.where(jnp.any(same & earlier, axis=1), 0.0, 1.0)
    leader = jnp.repeat(leader, POOL).reshape(1, blocks * POOL)
    ids = (
        (block_track[:, None] * POOL + jnp.arange(POOL, dtype=jnp.int32)[None, :])
        .reshape(1, blocks * POOL)
        .astype(jnp.float32)
    )
    chunk_weight = lax.dynamic_slice_in_dim(reg_weight, seq_index * chunk, chunk, axis=1).T

    part = attend(query_all, pieces, 0, (carried, slot_rows))
    part, query_all, selector, leader, ids, chunk_weight = lax.optimization_barrier(
        (part, query_all, selector, leader, ids, chunk_weight)
    )
    parts = [lax.all_to_all(part, "seq", 0, 0, axis_index_groups=GROUP_Z)]
    for pair in range(1, width // 128):
        part = attend(query_all, pieces, pair, ())
        parts[-1], part = lax.optimization_barrier((parts[-1], part))
        parts.append(lax.all_to_all(part, "seq", 0, 0, axis_index_groups=GROUP_Z))

    pooled, rider = merge(parts, residual, selector)
    pooled = lax.all_to_all(pooled, "seq", 0, 0, axis_index_groups=GROUP_Z)
    pooled = pooled.reshape(1, blocks * POOL // SIDE, width)
    every = jnp.concatenate(
        [jnp.broadcast_to(pooled, (SIDE, *pooled.shape[1:])), rider], axis=1
    )
    every = lax.all_to_all(every, "seq", 0, 0, axis_index_groups=GROUP_YX)
    mean, partial, divisor = track_means(ids, every, chunk_weight, head_count)
    partial = lax.all_to_all(partial, "head", 0, 0)
    final = error_messages(block_track, partial, every, leader, mean, seq_count)
    final = lax.all_to_all(final, "seq", 0, 0).reshape(target_d, width + 128)
    return finish(seq_index, final, reg_weight, selector, divisor)


def solution(mesh):
    return jax.shard_map(
        local,
        mesh=mesh,
        in_specs=(
            P("seq", "head"),
            P("seq", "head"),
            P("seq", "head"),
            P("seq", "head"),
            P("head", None),
            P("seq", None, None),
            P(),
            P("seq"),
            P("seq", None),
        ),
        out_specs=(P("head", None), P("seq", "head")),
        check_vma=False,
    )
```

time: 196 us -> 199 us (1.015)
  blocking collectives: 47.7 us -> 92.7 us
  starting transfers between devices: 56.4 us -> 26.5 us
  local copies, waits for them, and re-layouts: 20.6 us -> 14.4 us
  waiting for transfers between devices: 24.2 us -> 18.5 us
  Pallas kernels: 38.8 us -> 43.2 us
  matrix products: 3.04 us -> 0 us
    all_to_all x1 -> x3, blocking collectives: 11.5 us -> 56.5 us  [the longest x1 23.8 us: local(): parts.append(lax.all_to_all(part, 'seq', 0, 0, axis_index_groups=GROUP_Z))]
    all_to_all x3 -> x1, starting transfers between devices: 22.1 us -> 3.55 us  [local(): parts = [lax.all_to_all(part, 'seq', 0, 0, axis_index_groups=GROUP_Z)]]
    all_to_all x2 -> x1, waiting for transfers between devices: 18.3 us -> 8.27 us  [spread(): return lax.all_to_all(wide, 'seq', 0, 0, axis_index_groups=groups)]
    ppermute x7, waiting for transfers between devices: 0.02 us -> 9.03 us  [local(): lax.ppermute(own_kv, 'seq', shift(seq_count, d))]
    all_to_all x2 -> x1, starting transfers between devices: 16 us -> 8.61 us  [spread(): return lax.all_to_all(wide, 'seq', 0, 0, axis_index_groups=groups)]
    transpose x5 -> x1, local copies, waits for them, and re-layouts: 6.55 us -> 0.86 us  [local(): turned = targets.reshape(owned * POOL, target_d).T]
    all_to_all x3 -> x1, waiting for transfers between devices: 5.86 us -> 1.22 us  [local(): parts = [lax.all_to_all(part, 'seq', 0, 0, axis_index_groups=GROUP_Z)]]
    pallas_call x5 -> x6, Pallas kernels: 38.8 us -> 43.2 us  [the longest x2 31.4 us: attend(): pl.pallas_call(functools.partial(attend_kernel, len(riders)), grid=(SIDE,...]
  transfers between devices with their start and end apart: 12 -> 9, of which waited for: 3 -> 4; matrix products, arithmetic and copies ran while one was open for 8% -> 3% of each run, Pallas kernels for 17% -> 8%
where the time goes in v3:
time: 199 us; the launch traced here: 197 us
  blocking collectives  92.7 us (47%)
  Pallas kernels  43.2 us (22%)
  starting transfers between devices  26.5 us (13%)
  waiting for transfers between devices  18.5 us (9%)
  local copies, waits for them, and re-layouts  14.4 us (7%)
    pallas_call x2, Pallas kernels, attend(): pl.pallas_call(functools.partial(attend_kernel, len(riders)), grid=(SIDE,...  31.4 us
    all_to_all x1, blocking collectives, local(): final = lax.all_to_all(final, 'seq', 0, 0).reshape(target_d, width + 128)  27.8 us
    all_to_all x1, blocking collectives, local(): parts.append(lax.all_to_all(part, 'seq', 0, 0, axis_index_groups=GROUP_Z))  23.8 us
    all_to_all x1, blocking collectives, local(): every = lax.all_to_all(every, 'seq', 0, 0, axis_index_groups=GROUP_YX)  21.2 us
    ppermute x7, starting transfers between devices, local(): lax.ppermute(own_kv, 'seq', shift(seq_count, d))  14.3 us
    all_to_all x1, blocking collectives, local(): pooled = lax.all_to_all(pooled, 'seq', 0, 0, axis_index_groups=GROUP_Z)  11.5 us
    unnamed x39, local copies, waits for them, and re-layouts  9.06 us
    ppermute x7, waiting for transfers between devices, local(): lax.ppermute(own_kv, 'seq', shift(seq_count, d))  9.03 us
  transfers between devices with their start and end apart: 9, of which 4 were waited for; matrix products, arithmetic and copies ran while one was open for 3% of the time, Pallas kernels for 8%

profile of v3, /device:TPU:2, one launch (start us, length us, event | category | flops | bytes accessed | tf_op | source)
XLA Modules:
  0.0 196.9 jit_solution(14396314653880646199)
XLA Ops:
  1.5 0.9 constant_dynamic-update-slice_fusion.refs_2_.refs_0_
  2.5 2.3 %collective-permute-start.6 = (bf16[512,256]{1,0:T(8,128)(2,1)S(1)}, bf16[512,256]{1,0:T(8,128)(2,1)S(1)}, u32[]{:S(2)}, u32[]{:S(2)}) collective-permute-start(bf16[512,256]{1,0:T(8,128)(2,1)S(1)} %constant_dynamic-update-slice_fusion.refs_2_.refs_0_), channel_id=1, source_target_pairs={{0,96},{4,100},{8,104},{12,108},{16,112},{20,116},{24,120},{28,124... | collective-permute-start | bytes 786440 | tf_op jit(solution)/shard_map/ppermute | solution.py:363
  4.8 2.9 %collective-permute-start.4 = (bf16[512,256]{1,0:T(8,128)(2,1)S(1)}, bf16[512,256]{1,0:T(8,128)(2,1)S(1)}, u32[]{:S(2)}, u32[]{:S(2)}) collective-permute-start(bf16[512,256]{1,0:T(8,128)(2,1)S(1)} %constant_dynamic-update-slice_fusion.refs_2_.refs_0_), channel_id=1, source_target_pairs={{0,128},{4,132},{8,136},{12,140},{16,144},{20,148},{24,152},{28,15... | collective-permute-start | bytes 786440 | tf_op jit(solution)/shard_map/ppermute | solution.py:363
  7.8 3.3 %collective-permute-start.3 = (bf16[512,256]{1,0:T(8,128)(2,1)S(1)}, bf16[512,256]{1,0:T(8,128)(2,1)S(1)}, u32[]{:S(2)}, u32[]{:S(2)}) collective-permute-start(bf16[512,256]{1,0:T(8,128)(2,1)S(1)} %constant_dynamic-update-slice_fusion.refs_2_.refs_0_), channel_id=1, source_target_pairs={{0,64},{4,68},{8,72},{12,76},{16,80},{20,84},{24,88},{28,92},{32,9... | collective-permute-start | bytes 786440 | tf_op jit(solution)/shard_map/ppermute | solution.py:363
  11.1 2.0 %broadcast_in_dim.32 = bf16[8,256,256]{2,1,0:T(8,128)(2,1)} broadcast(bf16[256,256]{1,0:T(8,128)(2,1)} %param.9), dimensions={1,2} | broadcast | bytes 1179648 | tf_op jit(solution)/shard_map/broadcast_in_dim | solution.py:23
  13.1 8.6 %all-to-all-start = ((bf16[8,256,256]{2,1,0:T(8,128)(2,1)}), bf16[8,256,256]{2,1,0:T(8,128)(2,1)S(1)}, u32[]{:S(2)}, u32[]{:S(2)}) async-start(bf16[8,256,256]{2,1,0:T(8,128)(2,1)} %broadcast_in_dim.32), calls=%async_computation | async-start | bytes 2097152 | tf_op jit(solution)/shard_map/all_to_all | solution.py:24
  23.7 1.0 fusion.4
  24.7 4.5 %collective-permute-start.1 = (bf16[512,256]{1,0:T(8,128)(2,1)S(1)}, bf16[512,256]{1,0:T(8,128)(2,1)S(1)}, u32[]{:S(2)}, u32[]{:S(2)}) collective-permute-start(bf16[512,256]{1,0:T(8,128)(2,1)S(1)} %constant_dynamic-update-slice_fusion.refs_2_.refs_0_), channel_id=1, source_target_pairs={{0,160},{4,164},{8,168},{12,172},{16,176},{20,180},{24,184},{28,18... | collective-permute-start | bytes 786440 | tf_op jit(solution)/shard_map/ppermute | solution.py:363
  29.2 1.2 collective-permute-start
  30.6 6.1 %collective-permute-done.1.refs_4_.refs_2_ = bf16[512,256]{1,0:T(8,128)(2,1)S(1)} collective-permute-done((bf16[512,256]{1,0:T(8,128)(2,1)S(1)}, bf16[512,256]{1,0:T(8,128)(2,1)S(1)}, u32[]{:S(2)}, u32[]{:S(2)}) %collective-permute-start.1) | collective-permute-done | bytes 262176 | tf_op jit(solution)/shard_map/ppermute | solution.py:363
  37.5 2.9 %collective-permute-done.refs_3_.refs_1_ = bf16[512,256]{1,0:T(8,128)(2,1)S(1)} collective-permute-done((bf16[512,256]{1,0:T(8,128)(2,1)S(1)}, bf16[512,256]{1,0:T(8,128)(2,1)S(1)}, u32[]{:S(2)}, u32[]{:S(2)}) %collective-permute-start) | collective-permute-done | bytes 262176 | tf_op jit(solution)/shard_map/ppermute | solution.py:363
  41.1 8.3 %all-to-all-done = bf16[8,256,256]{2,1,0:T(8,128)(2,1)S(1)} async-done(((bf16[8,256,256]{2,1,0:T(8,128)(2,1)}), bf16[8,256,256]{2,1,0:T(8,128)(2,1)S(1)}, u32[]{:S(2)}, u32[]{:S(2)}) %all-to-all-start) | async-done | bytes 1048608 | tf_op jit(solution)/shard_map/all_to_all | solution.py:24
  49.3 0.9 copy-done.10
  50.3 0.9 copy-done.13
  51.2 16.0 %attend.2 = bf16[8,336,128]{2,1,0:T(8,128)(2,1)} custom-call(bf16[2048,256]{1,0:T(8,128)(2,1)S(1)} %bitcast.21, bf16[8,64,128]{2,1,0:T(8,128)(2,1)S(1)} %pad_maximum_fusion.1.refs_0_, f32[1,128]{1,0:T(1,128)S(1)} %pad.4.refs_1_, bf16[512,256]{1,0:T(8,128)(2,1)S(1)} %constant_dynamic-update-slice_fusion.refs_2_.refs_0_, bf16[512,256]{1,0:T(8,128)(2,1)S(1)} %copy-done.13, ...), custom_call_target="tpu_custom_call" | custom-call | flops 8589934592 | bytes 2097152 | tf_op jit(solution)/shard_map/attend/pallas_call | solution.py:101
  67.3 3.6 %all-to-all-start.1 = ((bf16[8,336,128]{2,1,0:T(8,128)(2,1)}), bf16[8,336,128]{2,1,0:T(8,128)(2,1)S(1)}, u32[]{:S(2)}, u32[]{:S(2)}) async-start(bf16[8,336,128]{2,1,0:T(8,128)(2,1)} %attend.2), calls=%async_computation.1 | async-start | bytes 1376256 | tf_op jit(solution)/shard_map/all_to_all | solution.py:397
  70.9 0.9 copy-done.4
  71.8 0.9 copy-done.6
  72.8 0.9 copy-done.8
  73.7 0.9 copy-done.11
  74.7 0.9 copy-done.14
  75.6 15.4 %attend.3 = bf16[8,272,128]{2,1,0:T(8,128)(2,1)S(1)} custom-call(bf16[2048,256]{1,0:T(8,128)(2,1)S(1)} %bitcast.22, bf16[512,256]{1,0:T(8,128)(2,1)S(1)} %constant_dynamic-update-slice_fusion.refs_2_.refs_0_, bf16[512,256]{1,0:T(8,128)(2,1)S(1)} %copy-done.14, bf16[512,256]{1,0:T(8,128)(2,1)S(1)} %copy-done.11, ...), custom_call_target="tpu_custom_call" | custom-call | flops 8589934592 | bytes 2097152 | tf_op jit(solution)/shard_map/attend/pallas_call | solution.py:101
  91.0 1.2 all-to-all-done.1.refs_0_
  92.2 23.8 %all_to_all.35.refs_1_ = bf16[8,272,128]{2,1,0:T(8,128)(2,1)S(1)} all-to-all(bf16[8,272,128]{2,1,0:T(8,128)(2,1)S(1)} %attend.3), channel_id=1, replica_groups={{0,4,8,12,16,20,24,28},{32,36,40,44,48,52,56,60},{64,68,72,76,80,84,88,..., dimensions={0} | all-to-all | bytes 1114112 | tf_op jit(solution)/shard_map/all_to_all | solution.py:401
  116.0 1.5 merge.1
  117.6 11.5 %all_to_all.36 = bf16[8,32,256]{2,1,0:T(8,128)(2,1)S(1)} all-to-all(bf16[8,32,256]{2,1,0:T(8,128)(2,1)S(1)} %get-tuple-element.21), channel_id=1, replica_groups={{0,4,8,12,16,20,24,28},{32,36,40,44,48,52,56,60},{64,68,72,76,80,84,88,..., dimensions={0} | all-to-all | bytes 262144 | tf_op jit(solution)/shard_map/all_to_all | solution.py:404
  129.2 21.2 %all_to_all.37.every_ref = bf16[8,304,256]{2,1,0:T(8,128)(2,1)S(1)} all-to-all(bf16[8,304,256]{2,1,0:T(8,128)(2,1)S(1)} %pad_maximum_fusion), channel_id=1, replica_groups={{0,32,64,96,128,160,192,224},{4,36,68,100,132,164,196,228},{8,40,72,104..., dimensions={0} | all-to-all | bytes 2490368 | tf_op jit(solution)/shard_map/all_to_all | solution.py:409
  150.5 6.8 %track_means.1 = (bf16[2048,256]{1,0:T(8,128)(2,1)S(1)}, bf16[4,16,2048]{2,1,0:T(8,128)(2,1)S(1)}, f32[2048,128]{1,0:T(8,128)S(1)}) custom-call(f32[1,2048]{1,0:T(1,128)S(1)} %convert_element_type.26.ids_here_ref.ids_ref, f32[1,2048]{1,0:T(1,128)S(1)} %convert_element_type.26.ids_here_ref.ids_ref, bf16[8,304,256]{2,1,0:T(8,128)(2,1)S(1)} %all_to_all.37.every_ref, ...), custom_call_target="tpu_custom_call" | custom-call | tf_op jit(solution)/shard_map/track_means/pallas_call | solution.py:230
  157.2 8.4 %all_to_all.38.part_ref = bf16[4,16,2048]{2,1,0:T(8,128)(2,1)S(1)} all-to-all(bf16[4,16,2048]{2,1,0:T(8,128)(2,1)S(1)} %get-tuple-element.24), channel_id=1, replica_groups=mesh['seq'=64,'head'=4] {'head'}, dimensions={0} | all-to-all | bytes 524288 | tf_op jit(solution)/shard_map/all_to_all | solution.py:411
  165.6 2.1 %error_messages.1 = bf16[64,16,384]{2,1,0:T(8,128)(2,1)S(1)} custom-call(s32[128]{0:T(128)S(1)} %copy-done.2, bf16[4,16,2048]{2,1,0:T(8,128)(2,1)S(1)} %all_to_all.38.part_ref, bf16[8,304,256]{2,1,0:T(8,128)(2,1)S(1)} %all_to_all.37.every_ref, f32[1,2048]{1,0:T(1,128)S(1)} %reshape_reshape.3.leader_ref, bf16[2048,256]{1,0:T(8,128)(2,1)S(1)} %get-tuple-element.26.mean_ref), custom_call_target="tpu_custom_call" | custom-call | tf_op jit(solution)/shard_map/error_messages/pallas_call | solution.py:299
  167.7 27.8 %all_to_all.39 = bf16[64,16,384]{2,1,0:T(8,128)(2,1)S(1)} all-to-all(bf16[64,16,384]{2,1,0:T(8,128)(2,1)S(1)} %error_messages.1), channel_id=1, replica_groups=mesh['seq'=64,'head'=4] {'seq'}, dimensions={0} | all-to-all | bytes 1572864 | tf_op jit(solution)/shard_map/all_to_all | solution.py:413
  195.5 1.4 finish.1
  (59 shorter events, 4.6 us)
Async XLA Ops:
  2.5 22.2 %collective-permute-start.6 = (bf16[512,256]{1,0:T(8,128)(2,1)S(1)}, bf16[512,256]{1,0:T(8,128)(2,1)S(1)}, u32[]{:S(2)}, u32[]{:S(2)}) collective-permute-start(bf16[512,256]{1,0:T(8,128)(2,1)S(1)} %constant_dynamic-update-slice_fusion.refs_2_.refs_0_), channel_id=1, source_target_pairs={{0,96},{4,100},{8,104},{12,108},{16,112},{20,116},{24,120},{28,124... | collective-permute-start | bytes 786440 | tf_op jit(solution)/shard_map/ppermute | solution.py:363
  4.8 24.4 %collective-permute-start.5 = (bf16[512,256]{1,0:T(8,128)(2,1)S(1)}, bf16[512,256]{1,0:T(8,128)(2,1)S(1)}, u32[]{:S(2)}, u32[]{:S(2)}) collective-permute-start(bf16[512,256]{1,0:T(8,128)(2,1)S(1)} %constant_dynamic-update-slice_fusion.refs_2_.refs_0_), channel_id=1, source_target_pairs={{0,32},{4,36},{8,40},{12,44},{16,48},{20,52},{24,56},{28,60},{32,6... | collective-permute-start | bytes 786440 | tf_op jit(solution)/shard_map/ppermute | solution.py:363
  4.8 25.8 %collective-permute-start.4 = (bf16[512,256]{1,0:T(8,128)(2,1)S(1)}, bf16[512,256]{1,0:T(8,128)(2,1)S(1)}, u32[]{:S(2)}, u32[]{:S(2)}) collective-permute-start(bf16[512,256]{1,0:T(8,128)(2,1)S(1)} %constant_dynamic-update-slice_fusion.refs_2_.refs_0_), channel_id=1, source_target_pairs={{0,128},{4,132},{8,136},{12,140},{16,144},{20,148},{24,152},{28,15... | collective-permute-start | bytes 786440 | tf_op jit(solution)/shard_map/ppermute | solution.py:363
  7.8 22.8 %collective-permute-start.3 = (bf16[512,256]{1,0:T(8,128)(2,1)S(1)}, bf16[512,256]{1,0:T(8,128)(2,1)S(1)}, u32[]{:S(2)}, u32[]{:S(2)}) collective-permute-start(bf16[512,256]{1,0:T(8,128)(2,1)S(1)} %constant_dynamic-update-slice_fusion.refs_2_.refs_0_), channel_id=1, source_target_pairs={{0,64},{4,68},{8,72},{12,76},{16,80},{20,84},{24,88},{28,92},{32,9... | collective-permute-start | bytes 786440 | tf_op jit(solution)/shard_map/ppermute | solution.py:363
  11.1 19.5 %collective-permute-start.2 = (bf16[512,256]{1,0:T(8,128)(2,1)S(1)}, bf16[512,256]{1,0:T(8,128)(2,1)}, u32[]{:S(2)}, u32[]{:S(2)}) collective-permute-start(bf16[512,256]{1,0:T(8,128)(2,1)S(1)} %constant_dynamic-update-slice_fusion.refs_2_.refs_0_), channel_id=1, source_target_pairs={{0,224},{4,228},{8,232},{12,236},{16,240},{20,244},{24,248},{28,25... | collective-permute-start | bytes 786440 | tf_op jit(solution)/shard_map/ppermute | solution.py:363
  13.1 8.6 %copy-start.2 = (s32[128]{0:T(128)S(1)}, s32[128]{0:T(128)}, u32[]{:S(2)}) copy-start(s32[128]{0:T(128)} %track_ref.1) | copy-start | bytes 1540
  13.1 8.8 %copy-start = (bf16[256,1024]{1,0:T(8,128)(2,1)S(1)}, bf16[256,1024]{1,0:T(8,128)(2,1)}, u32[]{:S(2)}) copy-start(bf16[256,1024]{1,0:T(8,128)(2,1)} %weight_ref.1) | copy-start | bytes 1572868
  13.1 9.0 %copy-start.17 = (s32[2]{0:T(128)S(1)}, s32[2]{0:T(128)}, u32[]{:S(2)}) copy-start(s32[2]{0:T(128)} %param.16) | copy-start | bytes 28
  13.1 9.0 %copy-start.16 = (s32[2,128]{1,0:T(2,128)S(1)}, s32[2,128]{1,0:T(2,128)}, u32[]{:S(2)}) copy-start(s32[2,128]{1,0:T(2,128)} %param.17) | copy-start | bytes 3076
  13.1 9.8 %copy-start.15 = (bf16[4,16,1024]{2,1,0:T(8,128)(2,1)S(1)}, bf16[4,16,1024]{2,1,0:T(8,128)(2,1)}, u32[]{:S(2)}) copy-start(bf16[4,16,1024]{2,1,0:T(8,128)(2,1)} %param.14) | copy-start | bytes 393220
  13.1 36.2 %all-to-all-start = ((bf16[8,256,256]{2,1,0:T(8,128)(2,1)}), bf16[8,256,256]{2,1,0:T(8,128)(2,1)S(1)}, u32[]{:S(2)}, u32[]{:S(2)}) async-start(bf16[8,256,256]{2,1,0:T(8,128)(2,1)} %broadcast_in_dim.32), calls=%async_computation | async-start | bytes 2097152 | tf_op jit(solution)/shard_map/all_to_all | solution.py:24
  24.7 12.0 %collective-permute-start.1 = (bf16[512,256]{1,0:T(8,128)(2,1)S(1)}, bf16[512,256]{1,0:T(8,128)(2,1)S(1)}, u32[]{:S(2)}, u32[]{:S(2)}) collective-permute-start(bf16[512,256]{1,0:T(8,128)(2,1)S(1)} %constant_dynamic-update-slice_fusion.refs_2_.refs_0_), channel_id=1, source_target_pairs={{0,160},{4,164},{8,168},{12,172},{16,176},{20,180},{24,184},{28,18... | collective-permute-start | bytes 786440 | tf_op jit(solution)/shard_map/ppermute | solution.py:363
  29.2 38.0 %copy-start.3 = (bf16[512,256]{1,0:T(8,128)(2,1)}, bf16[512,256]{1,0:T(8,128)(2,1)S(1)}, u32[]{:S(2)}) copy-start(bf16[512,256]{1,0:T(8,128)(2,1)S(1)} %collective-permute-done.5.refs_8_.refs_6_) | copy-start | bytes 786436
  29.2 11.1 %collective-permute-start = (bf16[512,256]{1,0:T(8,128)(2,1)S(1)}, bf16[512,256]{1,0:T(8,128)(2,1)S(1)}, u32[]{:S(2)}, u32[]{:S(2)}) collective-permute-start(bf16[512,256]{1,0:T(8,128)(2,1)S(1)} %constant_dynamic-update-slice_fusion.refs_2_.refs_0_), channel_id=1, source_target_pairs={{0,192},{4,196},{8,200},{12,204},{16,208},{20,212},{24,216},{28,22... | collective-permute-start | bytes 786440 | tf_op jit(solution)/shard_map/ppermute | solution.py:363
  30.6 36.7 %copy-start.5 = (bf16[512,256]{1,0:T(8,128)(2,1)}, bf16[512,256]{1,0:T(8,128)(2,1)S(1)}, u32[]{:S(2)}) copy-start(bf16[512,256]{1,0:T(8,128)(2,1)S(1)} %collective-permute-done.4.refs_7_.refs_5_) | copy-start | bytes 786436
  30.6 36.7 %copy-start.7 = (bf16[512,256]{1,0:T(8,128)(2,1)}, bf16[512,256]{1,0:T(8,128)(2,1)S(1)}, u32[]{:S(2)}) copy-start(bf16[512,256]{1,0:T(8,128)(2,1)S(1)} %collective-permute-done.3.refs_6_.refs_4_) | copy-start | bytes 786436
  36.8 0.7 copy-start.9
  40.4 0.7 copy-start.12
  49.3 1.0 copy-start.10
  50.3 0.9 copy-start.13
  67.3 24.9 %all-to-all-start.1 = ((bf16[8,336,128]{2,1,0:T(8,128)(2,1)}), bf16[8,336,128]{2,1,0:T(8,128)(2,1)S(1)}, u32[]{:S(2)}, u32[]{:S(2)}) async-start(bf16[8,336,128]{2,1,0:T(8,128)(2,1)} %attend.2), calls=%async_computation.1 | async-start | bytes 1376256 | tf_op jit(solution)/shard_map/all_to_all | solution.py:397
  70.8 1.0 copy-start.4
  71.8 0.9 copy-start.6
  72.7 0.9 copy-start.8
  73.7 0.9 copy-start.11
  74.6 0.9 copy-start.14
  75.6 40.4 %copy-start.1 = (bf16[256,256]{1,0:T(8,128)(2,1)S(1)}, bf16[256,256]{1,0:T(8,128)(2,1)}, u32[]{:S(2)}) copy-start(bf16[256,256]{1,0:T(8,128)(2,1)} %refs_2_.1) | copy-start | bytes 393220

commit v4 on v3

--- a/solution.py
+++ b/solution.py
@@ -33,13 +33,13 @@
     return pairs
 
 
-def attend_kernel(riders, q_ref, *refs):
-    extra_refs, kv_refs, (o_ref, k_own, v_own) = refs[:riders], refs[riders:-3], refs[-3:]
-    rows = q_ref.shape[0]
+def attend_kernel(q_ref, piece_ref, count_ref, *refs):
+    kv_refs, (o_ref, k_own, v_own) = refs[:-3], refs[-3:]
+    rows = q_ref.shape[0] // o_ref.shape[0]
     lane = lax.broadcasted_iota(jnp.int32, (1, 128), 1)
     first = lane < HEAD_DIM
 
-    @pl.when(pl.program_id(0) == 0)
+    @pl.when(pl.program_id(1) == 0)
     def _():
         zero = jnp.zeros((), jnp.bfloat16)
         one = jnp.ones((), jnp.bfloat16)
@@ -48,89 +48,80 @@
             span = pl.ds(i * n, n)
             k = kv_ref[:n]
             v = kv_ref[n:]
-            k_own[0, span] = jnp.where(first, k, zero)
-            k_own[1, span] = jnp.where(first, zero, k)
+            k_own[0, :, span] = jnp.where(first, k, zero).T
+            k_own[1, :, span] = jnp.where(first, zero, k).T
             v_own[0, span] = jnp.where(first, v, one)
             v_own[1, span] = jnp.where(first, one, v)
 
     scale = LOG2E * HEAD_DIM ** (-0.5)
     q = q_ref[...]
-    tops, sums = [], []
-    for h in range(2):
-        s = lax.dot_general(
-            q, k_own[h], (((1,), (1,)), ((), ())), preferred_element_type=jnp.float32
-        )
-        top = jnp.max(s, axis=1, keepdims=True)
-        p = jnp.exp2((s - top) * scale).astype(jnp.bfloat16)
-        sums.append(jnp.dot(p, v_own[h], preferred_element_type=jnp.float32))
-        tops.append(top * scale)
+    scores = [jnp.dot(q, k_own[h], preferred_element_type=jnp.float32) for h in range(2)]
+    tops = [jnp.max(s, axis=1, keepdims=True) for s in scores]
+    weights = [
+        jnp.exp2((s - top) * scale).astype(jnp.bfloat16) for s, top in zip(scores, tops)
+    ]
+    sums = [
+        jnp.dot(w, v_own[h], preferred_element_type=jnp.float32) for h, w in enumerate(weights)
+    ]
     num = jnp.where(first, sums[0], sums[1])
     den_other = jnp.where(first, sums[1], sums[0])
     den = pltpu.roll(den_other, HEAD_DIM, 1)
-    o_ref[0, :rows] = (num / den).astype(jnp.bfloat16)
-    lse = jnp.where(first, tops[1], tops[0]) + jnp.log2(den_other)
-    turned = lse.T
-    left = jnp.concatenate([turned[HEAD_DIM : HEAD_DIM + 1], turned[0:1]], axis=0)
-    left = jnp.concatenate([left[:, :128], left[:, 128:]], axis=0)
-    hi = left.astype(jnp.bfloat16)
-    rest = left - hi.astype(jnp.float32)
-    mid = rest.astype(jnp.bfloat16)
-    rest = rest - mid.astype(jnp.float32)
-    pad = jnp.zeros_like(left)
-    if riders:
-        piece_ref, count_ref = extra_refs
-        pad = jnp.concatenate([count_ref[...], pad[1:]], axis=0)
-        o_ref[0, rows + STAT :] = piece_ref[0]
-    o_ref[0, rows : rows + STAT] = jnp.concatenate(
-        [hi.astype(jnp.float32), mid.astype(jnp.float32), rest, pad], axis=0
-    ).astype(jnp.bfloat16)
-
-
-def attend(queries, pieces, pair, riders):
-    n = queries.shape[0]
+    context = (num / den).astype(jnp.bfloat16)
+    lse = jnp.where(first, tops[1], tops[0]) * scale + jnp.log2(den_other)
+    pad = jnp.concatenate([count_ref[...], jnp.zeros((3, 128), jnp.float32)], axis=0)
+    for i in range(o_ref.shape[0]):
+        span = slice(i * rows, i * rows + rows)
+        turned = lse[span].T
+        left = jnp.concatenate([turned[HEAD_DIM : HEAD_DIM + 1], turned[0:1]], axis=0)
+        left = jnp.concatenate([left[:, :128], left[:, 128:]], axis=0)
+        hi = left.astype(jnp.bfloat16)
+        rest = left - hi.astype(jnp.float32)
+        mid = rest.astype(jnp.bfloat16)
+        rest = rest - mid.astype(jnp.float32)
+        o_ref[i, :rows] = context[span]
+        o_ref[i, rows : rows + STAT] = jnp.concatenate(
+            [hi.astype(jnp.float32), mid.astype(jnp.float32), rest, pad], axis=0
+        ).astype(jnp.bfloat16)
+        o_ref[i, rows + STAT :] = piece_ref[i]
+
+
+def attend(queries, pieces, carried, counts):
+    n, width = queries.shape
     rows = n // SIDE
     keys_n = sum(x.shape[0] for x in pieces) // 2
-    out_rows = rows + STAT
-    rider_specs = []
-    if riders:
-        rider_specs = [
-            pl.BlockSpec((1, *riders[0].shape[1:]), lambda i: (i, 0, 0)),
-            pl.BlockSpec(riders[1].shape, lambda i: (0, 0)),
+    pairs = width // 128
+    out_rows = rows + STAT + carried.shape[1]
+    return pl.pallas_call(
+        attend_kernel,
+        grid=(pairs, SIDE // 2),
+        in_specs=[
+            pl.BlockSpec((2 * rows, 128), lambda p, i: (i, p)),
+            pl.BlockSpec((2, carried.shape[1], 128), lambda p, i: (i, 0, p)),
+            pl.BlockSpec(counts.shape, lambda p, i: (0, 0)),
         ]
-        out_rows = out_rows + riders[0].shape[1]
-    return pl.pallas_call(
-        functools.partial(attend_kernel, len(riders)),
-        grid=(SIDE,),
-        in_specs=[pl.BlockSpec((rows, 128), lambda i: (i, pair))]
-        + rider_specs
-        + [pl.BlockSpec((x.shape[0], 128), lambda i: (0, pair)) for x in pieces],
-        out_specs=pl.BlockSpec((1, out_rows, 128), lambda i: (i, 0, 0)),
-        out_shape=jax.ShapeDtypeStruct((SIDE, out_rows, 128), jnp.bfloat16),
+        + [pl.BlockSpec((x.shape[0], 128), lambda p, i: (0, p)) for x in pieces],
+        out_specs=pl.BlockSpec((2, out_rows, 128), lambda p, i: (i, 0, p)),
+        out_shape=jax.ShapeDtypeStruct((SIDE, out_rows, width), jnp.bfloat16),
         scratch_shapes=[
+            pltpu.VMEM((2, 128, keys_n), jnp.bfloat16),
             pltpu.VMEM((2, keys_n, 128), jnp.bfloat16),
-            pltpu.VMEM((2, keys_n, 128), jnp.bfloat16),
-        ],
-        compiler_params=pltpu.CompilerParams(vmem_limit_bytes=VMEM_BYTES),
-        cost_estimate=pl.CostEstimate(
-            flops=2 * 2 * 2 * n * keys_n * 256,
-            bytes_accessed=8 * n * 128,
-            transcendentals=2 * n * keys_n,
-        ),
+        ],
+        compiler_params=pltpu.CompilerParams(vmem_limit_bytes=40 * 1024 * 1024),
         name="attend",
-    )(queries, *riders, *pieces)
-
-
-def merge_kernel(*refs):
-    part_refs, (residual_ref, sel_ref, out_ref, rider_ref) = refs[:-4], refs[-4:]
-    rows = residual_ref.shape[0]
+    )(queries, carried, counts, *pieces)
+
+
+def merge_kernel(part_ref, residual_ref, sel_ref, out_ref, rider_ref):
+    rows, width = residual_ref.shape
     lane = lax.broadcasted_iota(jnp.int32, (1, 128), 1)
     first = lane < HEAD_DIM
+    stats = part_ref[:, rows : rows + STAT].astype(jnp.float32)
+    merged = stats[:, 0:4] + stats[:, 4:8] + stats[:, 8:12]
     scaled = []
-    for part_ref in part_refs:
-        stats = part_ref[:, rows : rows + STAT, :].astype(jnp.float32)
-        merged = stats[:, 0:4] + stats[:, 4:8] + stats[:, 8:12]
+    for p in range(width // 128):
+        cols = slice(p * 128, p * 128 + 128)
         for h in range(2):
-            x = jnp.concatenate([merged[:, h], merged[:, 2 + h]], axis=1)
+            x = jnp.concatenate([merged[:, h, cols], merged[:, 2 + h, cols]], axis=1)
             w = jnp.exp2(x - jnp.max(x, axis=0, keepdims=True))
             scaled.append(w / jnp.sum(w, axis=0, keepdims=True))
     weights = jnp.concatenate(scaled, axis=0)
@@ -138,14 +129,14 @@
         [weights, jnp.zeros((128 - weights.shape[0], rows), jnp.float32)], axis=0
     ).T
     streams = []
-    for p, part_ref in enumerate(part_refs):
+    for p in range(width // 128):
         cols = slice(p * 128, p * 128 + 128)
         total = jnp.zeros((rows, 128), jnp.float32)
         for j in range(SIDE):
             a = (2 * p) * SIDE + j
             b = (2 * p + 1) * SIDE + j
             w = jnp.where(first, weights[:, a : a + 1], weights[:, b : b + 1])
-            total = total + w * part_ref[j, :rows].astype(jnp.float32)
+            total = total + w * part_ref[j, :rows, cols].astype(jnp.float32)
         context = total.astype(jnp.bfloat16).astype(jnp.float32)
         streams.append(
             (residual_ref[:, cols].astype(jnp.float32) + context).astype(jnp.bfloat16)
@@ -155,8 +146,8 @@
     for j in range(SIDE):
         out_ref[j] = pooled
 
-    carried = part_refs[0][:, rows + STAT :].astype(jnp.float32)
-    counts = part_refs[0][:, rows : rows + STAT].astype(jnp.float32)[:, 12:13]
+    carried = part_ref[:, rows + STAT :].astype(jnp.float32)
+    counts = stats[:, 12:13, :128]
     back = sel_ref.shape[0]
     per = 128 // back
     count_tiles = []
@@ -170,9 +161,10 @@
     count_row = jnp.concatenate(count_tiles, axis=1)
     tail = jnp.concatenate([count_row, jnp.zeros((15, count_row.shape[1]), jnp.float32)], axis=0)
     for g in range(SIDE):
-        span = slice(g * 8, g * 8 + 8)
+        span = slice(g % 4 * 8, g % 4 * 8 + 8)
+        cols = slice(g // 4 * 128, g // 4 * 128 + 128)
         halves = [
-            jnp.concatenate([carried[half * 4 + q, span] for q in range(4)], axis=0)
+            jnp.concatenate([carried[half * 4 + q, span, cols] for q in range(4)], axis=0)
             for half in range(2)
         ]
         rider_ref[g] = jnp.concatenate(
@@ -180,7 +172,7 @@
         ).astype(jnp.bfloat16)
 
 
-def merge(parts, residual, sel):
+def merge(part, residual, sel):
     back, width = sel.shape[0], residual.shape[1]
     return pl.pallas_call(
         merge_kernel,
@@ -190,7 +182,7 @@
         ],
         compiler_params=pltpu.CompilerParams(vmem_limit_bytes=VMEM_BYTES),
         name="merge",
-    )(*parts, residual, sel)
+    )(part, residual, sel)
 
 
 def column(row):
@@ -215,14 +207,12 @@
     divisor_ref[...] = jnp.broadcast_to(divisor, divisor_ref.shape)
     mean = (sums / divisor).astype(jnp.bfloat16)
     mean_ref[...] = mean
-    part = lax.dot_general(
+    part_ref[...] = lax.dot_general(
         weight_ref[...], mean, (((1,), (1,)), ((), ())), preferred_element_type=jnp.float32
     ).astype(jnp.bfloat16)
-    for h in range(part_ref.shape[0]):
-        part_ref[h] = part
-
-
-def track_means(ids, every, weight, head_count):
+
+
+def track_means(ids, every, weight):
     width = every.shape[2]
     rows = ids.shape[1]
     chunk = weight.shape[0]
@@ -238,12 +228,12 @@
         ],
         out_specs=[
             pl.BlockSpec((step, width), lambda i: (i, 0)),
-            pl.BlockSpec((head_count, chunk, step), lambda i: (0, 0, i)),
+            pl.BlockSpec((chunk, step), lambda i: (0, i)),
             pl.BlockSpec((step, 128), lambda i: (i, 0)),
         ],
         out_shape=[
             jax.ShapeDtypeStruct((rows, width), jnp.bfloat16),
-            jax.ShapeDtypeStruct((head_count, chunk, rows), jnp.bfloat16),
+            jax.ShapeDtypeStruct((chunk, rows), jnp.bfloat16),
             jax.ShapeDtypeStruct((rows, 128), jnp.float32),
         ],
         compiler_params=pltpu.CompilerParams(vmem_limit_bytes=VMEM_BYTES),
@@ -251,10 +241,10 @@
     )(ids, ids, every, weight)
 
 
-def error_kernel(track_ref, part_ref, every_ref, leader_ref, mean_ref, out_ref, target_buf):
-    back = part_ref.shape[2] // out_ref.shape[0]
+def error_kernel(track_ref, part_ref, other_ref, every_ref, leader_ref, mean_ref, out_ref, target_buf):
+    back = part_ref.shape[1] // out_ref.shape[0]
     width = mean_ref.shape[1]
-    step = part_ref.shape[2] // SIDE
+    step = part_ref.shape[1] // SIDE
     for g in range(SIDE):
         carried = every_ref[g, step : step + 32].astype(jnp.float32)
         for z in range(SIDE):
@@ -263,7 +253,7 @@
             ]
     lane = lax.broadcasted_iota(jnp.int32, (8, 128), 1)
     tiles = []
-    for group in range(part_ref.shape[2] // 128):
+    for group in range(part_ref.shape[1] // 128):
         low = jnp.zeros((8, 128), jnp.float32)
         high = jnp.zeros((8, 128), jnp.float32)
         for j in range(8):
@@ -275,9 +265,7 @@
             high = jnp.where(here, pltpu.roll(tile, lax.rem(turn + 64, 128), 1), high)
         tiles.append(jnp.concatenate([low, high], axis=0))
     target = jnp.concatenate(tiles, axis=1)
-    total = part_ref[0].astype(jnp.float32)
-    for h in range(1, part_ref.shape[0]):
-        total = total + part_ref[h].astype(jnp.float32)
+    total = part_ref[...].astype(jnp.float32) + other_ref[...].astype(jnp.float32)
     error = (total - target).astype(jnp.bfloat16).astype(jnp.float32)
     grad = jnp.dot(
         (error * leader_ref[...]).astype(jnp.bfloat16),
@@ -293,17 +281,17 @@
         out_ref[s, :, width:] = rows.astype(jnp.bfloat16)
 
 
-def error_messages(tracks, partial, every, leader, mean, seq_count):
-    chunk = partial.shape[1]
+def error_messages(tracks, partial, other, every, leader, mean, seq_count):
+    chunk = partial.shape[0]
     vmem = pl.BlockSpec(memory_space=pltpu.VMEM)
     return pl.pallas_call(
         error_kernel,
-        in_specs=[pl.BlockSpec(memory_space=pltpu.SMEM), vmem, vmem, vmem, vmem],
+        in_specs=[pl.BlockSpec(memory_space=pltpu.SMEM), vmem, vmem, vmem, vmem, vmem],
         out_shape=jax.ShapeDtypeStruct((seq_count, chunk, mean.shape[1] + 128), jnp.bfloat16),
         scratch_shapes=[pltpu.VMEM((seq_count, 8, 128), jnp.float32)],
         compiler_params=pltpu.CompilerParams(vmem_limit_bytes=VMEM_BYTES),
         name="error_messages",
-    )(tracks, partial, every, leader, mean)
+    )(tracks, partial, other, every, leader, mean)
 
 
 def finish_kernel(index_ref, final_ref, weight_ref, sel_ref, divisor_ref, grad_ref, context_ref):
@@ -351,7 +339,6 @@
     tok_rows, width = queries.shape
     here = tok_rows // BLK
     seq_count = lax.axis_size("seq")
-    head_count = lax.axis_size("head")
     seq_index = lax.axis_index("seq")
     blocks = here * seq_count
     target_d = reg_weight.shape[1]
@@ -378,7 +365,8 @@
     turned = targets.reshape(owned * POOL, target_d).T
     turned = turned.reshape(SIDE, SIDE, 2, chunk // 2, owned * POOL).transpose(1, 0, 2, 3, 4)
     carried = jnp.concatenate([turned[:, :, 0], turned[:, :, 1]], axis=3)
-    carried = carried.reshape(SIDE, SIDE * chunk // 2, 128)
+    carried = carried.reshape(SIDE, 2, SIDE * chunk // 4, 128)
+    carried = jnp.concatenate([carried[:, 0], carried[:, 1]], axis=2)
     same = block_track[:, None] == block_track[None, :]
     earlier = jnp.arange(blocks)[None, :] < jnp.arange(blocks)[:, None]
     leader = jnp.where(jnp.any(same & earlier, axis=1), 0.0, 1.0)
@@ -390,26 +378,23 @@
     )
     chunk_weight = lax.dynamic_slice_in_dim(reg_weight, seq_index * chunk, chunk, axis=1).T
 
-    part = attend(query_all, pieces, 0, (carried, slot_rows))
-    part, query_all, selector, leader, ids, chunk_weight = lax.optimization_barrier(
-        (part, query_all, selector, leader, ids, chunk_weight)
+    part = attend(query_all, pieces, carried, slot_rows)
+    part, selector, leader, ids, chunk_weight = lax.optimization_barrier(
+        (part, selector, leader, ids, chunk_weight)
     )
-    parts = [lax.all_to_all(part, "seq", 0, 0, axis_index_groups=GROUP_Z)]
-    for pair in range(1, width // 128):
-        part = attend(query_all, pieces, pair, ())
-        parts[-1], part = lax.optimization_barrier((parts[-1], part))
-        parts.append(lax.all_to_all(part, "seq", 0, 0, axis_index_groups=GROUP_Z))
-
-    pooled, rider = merge(parts, residual, selector)
+    part = lax.all_to_all(part, "seq", 0, 0, axis_index_groups=GROUP_Z)
+    pooled, rider = merge(part, residual, selector)
     pooled = lax.all_to_all(pooled, "seq", 0, 0, axis_index_groups=GROUP_Z)
     pooled = pooled.reshape(1, blocks * POOL // SIDE, width)
     every = jnp.concatenate(
         [jnp.broadcast_to(pooled, (SIDE, *pooled.shape[1:])), rider], axis=1
     )
     every = lax.all_to_all(every, "seq", 0, 0, axis_index_groups=GROUP_YX)
-    mean, partial, divisor = track_means(ids, every, chunk_weight, head_count)
-    partial = lax.all_to_all(partial, "head", 0, 0)
-    final = error_messages(block_track, partial, every, leader, mean, seq_count)
+    mean, partial, divisor = track_means(ids, every, chunk_weight)
+    core_mate = lax.ppermute(partial, "head", [(0, 1), (1, 0), (2, 3), (3, 2)])
+    partial = (partial.astype(jnp.float32) + core_mate.astype(jnp.float32)).astype(jnp.bfloat16)
+    other = lax.ppermute(partial, "head", [(0, 2), (2, 0), (1, 3), (3, 1)])
+    final = error_messages(block_track, partial, other, every, leader, mean, seq_count)
     final = lax.all_to_all(final, "seq", 0, 0).reshape(target_d, width + 128)
     return finish(seq_index, final, reg_weight, selector, divisor)
 

time: 199 us -> 194 us (0.975)
  Pallas kernels: 43.2 us -> 35.2 us
  blocking collectives: 92.7 us -> 97.4 us
  starting transfers between devices: 26.5 us -> 23.4 us
  other arithmetic: 0.72 us -> 3.4 us
  waiting for transfers between devices: 18.5 us -> 16.5 us
    ppermute x7, waiting for transfers between devices: 9.03 us -> 0.02 us  [local(): lax.ppermute(own_kv, 'seq', shift(seq_count, d))]
    pallas_call x2 -> x1, Pallas kernels: 31.4 us -> 23.4 us  [attend(): pl.pallas_call(attend_kernel, grid=(pairs, SIDE // 2), in_specs=[pl.Block...]
    unnamed x39 -> x25, local copies, waits for them, and re-layouts: 9.06 us -> 3.84 us
    ppermute x0 -> x2, waiting for transfers between devices: none -> 4.83 us  [the longest x1 3.59 us: local(): other = lax.ppermute(partial, 'head', [(0, 2), (2, 0), (1, 3), (3, 1)])]
    all_to_all x2 -> x1, blocking collectives: 32.2 us -> 35.9 us  [local(): part = lax.all_to_all(part, 'seq', 0, 0, axis_index_groups=GROUP_Z)]
    all_to_all x1 -> x0, starting transfers between devices: 3.55 us -> none  [local(): parts = [lax.all_to_all(part, 'seq', 0, 0, axis_index_groups=GROUP_Z)]]
    all_to_all x1, waiting for transfers between devices: 8.27 us -> 11.7 us  [spread(): return lax.all_to_all(wide, 'seq', 0, 0, axis_index_groups=groups)]
  transfers between devices with their start and end apart: 9 -> 10, of which waited for: 4 -> 3; matrix products, arithmetic and copies ran while one was open for 3% -> 8% of each run, Pallas kernels for 8% -> 0%
where the time goes in v4:
time: 194 us; the launch traced here: 191 us
  blocking collectives  97.4 us (50%)
  Pallas kernels  35.2 us (18%)
  starting transfers between devices  23.4 us (12%)
  waiting for transfers between devices  16.5 us (9%)
  local copies, waits for them, and re-layouts  14.6 us (8%)
  other arithmetic  3.4 us (2%)
    all_to_all x1, blocking collectives, local(): part = lax.all_to_all(part, 'seq', 0, 0, axis_index_groups=GROUP_Z)  35.9 us
    all_to_all x1, blocking collectives, local(): final = lax.all_to_all(final, 'seq', 0, 0).reshape(target_d, width + 128)  27.7 us
    pallas_call x1, Pallas kernels, attend(): pl.pallas_call(attend_kernel, grid=(pairs, SIDE // 2), in_specs=[pl.Block...  23.4 us
    all_to_all x1, blocking collectives, local(): every = lax.all_to_all(every, 'seq', 0, 0, axis_index_groups=GROUP_YX)  21.9 us
    ppermute x7, starting transfers between devices, local(): lax.ppermute(own_kv, 'seq', shift(seq_count, d))  13.8 us
    all_to_all x1, blocking collectives, local(): pooled = lax.all_to_all(pooled, 'seq', 0, 0, axis_index_groups=GROUP_Z)  11.8 us
    all_to_all x1, waiting for transfers between devices, spread(): return lax.all_to_all(wide, 'seq', 0, 0, axis_index_groups=groups)  11.7 us
    all_to_all x1, starting transfers between devices, spread(): return lax.all_to_all(wide, 'seq', 0, 0, axis_index_groups=groups)  8.61 us
  transfers between devices with their start and end apart: 10, of which 3 were waited for; matrix products, arithmetic and copies ran while one was open for 8% of the time, Pallas kernels for 0%

profile of v4, /device:TPU:2, one launch (start us, length us, event | category | flops | bytes accessed | tf_op | source)
XLA Modules:
  0.0 191.2 jit_solution(14160532911100215725)
XLA Ops:
  0.6 0.9 constant_dynamic-update-slice_fusion.1
  1.5 0.9 constant_dynamic-update-slice_fusion.refs_0_
  2.5 4.8 %collective-permute-start = (bf16[512,256]{1,0:T(8,128)(2,1)S(1)}, bf16[512,256]{1,0:T(8,128)(2,1)S(1)}, u32[]{:S(2)}, u32[]{:S(2)}) collective-permute-start(bf16[512,256]{1,0:T(8,128)(2,1)S(1)} %constant_dynamic-update-slice_fusion.refs_0_), channel_id=1, source_target_pairs={{0,192},{4,196},{8,200},{12,204},{16,208},{20,212},{24,216},{28,22... | collective-permute-start | bytes 786440 | tf_op jit(solution)/shard_map/ppermute | solution.py:350
  7.3 1.4 collective-permute-start.1
  8.7 3.0 %collective-permute-start.2 = (bf16[512,256]{1,0:T(8,128)(2,1)S(1)}, bf16[512,256]{1,0:T(8,128)(2,1)S(1)}, u32[]{:S(2)}, u32[]{:S(2)}) collective-permute-start(bf16[512,256]{1,0:T(8,128)(2,1)S(1)} %constant_dynamic-update-slice_fusion.refs_0_), channel_id=1, source_target_pairs={{0,224},{4,228},{8,232},{12,236},{16,240},{20,244},{24,248},{28,25... | collective-permute-start | bytes 786440 | tf_op jit(solution)/shard_map/ppermute | solution.py:350
  11.7 1.4 collective-permute-start.3
  13.8 2.0 %broadcast_in_dim.32 = bf16[8,256,256]{2,1,0:T(8,128)(2,1)} broadcast(bf16[256,256]{1,0:T(8,128)(2,1)} %param.9), dimensions={1,2} | broadcast | bytes 1179648 | tf_op jit(solution)/shard_map/broadcast_in_dim | solution.py:23
  15.8 8.6 %all-to-all-start = ((bf16[8,256,256]{2,1,0:T(8,128)(2,1)}), bf16[8,256,256]{2,1,0:T(8,128)(2,1)S(1)}, u32[]{:S(2)}, u32[]{:S(2)}) async-start(bf16[8,256,256]{2,1,0:T(8,128)(2,1)} %broadcast_in_dim.32), calls=%async_computation | async-start | bytes 2097152 | tf_op jit(solution)/shard_map/all_to_all | solution.py:24
  25.2 0.7 fusion.5
  25.9 0.7 add_convert_fusion.1
  26.6 0.7 constant_dynamic-slice_fusion
  27.6 2.5 %collective-permute-start.5 = (bf16[512,256]{1,0:T(8,128)(2,1)S(1)}, bf16[512,256]{1,0:T(8,128)(2,1)S(1)}, u32[]{:S(2)}, u32[]{:S(2)}) collective-permute-start(bf16[512,256]{1,0:T(8,128)(2,1)S(1)} %constant_dynamic-update-slice_fusion.refs_0_), channel_id=1, source_target_pairs={{0,32},{4,36},{8,40},{12,44},{16,48},{20,52},{24,56},{28,60},{32,6... | collective-permute-start | bytes 786440 | tf_op jit(solution)/shard_map/ppermute | solution.py:350
  31.5 1.5 copy.33
  33.0 0.7 copy.36
  33.7 1.3 broadcast_in_dim.62
  35.1 1.5 reshape_reshape.3.leader_ref
  36.6 1.5 convert_element_type.35.ids_here_ref.ids_ref
  38.1 1.1 pad.4.count_ref
  39.3 1.0 fusion.1
  40.3 11.7 %all-to-all-done = bf16[8,256,256]{2,1,0:T(8,128)(2,1)S(1)} async-done(((bf16[8,256,256]{2,1,0:T(8,128)(2,1)}), bf16[8,256,256]{2,1,0:T(8,128)(2,1)S(1)}, u32[]{:S(2)}, u32[]{:S(2)}) %all-to-all-start) | async-done | bytes 1048608 | tf_op jit(solution)/shard_map/all_to_all | solution.py:24
  52.6 23.4 %attend.1 = bf16[8,304,256]{2,1,0:T(8,128)(2,1)S(1)} custom-call(bf16[2048,256]{1,0:T(8,128)(2,1)S(1)} %bitcast.26, bf16[8,32,256]{2,1,0:T(8,128)(2,1)S(1)} %pad_maximum_fusion.1.piece_ref, f32[1,128]{1,0:T(1,128)S(1)} %copy-done.5, bf16[512,256]{1,0:T(8,128)(2,1)S(1)} %constant_dynamic-update-slice_fusion.refs_0_, ...), custom_call_target="tpu_custom_call" | custom-call | tf_op jit(solution)/shard_map/attend/pallas_call | solution.py:94
  76.1 35.9 %all_to_all.25.part_ref = bf16[8,304,256]{2,1,0:T(8,128)(2,1)S(1)} all-to-all(bf16[8,304,256]{2,1,0:T(8,128)(2,1)S(1)} %attend.1), channel_id=1, replica_groups={{0,4,8,12,16,20,24,28},{32,36,40,44,48,52,56,60},{64,68,72,76,80,84,88,..., dimensions={0} | all-to-all | bytes 2490368 | tf_op jit(solution)/shard_map/all_to_all | solution.py:385
  112.0 1.5 merge.1
  113.5 11.8 %all_to_all.26 = bf16[8,32,256]{2,1,0:T(8,128)(2,1)S(1)} all-to-all(bf16[8,32,256]{2,1,0:T(8,128)(2,1)S(1)} %get-tuple-element.15), channel_id=1, replica_groups={{0,4,8,12,16,20,24,28},{32,36,40,44,48,52,56,60},{64,68,72,76,80,84,88,..., dimensions={0} | all-to-all | bytes 262144 | tf_op jit(solution)/shard_map/all_to_all | solution.py:387
  125.5 21.9 %all_to_all.27.every_ref = bf16[8,304,256]{2,1,0:T(8,128)(2,1)S(1)} all-to-all(bf16[8,304,256]{2,1,0:T(8,128)(2,1)S(1)} %pad_maximum_fusion), channel_id=1, replica_groups={{0,32,64,96,128,160,192,224},{4,36,68,100,132,164,196,228},{8,40,72,104..., dimensions={0} | all-to-all | bytes 2490368 | tf_op jit(solution)/shard_map/all_to_all | solution.py:392
  147.5 6.8 %track_means.1 = (bf16[2048,256]{1,0:T(8,128)(2,1)S(1)}, bf16[16,2048]{1,0:T(8,128)(2,1)S(1)}, f32[2048,128]{1,0:T(8,128)S(1)}) custom-call(f32[1,2048]{1,0:T(1,128)S(1)} %copy-done.2, f32[1,2048]{1,0:T(1,128)S(1)} %copy-done.2, bf16[8,304,256]{2,1,0:T(8,128)(2,1)S(1)} %all_to_all.27.every_ref, bf16[16,256]{1,0:T(8,128)(2,1)S(1)} %bitcast.30), custom_call_target="tpu_custom_call" | custom-call | tf_op jit(solution)/shard_map/track_means/pallas_call | solution.py:220
  154.4 1.2 collective-permute-done.7
  155.7 0.8 collective-permute-start.8
  156.5 3.6 %collective-permute-done.8.other_ref = bf16[16,2048]{1,0:T(8,128)(2,1)S(1)} collective-permute-done((bf16[16,2048]{1,0:T(8,128)(2,1)S(1)}, bf16[16,2048]{1,0:T(8,128)(2,1)S(1)}, u32[]{:S(2)}, u32[]{:S(2)}) %collective-permute-start.8) | collective-permute-done | bytes 65568 | tf_op jit(solution)/shard_map/ppermute | solution.py:396
  160.1 2.1 %error_messages.1 = bf16[64,16,384]{2,1,0:T(8,128)(2,1)S(1)} custom-call(s32[128]{0:T(128)S(1)} %copy-done.7, bf16[16,2048]{1,0:T(8,128)(2,1)S(1)} %add_convert_fusion.part_ref, bf16[16,2048]{1,0:T(8,128)(2,1)S(1)} %collective-permute-done.8.other_ref, bf16[8,304,256]{2,1,0:T(8,128)(2,1)S(1)} %all_to_all.27.every_ref, f32[1,2048]{1,0:T(1,128)S(1)} %copy-done.3, ...), custom_call_target="tpu_custom_call" | custom-call | tf_op jit(solution)/shard_map/error_messages/pallas_call | solution.py:287
  162.1 27.7 %all_to_all.28 = bf16[64,16,384]{2,1,0:T(8,128)(2,1)S(1)} all-to-all(bf16[64,16,384]{2,1,0:T(8,128)(2,1)S(1)} %error_messages.1), channel_id=1, replica_groups=mesh['seq'=64,'head'=4] {'seq'}, dimensions={0} | all-to-all | bytes 1572864 | tf_op jit(solution)/shard_map/all_to_all | solution.py:398
  189.8 1.4 finish.1
  (48 shorter events, 4.2 us)
Async XLA Ops:
  2.5 25.1 %collective-permute-start = (bf16[512,256]{1,0:T(8,128)(2,1)S(1)}, bf16[512,256]{1,0:T(8,128)(2,1)S(1)}, u32[]{:S(2)}, u32[]{:S(2)}) collective-permute-start(bf16[512,256]{1,0:T(8,128)(2,1)S(1)} %constant_dynamic-update-slice_fusion.refs_0_), channel_id=1, source_target_pairs={{0,192},{4,196},{8,200},{12,204},{16,208},{20,212},{24,216},{28,22... | collective-permute-start | bytes 786440 | tf_op jit(solution)/shard_map/ppermute | solution.py:350
  7.3 22.8 %collective-permute-start.1 = (bf16[512,256]{1,0:T(8,128)(2,1)S(1)}, bf16[512,256]{1,0:T(8,128)(2,1)S(1)}, u32[]{:S(2)}, u32[]{:S(2)}) collective-permute-start(bf16[512,256]{1,0:T(8,128)(2,1)S(1)} %constant_dynamic-update-slice_fusion.refs_0_), channel_id=1, source_target_pairs={{0,160},{4,164},{8,168},{12,172},{16,176},{20,180},{24,184},{28,18... | collective-permute-start | bytes 786440 | tf_op jit(solution)/shard_map/ppermute | solution.py:350
  8.7 31.6 %collective-permute-start.2 = (bf16[512,256]{1,0:T(8,128)(2,1)S(1)}, bf16[512,256]{1,0:T(8,128)(2,1)S(1)}, u32[]{:S(2)}, u32[]{:S(2)}) collective-permute-start(bf16[512,256]{1,0:T(8,128)(2,1)S(1)} %constant_dynamic-update-slice_fusion.refs_0_), channel_id=1, source_target_pairs={{0,224},{4,228},{8,232},{12,236},{16,240},{20,244},{24,248},{28,25... | collective-permute-start | bytes 786440 | tf_op jit(solution)/shard_map/ppermute | solution.py:350
  11.7 28.6 %collective-permute-start.3 = (bf16[512,256]{1,0:T(8,128)(2,1)S(1)}, bf16[512,256]{1,0:T(8,128)(2,1)S(1)}, u32[]{:S(2)}, u32[]{:S(2)}) collective-permute-start(bf16[512,256]{1,0:T(8,128)(2,1)S(1)} %constant_dynamic-update-slice_fusion.refs_0_), channel_id=1, source_target_pairs={{0,64},{4,68},{8,72},{12,76},{16,80},{20,84},{24,88},{28,92},{32,9... | collective-permute-start | bytes 786440 | tf_op jit(solution)/shard_map/ppermute | solution.py:350
  13.1 27.2 %collective-permute-start.4 = (bf16[512,256]{1,0:T(8,128)(2,1)S(1)}, bf16[512,256]{1,0:T(8,128)(2,1)S(1)}, u32[]{:S(2)}, u32[]{:S(2)}) collective-permute-start(bf16[512,256]{1,0:T(8,128)(2,1)S(1)} %constant_dynamic-update-slice_fusion.refs_0_), channel_id=1, source_target_pairs={{0,128},{4,132},{8,136},{12,140},{16,144},{20,148},{24,152},{28,15... | collective-permute-start | bytes 786440 | tf_op jit(solution)/shard_map/ppermute | solution.py:350
  15.7 8.6 %copy-start.6 = (s32[128]{0:T(128)S(1)}, s32[128]{0:T(128)}, u32[]{:S(2)}) copy-start(s32[128]{0:T(128)} %track_ref.1) | copy-start | bytes 1540
  15.7 8.8 %copy-start.10 = (s32[2]{0:T(128)S(1)}, s32[2]{0:T(128)}, u32[]{:S(2)}) copy-start(s32[2]{0:T(128)} %param.16) | copy-start | bytes 28
  15.7 9.5 %copy-start.9 = (s32[2,128]{1,0:T(2,128)S(1)}, s32[2,128]{1,0:T(2,128)}, u32[]{:S(2)}) copy-start(s32[2,128]{1,0:T(2,128)} %param.17) | copy-start | bytes 3076
  15.8 10.9 %copy-start = (bf16[256,1024]{1,0:T(8,128)(2,1)S(1)}, bf16[256,1024]{1,0:T(8,128)(2,1)}, u32[]{:S(2)}) copy-start(bf16[256,1024]{1,0:T(8,128)(2,1)} %weight_ref.1) | copy-start | bytes 1572868
  15.8 11.6 %copy-start.8 = (bf16[4,16,1024]{2,1,0:T(8,128)(2,1)S(1)}, bf16[4,16,1024]{2,1,0:T(8,128)(2,1)}, u32[]{:S(2)}) copy-start(bf16[4,16,1024]{2,1,0:T(8,128)(2,1)} %param.14) | copy-start | bytes 393220
  15.8 36.2 %all-to-all-start = ((bf16[8,256,256]{2,1,0:T(8,128)(2,1)}), bf16[8,256,256]{2,1,0:T(8,128)(2,1)S(1)}, u32[]{:S(2)}, u32[]{:S(2)}) async-start(bf16[8,256,256]{2,1,0:T(8,128)(2,1)} %broadcast_in_dim.32), calls=%async_computation | async-start | bytes 2097152 | tf_op jit(solution)/shard_map/all_to_all | solution.py:24
  27.6 12.7 %collective-permute-start.5 = (bf16[512,256]{1,0:T(8,128)(2,1)S(1)}, bf16[512,256]{1,0:T(8,128)(2,1)S(1)}, u32[]{:S(2)}, u32[]{:S(2)}) collective-permute-start(bf16[512,256]{1,0:T(8,128)(2,1)S(1)} %constant_dynamic-update-slice_fusion.refs_0_), channel_id=1, source_target_pairs={{0,32},{4,36},{8,40},{12,44},{16,48},{20,52},{24,56},{28,60},{32,6... | collective-permute-start | bytes 786440 | tf_op jit(solution)/shard_map/ppermute | solution.py:350
  30.1 10.2 %collective-permute-start.6 = (bf16[512,256]{1,0:T(8,128)(2,1)S(1)}, bf16[512,256]{1,0:T(8,128)(2,1)}, u32[]{:S(2)}, u32[]{:S(2)}) collective-permute-start(bf16[512,256]{1,0:T(8,128)(2,1)S(1)} %constant_dynamic-update-slice_fusion.refs_0_), channel_id=1, source_target_pairs={{0,96},{4,100},{8,104},{12,108},{16,112},{20,116},{24,120},{28,124... | collective-permute-start | bytes 786440 | tf_op jit(solution)/shard_map/ppermute | solution.py:350
  52.0 0.7 copy-start.5
  76.1 36.0 %copy-start.1 = (bf16[256,256]{1,0:T(8,128)(2,1)S(1)}, bf16[256,256]{1,0:T(8,128)(2,1)}, u32[]{:S(2)}) copy-start(bf16[256,256]{1,0:T(8,128)(2,1)} %residual_ref.1) | copy-start | bytes 393220
  125.5 22.0 %copy-start.2 = (f32[1,2048]{1,0:T(1,128)S(1)}, f32[1,2048]{1,0:T(1,128)}, u32[]{:S(2)}) copy-start(f32[1,2048]{1,0:T(1,128)} %convert_element_type.35.ids_here_ref.ids_ref) | copy-start | bytes 24580
  125.5 22.0 %copy-start.4 = (bf16[256,16]{0,1:T(8,128)(2,1)S(1)}, bf16[256,16]{0,1:T(8,128)(2,1)}, u32[]{:S(2)}) copy-start(bf16[256,16]{0,1:T(8,128)(2,1)} %copy.33) | copy-start | bytes 24580
  147.5 12.6 %copy-start.3 = (f32[1,2048]{1,0:T(1,128)S(1)}, f32[1,2048]{1,0:T(1,128)}, u32[]{:S(2)}) copy-start(f32[1,2048]{1,0:T(1,128)} %reshape_reshape.3.leader_ref) | copy-start | bytes 24580
  147.5 12.6 %copy-start.7 = (s32[128]{0:T(128)S(1)}, s32[128]{0:T(128)}, u32[]{:S(2)}) copy-start(s32[128]{0:T(128)} %track_ref.1) | copy-start | bytes 1540
  154.2 1.4 collective-permute-start.7
  155.7 4.4 %collective-permute-start.8 = (bf16[16,2048]{1,0:T(8,128)(2,1)S(1)}, bf16[16,2048]{1,0:T(8,128)(2,1)S(1)}, u32[]{:S(2)}, u32[]{:S(2)}) collective-permute-start(bf16[16,2048]{1,0:T(8,128)(2,1)S(1)} %add_convert_fusion.part_ref), channel_id=1, source_target_pairs={{0,2},{2,0},{1,3},{3,1},{4,6},{6,4},{5,7},{7,5},{8,10},{10,8},{9,1... | collective-permute-start | bytes 196616 | tf_op jit(solution)/shard_map/ppermute | solution.py:396

commit v5 on v4

--- a/solution.py
+++ b/solution.py
@@ -24,13 +24,23 @@
     return lax.all_to_all(wide, "seq", 0, 0, axis_index_groups=groups)
 
 
-def shift(seq_count, dg):
-    dy, dx = dg // 4, dg % 4
-    pairs = []
-    for g in range(seq_count // SIDE):
-        to = (g // 4 + dy) % 2 * 4 + (g % 4 + dx) % 4
-        pairs += [(g * SIDE + i, to * SIDE + i) for i in range(SIDE)]
-    return pairs
+def ring(seq_count, step):
+    return [
+        (g * SIDE + i, g * SIDE + (i + step) % SIDE)
+        for g in range(seq_count // SIDE)
+        for i in range(SIDE)
+    ]
+
+
+def gather_ring(x, seq_count):
+    pieces, up, down = [x], x, x
+    for i in range(SIDE // 2):
+        up = lax.ppermute(up, "seq", ring(seq_count, 1))
+        pieces.append(up)
+        if i + 1 < SIDE // 2:
+            down = lax.ppermute(down, "seq", ring(seq_count, -1))
+            pieces.append(down)
+    return pieces
 
 
 def attend_kernel(q_ref, piece_ref, count_ref, *refs):
@@ -111,7 +121,7 @@
     )(queries, carried, counts, *pieces)
 
 
-def merge_kernel(part_ref, residual_ref, sel_ref, out_ref, rider_ref):
+def merge_kernel(part_ref, residual_ref, sel_ref, out_ref):
     rows, width = residual_ref.shape
     lane = lax.broadcasted_iota(jnp.int32, (1, 128), 1)
     first = lane < HEAD_DIM
@@ -143,12 +153,12 @@
         )
     stream = jnp.concatenate(streams, axis=1)
     pooled = jnp.dot(sel_ref[...], stream, preferred_element_type=jnp.float32).astype(jnp.bfloat16)
+    back = sel_ref.shape[0]
     for j in range(SIDE):
-        out_ref[j] = pooled
+        out_ref[j, :back] = pooled
 
     carried = part_ref[:, rows + STAT :].astype(jnp.float32)
     counts = stats[:, 12:13, :128]
-    back = sel_ref.shape[0]
     per = 128 // back
     count_tiles = []
     for half in range(SIDE // per):
@@ -167,7 +177,7 @@
             jnp.concatenate([carried[half * 4 + q, span, cols] for q in range(4)], axis=0)
             for half in range(2)
         ]
-        rider_ref[g] = jnp.concatenate(
+        out_ref[g, back:] = jnp.concatenate(
             [jnp.concatenate(halves, axis=1), tail], axis=0
         ).astype(jnp.bfloat16)
 
@@ -176,10 +186,7 @@
     back, width = sel.shape[0], residual.shape[1]
     return pl.pallas_call(
         merge_kernel,
-        out_shape=[
-            jax.ShapeDtypeStruct((SIDE, back, width), jnp.bfloat16),
-            jax.ShapeDtypeStruct((SIDE, 48, 256), jnp.bfloat16),
-        ],
+        out_shape=jax.ShapeDtypeStruct((SIDE, back + 48, width), jnp.bfloat16),
         compiler_params=pltpu.CompilerParams(vmem_limit_bytes=VMEM_BYTES),
         name="merge",
     )(part, residual, sel)
@@ -189,8 +196,27 @@
     return jnp.broadcast_to(row, (128, row.shape[1])).T[:, :1]
 
 
-def track_kernel(ids_here_ref, ids_ref, every_ref, weight_ref, mean_ref, part_ref, divisor_ref):
+def track_kernel(
+    ids_here_ref, ids_ref, every_ref, both_ref, weight_ref, mean_ref, part_ref, divisor_ref, count_buf
+):
     step = mean_ref.shape[0]
+
+    @pl.when(pl.program_id(0) == 0)
+    def _():
+        lane = lax.broadcasted_iota(jnp.int32, (1, 128), 1)
+        rows = [
+            both_ref[z, both_ref.shape[1] - 16 :].astype(jnp.float32)[:1] for z in range(SIDE)
+        ]
+        for g in range(SIDE):
+            for half in range(2):
+                tile = jnp.zeros((1, 128), jnp.float32)
+                for q in range(4):
+                    row = rows[half * 4 + q][:, g // 4 * 128 : g // 4 * 128 + 128]
+                    turn = (q - g % 4) % 4 * 32
+                    row = pltpu.roll(row, turn, 1) if turn else row
+                    tile = jnp.where(lane // 32 == q, row, tile)
+                count_buf[g : g + 1, half * 128 : half * 128 + 128] = tile
+
     here = column(ids_here_ref[...])
     sums = jnp.zeros(mean_ref.shape, jnp.float32)
     counts = jnp.zeros((step, step), jnp.float32)
@@ -198,11 +224,10 @@
         match = here == ids_ref[:, g * step : g * step + step]
         sums = sums + jnp.dot(
             jnp.where(match, 1.0, 0.0).astype(jnp.bfloat16),
-            every_ref[g, :step],
+            every_ref[g],
             preferred_element_type=jnp.float32,
         )
-        count_row = every_ref[g, step + 32 :].astype(jnp.float32)[:1]
-        counts = counts + jnp.where(match, count_row, 0.0)
+        counts = counts + jnp.where(match, count_buf[g : g + 1], 0.0)
     divisor = jnp.maximum(jnp.sum(counts, axis=1, keepdims=True), 1.0)
     divisor_ref[...] = jnp.broadcast_to(divisor, divisor_ref.shape)
     mean = (sums / divisor).astype(jnp.bfloat16)
@@ -212,7 +237,7 @@
     ).astype(jnp.bfloat16)
 
 
-def track_means(ids, every, weight):
+def track_means(ids, every, both, weight):
     width = every.shape[2]
     rows = ids.shape[1]
     chunk = weight.shape[0]
@@ -224,6 +249,7 @@
             pl.BlockSpec((1, step), lambda i: (0, i)),
             pl.BlockSpec((1, rows), lambda i: (0, 0)),
             pl.BlockSpec(every.shape, lambda i: (0, 0, 0)),
+            pl.BlockSpec(both.shape, lambda i: (0, 0, 0)),
             pl.BlockSpec((chunk, width), lambda i: (0, 0)),
         ],
         out_specs=[
@@ -236,20 +262,20 @@
             jax.ShapeDtypeStruct((chunk, rows), jnp.bfloat16),
             jax.ShapeDtypeStruct((rows, 128), jnp.float32),
         ],
+        scratch_shapes=[pltpu.VMEM((SIDE, step), jnp.float32)],
         compiler_params=pltpu.CompilerParams(vmem_limit_bytes=VMEM_BYTES),
         name="track_means",
-    )(ids, ids, every, weight)
-
-
-def error_kernel(track_ref, part_ref, other_ref, every_ref, leader_ref, mean_ref, out_ref, target_buf):
+    )(ids, ids, every, both, weight)
+
+
+def error_kernel(track_ref, part_ref, other_ref, both_ref, leader_ref, mean_ref, out_ref, target_buf):
     back = part_ref.shape[1] // out_ref.shape[0]
     width = mean_ref.shape[1]
-    step = part_ref.shape[1] // SIDE
-    for g in range(SIDE):
-        carried = every_ref[g, step : step + 32].astype(jnp.float32)
-        for z in range(SIDE):
+    for z in range(SIDE):
+        carried = both_ref[z, back : back + 32].astype(jnp.float32)
+        for g in range(SIDE):
             target_buf[g * SIDE + z] = carried[
-                z % 4 * 8 : z % 4 * 8 + 8, z // 4 * 128 : z // 4 * 128 + 128
+                g % 4 * 8 : g % 4 * 8 + 8, g // 4 * 128 : g // 4 * 128 + 128
             ]
     lane = lax.broadcasted_iota(jnp.int32, (8, 128), 1)
     tiles = []
@@ -281,7 +307,7 @@
         out_ref[s, :, width:] = rows.astype(jnp.bfloat16)
 
 
-def error_messages(tracks, partial, other, every, leader, mean, seq_count):
+def error_messages(tracks, partial, other, both, leader, mean, seq_count):
     chunk = partial.shape[0]
     vmem = pl.BlockSpec(memory_space=pltpu.VMEM)
     return pl.pallas_call(
@@ -291,7 +317,7 @@
         scratch_shapes=[pltpu.VMEM((seq_count, 8, 128), jnp.float32)],
         compiler_params=pltpu.CompilerParams(vmem_limit_bytes=VMEM_BYTES),
         name="error_messages",
-    )(tracks, partial, other, every, leader, mean)
+    )(tracks, partial, other, both, leader, mean)
 
 
 def finish_kernel(index_ref, final_ref, weight_ref, sel_ref, divisor_ref, grad_ref, context_ref):
@@ -346,10 +372,8 @@
     owned = targets.shape[0]
 
     own_kv = jnp.concatenate([keys, values], axis=0)
-    pieces = [own_kv] + [
-        lax.ppermute(own_kv, "seq", shift(seq_count, d)) for d in (6, 5, 7, 2, 4, 1, 3)
-    ]
-    query_all = spread(queries, GROUP_Z).reshape(SIDE * tok_rows, width)
+    pieces = gather_ring(own_kv, seq_count)
+    query_all = spread(queries, GROUP_YX).reshape(SIDE * tok_rows, width)
 
     valid = jnp.arange(BLK, dtype=jnp.int32)[None, :] < row_count[:, None]
     match = pool_slot[:, None, :] == jnp.arange(POOL, dtype=jnp.int32)[None, :, None]
@@ -363,7 +387,7 @@
     slot_rows = jnp.sum(jnp.where(sel, 1.0, 0.0), axis=2).reshape(1, here * POOL)
     slot_rows = jnp.pad(slot_rows, ((0, 0), (0, 128 - here * POOL)))
     turned = targets.reshape(owned * POOL, target_d).T
-    turned = turned.reshape(SIDE, SIDE, 2, chunk // 2, owned * POOL).transpose(1, 0, 2, 3, 4)
+    turned = turned.reshape(SIDE, SIDE, 2, chunk // 2, owned * POOL)
     carried = jnp.concatenate([turned[:, :, 0], turned[:, :, 1]], axis=3)
     carried = carried.reshape(SIDE, 2, SIDE * chunk // 4, 128)
     carried = jnp.concatenate([carried[:, 0], carried[:, 1]], axis=2)
@@ -382,19 +406,16 @@
     part, selector, leader, ids, chunk_weight = lax.optimization_barrier(
         (part, selector, leader, ids, chunk_weight)
     )
-    part = lax.all_to_all(part, "seq", 0, 0, axis_index_groups=GROUP_Z)
-    pooled, rider = merge(part, residual, selector)
-    pooled = lax.all_to_all(pooled, "seq", 0, 0, axis_index_groups=GROUP_Z)
-    pooled = pooled.reshape(1, blocks * POOL // SIDE, width)
-    every = jnp.concatenate(
-        [jnp.broadcast_to(pooled, (SIDE, *pooled.shape[1:])), rider], axis=1
-    )
-    every = lax.all_to_all(every, "seq", 0, 0, axis_index_groups=GROUP_YX)
-    mean, partial, divisor = track_means(ids, every, chunk_weight)
+    part = lax.all_to_all(part, "seq", 0, 0, axis_index_groups=GROUP_YX)
+    both = merge(part, residual, selector)
+    both = lax.all_to_all(both, "seq", 0, 0, axis_index_groups=GROUP_Z)
+    pooled = both[:, : here * POOL].reshape(blocks * POOL // SIDE, width)
+    every = spread(pooled, GROUP_YX)
+    mean, partial, divisor = track_means(ids, every, both, chunk_weight)
     core_mate = lax.ppermute(partial, "head", [(0, 1), (1, 0), (2, 3), (3, 2)])
     partial = (partial.astype(jnp.float32) + core_mate.astype(jnp.float32)).astype(jnp.bfloat16)
     other = lax.ppermute(partial, "head", [(0, 2), (2, 0), (1, 3), (3, 1)])
-    final = error_messages(block_track, partial, other, every, leader, mean, seq_count)
+    final = error_messages(block_track, partial, other, both, leader, mean, seq_count)
     final = lax.all_to_all(final, "seq", 0, 0).reshape(target_d, width + 128)
     return finish(seq_index, final, reg_weight, selector, divisor)
 

time: 194 us -> 171 us (0.88)
  blocking collectives: 97.4 us -> 81.6 us
  waiting for transfers between devices: 16.5 us -> 12.1 us
  starting transfers between devices: 23.4 us -> 20.9 us
    all_to_all x3, blocking collectives: 69.7 us -> 54.4 us  [the longest x1 22.4 us: local(): part = lax.all_to_all(part, 'seq', 0, 0, axis_index_groups=GROUP_YX)]
    all_to_all x1, waiting for transfers between devices: 11.7 us -> 0.01 us  [spread(): return lax.all_to_all(wide, 'seq', 0, 0, axis_index_groups=groups)]
    ppermute x7, waiting for transfers between devices: 0.02 us -> 7.22 us  [the longest x4 7.21 us: gather_ring(): up = lax.ppermute(up, 'seq', ring(seq_count, 1))]
  transfers between devices with their start and end apart: 10 -> 10, of which waited for: 3 -> 4; matrix products, arithmetic and copies ran while one was open for 8% -> 9% of each run, Pallas kernels for 0% -> 0%
where the time goes in v5:
time: 171 us; the launch traced here: 168 us
  blocking collectives  81.6 us (48%)
  Pallas kernels  35.3 us (21%)
  starting transfers between devices  20.9 us (12%)
  local copies, waits for them, and re-layouts  14.5 us (8%)
  waiting for transfers between devices  12.1 us (7%)
  other arithmetic  3.25 us (2%)
    all_to_all x1, blocking collectives, local(): final = lax.all_to_all(final, 'seq', 0, 0).reshape(target_d, width + 128)  27.3 us
    pallas_call x1, Pallas kernels, attend(): pl.pallas_call(attend_kernel, grid=(pairs, SIDE // 2), in_specs=[pl.Block...  23.4 us
    all_to_all x1, blocking collectives, local(): part = lax.all_to_all(part, 'seq', 0, 0, axis_index_groups=GROUP_YX)  22.4 us
    all_to_all x1, blocking collectives, local(): both = lax.all_to_all(both, 'seq', 0, 0, axis_index_groups=GROUP_Z)  16.4 us
    all_to_all x1, blocking collectives, spread(): return lax.all_to_all(wide, 'seq', 0, 0, axis_index_groups=groups)  15.5 us
    ppermute x3, starting transfers between devices, gather_ring(): down = lax.ppermute(down, 'seq', ring(seq_count, -1))  10.5 us
    all_to_all x1, starting transfers between devices, spread(): return lax.all_to_all(wide, 'seq', 0, 0, axis_index_groups=groups)  7.6 us
    ppermute x4, waiting for transfers between devices, gather_ring(): up = lax.ppermute(up, 'seq', ring(seq_count, 1))  7.21 us
  transfers between devices with their start and end apart: 10, of which 4 were waited for; matrix products, arithmetic and copies ran while one was open for 9% of the time, Pallas kernels for 0%

profile of v5, /device:TPU:2, one launch (start us, length us, event | category | flops | bytes accessed | tf_op | source)
XLA Modules:
  0.0 168.5 jit_solution(8118200150303905182)
XLA Ops:
  0.6 0.9 constant_dynamic-update-slice_fusion.1
  1.5 0.9 constant_dynamic-update-slice_fusion.refs_0_
  2.5 2.0 %collective-permute-start = (bf16[512,256]{1,0:T(8,128)(2,1)S(1)}, bf16[512,256]{1,0:T(8,128)(2,1)S(1)}, u32[]{:S(2)}, u32[]{:S(2)}) collective-permute-start(bf16[512,256]{1,0:T(8,128)(2,1)S(1)} %constant_dynamic-update-slice_fusion.refs_0_), channel_id=1, source_target_pairs={{0,4},{4,8},{8,12},{12,16},{16,20},{20,24},{24,28},{28,0},{32,36},... | collective-permute-start | bytes 786440 | tf_op jit(solution)/shard_map/ppermute | solution.py:38
  4.5 4.0 %collective-permute-start.1 = (bf16[512,256]{1,0:T(8,128)(2,1)S(1)}, bf16[512,256]{1,0:T(8,128)(2,1)S(1)}, u32[]{:S(2)}, u32[]{:S(2)}) collective-permute-start(bf16[512,256]{1,0:T(8,128)(2,1)S(1)} %constant_dynamic-update-slice_fusion.refs_0_), channel_id=1, source_target_pairs={{0,28},{4,0},{8,4},{12,8},{16,12},{20,16},{24,20},{28,24},{32,60},... | collective-permute-start | bytes 786440 | tf_op jit(solution)/shard_map/ppermute | solution.py:41
  8.5 1.9 %broadcast_in_dim.32 = bf16[8,256,256]{2,1,0:T(8,128)(2,1)} broadcast(bf16[256,256]{1,0:T(8,128)(2,1)} %param.9), dimensions={1,2} | broadcast | bytes 1179648 | tf_op jit(solution)/shard_map/broadcast_in_dim | solution.py:23
  10.5 7.6 %all-to-all-start = ((bf16[8,256,256]{2,1,0:T(8,128)(2,1)}), bf16[8,256,256]{2,1,0:T(8,128)(2,1)S(1)}, u32[]{:S(2)}, u32[]{:S(2)}) async-start(bf16[8,256,256]{2,1,0:T(8,128)(2,1)} %broadcast_in_dim.32), calls=%async_computation | async-start | bytes 2097152 | tf_op jit(solution)/shard_map/all_to_all | solution.py:24
  18.8 0.7 add_convert_fusion.1
  20.3 3.2 %collective-permute-start.3 = (bf16[512,256]{1,0:T(8,128)(2,1)S(1)}, bf16[512,256]{1,0:T(8,128)(2,1)S(1)}, u32[]{:S(2)}, u32[]{:S(2)}) collective-permute-start(bf16[512,256]{1,0:T(8,128)(2,1)S(1)} %collective-permute-done.1.refs_2_), channel_id=1, source_target_pairs={{0,28},{4,0},{8,4},{12,8},{16,12},{20,16},{24,20},{28,24},{32,60},... | collective-permute-start | bytes 786440 | tf_op jit(solution)/shard_map/ppermute | solution.py:41
  23.5 4.5 %collective-permute-done.2.refs_3_ = bf16[512,256]{1,0:T(8,128)(2,1)S(1)} collective-permute-done((bf16[512,256]{1,0:T(8,128)(2,1)S(1)}, bf16[512,256]{1,0:T(8,128)(2,1)S(1)}, u32[]{:S(2)}, u32[]{:S(2)}) %collective-permute-start.2) | collective-permute-done | bytes 262176 | tf_op jit(solution)/shard_map/ppermute | solution.py:38
  28.0 0.7 constant_dynamic-slice_fusion
  28.9 0.7 fusion.7
  29.6 3.2 %collective-permute-start.5 = (bf16[512,256]{1,0:T(8,128)(2,1)S(1)}, bf16[512,256]{1,0:T(8,128)(2,1)S(1)}, u32[]{:S(2)}, u32[]{:S(2)}) collective-permute-start(bf16[512,256]{1,0:T(8,128)(2,1)S(1)} %collective-permute-done.3.refs_4_), channel_id=1, source_target_pairs={{0,28},{4,0},{8,4},{12,8},{16,12},{20,16},{24,20},{28,24},{32,60},... | collective-permute-start | bytes 786440 | tf_op jit(solution)/shard_map/ppermute | solution.py:41
  32.8 2.7 %collective-permute-done.4.refs_5_ = bf16[512,256]{1,0:T(8,128)(2,1)S(1)} collective-permute-done((bf16[512,256]{1,0:T(8,128)(2,1)S(1)}, bf16[512,256]{1,0:T(8,128)(2,1)S(1)}, u32[]{:S(2)}, u32[]{:S(2)}) %collective-permute-start.4) | collective-permute-done | bytes 262176 | tf_op jit(solution)/shard_map/ppermute | solution.py:38
  36.3 1.5 copy.27
  37.8 0.7 copy.30
  38.5 1.3 broadcast_in_dim.62
  39.8 1.5 reshape_reshape.3.leader_ref
  41.3 1.5 convert_element_type.35.ids_here_ref.ids_ref
  42.8 1.1 pad.4.count_ref
  44.0 1.0 fusion.1
  45.7 23.4 %attend.1 = bf16[8,304,256]{2,1,0:T(8,128)(2,1)S(1)} custom-call(bf16[2048,256]{1,0:T(8,128)(2,1)S(1)} %bitcast.24, bf16[8,32,256]{2,1,0:T(8,128)(2,1)S(1)} %pad_maximum_fusion.piece_ref, f32[1,128]{1,0:T(1,128)S(1)} %copy-done.7, bf16[512,256]{1,0:T(8,128)(2,1)S(1)} %constant_dynamic-update-slice_fusion.refs_0_, ...), custom_call_target="tpu_custom_call" | custom-call | tf_op jit(solution)/shard_map/attend/pallas_call | solution.py:104
  69.1 22.4 %all_to_all.25.part_ref = bf16[8,304,256]{2,1,0:T(8,128)(2,1)S(1)} all-to-all(bf16[8,304,256]{2,1,0:T(8,128)(2,1)S(1)} %attend.1), channel_id=1, replica_groups={{0,32,64,96,128,160,192,224},{4,36,68,100,132,164,196,228},{8,40,72,104..., dimensions={0} | all-to-all | bytes 2490368 | tf_op jit(solution)/shard_map/all_to_all | solution.py:409
  91.5 1.5 merge.1
  93.0 16.4 %all_to_all.26.both_ref = bf16[8,80,256]{2,1,0:T(8,128)(2,1)S(1)} all-to-all(bf16[8,80,256]{2,1,0:T(8,128)(2,1)S(1)} %merge.1), channel_id=1, replica_groups={{0,4,8,12,16,20,24,28},{32,36,40,44,48,52,56,60},{64,68,72,76,80,84,88,..., dimensions={0} | all-to-all | bytes 655360 | tf_op jit(solution)/shard_map/all_to_all | solution.py:411
  109.6 15.5 %all_to_all.27.every_ref = bf16[8,256,256]{2,1,0:T(8,128)(2,1)S(1)} all-to-all(bf16[8,256,256]{2,1,0:T(8,128)(2,1)S(1)} %broadcast_in_dim.64), channel_id=1, replica_groups={{0,32,64,96,128,160,192,224},{4,36,68,100,132,164,196,228},{8,40,72,104..., dimensions={0} | all-to-all | bytes 2097152 | tf_op jit(solution)/shard_map/all_to_all | solution.py:24
  125.1 7.0 %track_means.1 = (bf16[2048,256]{1,0:T(8,128)(2,1)S(1)}, bf16[16,2048]{1,0:T(8,128)(2,1)S(1)}, f32[2048,128]{1,0:T(8,128)S(1)}) custom-call(f32[1,2048]{1,0:T(1,128)S(1)} %copy-done.2, f32[1,2048]{1,0:T(1,128)S(1)} %copy-done.2, bf16[8,256,256]{2,1,0:T(8,128)(2,1)S(1)} %all_to_all.27.every_ref, bf16[8,80,256]{2,1,0:T(8,128)(2,1)S(1)} %all_to_all.26.both_ref, ...), custom_call_target="tpu_custom_call" | custom-call | tf_op jit(solution)/shard_map/track_means/pallas_call | solution.py:245
  132.1 1.3 collective-permute-done.7
  133.4 0.8 collective-permute-start.8
  134.1 3.6 %collective-permute-done.8.other_ref = bf16[16,2048]{1,0:T(8,128)(2,1)S(1)} collective-permute-done((bf16[16,2048]{1,0:T(8,128)(2,1)S(1)}, bf16[16,2048]{1,0:T(8,128)(2,1)S(1)}, u32[]{:S(2)}, u32[]{:S(2)}) %collective-permute-start.8) | collective-permute-done | bytes 65568 | tf_op jit(solution)/shard_map/ppermute | solution.py:417
  137.7 2.1 %error_messages.1 = bf16[64,16,384]{2,1,0:T(8,128)(2,1)S(1)} custom-call(s32[128]{0:T(128)S(1)} %copy-done.6, bf16[16,2048]{1,0:T(8,128)(2,1)S(1)} %add_convert_fusion.part_ref, bf16[16,2048]{1,0:T(8,128)(2,1)S(1)} %collective-permute-done.8.other_ref, bf16[8,80,256]{2,1,0:T(8,128)(2,1)S(1)} %all_to_all.26.both_ref, f32[1,2048]{1,0:T(1,128)S(1)} %copy-done.3, ...), custom_call_target="tpu_custom_call" | custom-call | tf_op jit(solution)/shard_map/error_messages/pallas_call | solution.py:313
  139.8 27.3 %all_to_all.28 = bf16[64,16,384]{2,1,0:T(8,128)(2,1)S(1)} all-to-all(bf16[64,16,384]{2,1,0:T(8,128)(2,1)S(1)} %error_messages.1), channel_id=1, replica_groups=mesh['seq'=64,'head'=4] {'seq'}, dimensions={0} | all-to-all | bytes 1572864 | tf_op jit(solution)/shard_map/all_to_all | solution.py:419
  167.1 1.4 finish.1
  (46 shorter events, 3.1 us)
Async XLA Ops:
  2.5 17.1 %collective-permute-start = (bf16[512,256]{1,0:T(8,128)(2,1)S(1)}, bf16[512,256]{1,0:T(8,128)(2,1)S(1)}, u32[]{:S(2)}, u32[]{:S(2)}) collective-permute-start(bf16[512,256]{1,0:T(8,128)(2,1)S(1)} %constant_dynamic-update-slice_fusion.refs_0_), channel_id=1, source_target_pairs={{0,4},{4,8},{8,12},{12,16},{16,20},{20,24},{24,28},{28,0},{32,36},... | collective-permute-start | bytes 786440 | tf_op jit(solution)/shard_map/ppermute | solution.py:38
  4.5 15.8 %collective-permute-start.1 = (bf16[512,256]{1,0:T(8,128)(2,1)S(1)}, bf16[512,256]{1,0:T(8,128)(2,1)S(1)}, u32[]{:S(2)}, u32[]{:S(2)}) collective-permute-start(bf16[512,256]{1,0:T(8,128)(2,1)S(1)} %constant_dynamic-update-slice_fusion.refs_0_), channel_id=1, source_target_pairs={{0,28},{4,0},{8,4},{12,8},{16,12},{20,16},{24,20},{28,24},{32,60},... | collective-permute-start | bytes 786440 | tf_op jit(solution)/shard_map/ppermute | solution.py:41
  10.4 7.6 %copy-start.5 = (s32[128]{0:T(128)S(1)}, s32[128]{0:T(128)}, u32[]{:S(2)}) copy-start(s32[128]{0:T(128)} %track_ref.1) | copy-start | bytes 1540
  10.4 7.8 %copy-start.10 = (s32[2]{0:T(128)S(1)}, s32[2]{0:T(128)}, u32[]{:S(2)}) copy-start(s32[2]{0:T(128)} %param.16) | copy-start | bytes 28
  10.4 7.9 %copy-start.9 = (s32[2,128]{1,0:T(2,128)S(1)}, s32[2,128]{1,0:T(2,128)}, u32[]{:S(2)}) copy-start(s32[2,128]{1,0:T(2,128)} %param.17) | copy-start | bytes 3076
  10.4 17.5 %copy-start = (bf16[256,1024]{1,0:T(8,128)(2,1)S(1)}, bf16[256,1024]{1,0:T(8,128)(2,1)}, u32[]{:S(2)}) copy-start(bf16[256,1024]{1,0:T(8,128)(2,1)} %weight_ref.1) | copy-start | bytes 1572868
  10.4 18.2 %copy-start.8 = (bf16[4,16,1024]{2,1,0:T(8,128)(2,1)S(1)}, bf16[4,16,1024]{2,1,0:T(8,128)(2,1)}, u32[]{:S(2)}) copy-start(bf16[4,16,1024]{2,1,0:T(8,128)(2,1)} %param.14) | copy-start | bytes 393220
  10.5 34.5 %all-to-all-start = ((bf16[8,256,256]{2,1,0:T(8,128)(2,1)}), bf16[8,256,256]{2,1,0:T(8,128)(2,1)S(1)}, u32[]{:S(2)}, u32[]{:S(2)}) async-start(bf16[8,256,256]{2,1,0:T(8,128)(2,1)} %broadcast_in_dim.32), calls=%async_computation | async-start | bytes 2097152 | tf_op jit(solution)/shard_map/all_to_all | solution.py:24
  19.6 8.4 %collective-permute-start.2 = (bf16[512,256]{1,0:T(8,128)(2,1)S(1)}, bf16[512,256]{1,0:T(8,128)(2,1)S(1)}, u32[]{:S(2)}, u32[]{:S(2)}) collective-permute-start(bf16[512,256]{1,0:T(8,128)(2,1)S(1)} %collective-permute-done.refs_1_), channel_id=1, source_target_pairs={{0,4},{4,8},{8,12},{12,16},{16,20},{20,24},{24,28},{28,0},{32,36},... | collective-permute-start | bytes 786440 | tf_op jit(solution)/shard_map/ppermute | solution.py:38
  20.3 9.3 %collective-permute-start.3 = (bf16[512,256]{1,0:T(8,128)(2,1)S(1)}, bf16[512,256]{1,0:T(8,128)(2,1)S(1)}, u32[]{:S(2)}, u32[]{:S(2)}) collective-permute-start(bf16[512,256]{1,0:T(8,128)(2,1)S(1)} %collective-permute-done.1.refs_2_), channel_id=1, source_target_pairs={{0,28},{4,0},{8,4},{12,8},{16,12},{20,16},{24,20},{28,24},{32,60},... | collective-permute-start | bytes 786440 | tf_op jit(solution)/shard_map/ppermute | solution.py:41
  28.0 7.6 %collective-permute-start.4 = (bf16[512,256]{1,0:T(8,128)(2,1)S(1)}, bf16[512,256]{1,0:T(8,128)(2,1)S(1)}, u32[]{:S(2)}, u32[]{:S(2)}) collective-permute-start(bf16[512,256]{1,0:T(8,128)(2,1)S(1)} %collective-permute-done.2.refs_3_), channel_id=1, source_target_pairs={{0,4},{4,8},{8,12},{12,16},{16,20},{20,24},{24,28},{28,0},{32,36},... | collective-permute-start | bytes 786440 | tf_op jit(solution)/shard_map/ppermute | solution.py:38
  29.6 15.4 %collective-permute-start.5 = (bf16[512,256]{1,0:T(8,128)(2,1)S(1)}, bf16[512,256]{1,0:T(8,128)(2,1)S(1)}, u32[]{:S(2)}, u32[]{:S(2)}) collective-permute-start(bf16[512,256]{1,0:T(8,128)(2,1)S(1)} %collective-permute-done.3.refs_4_), channel_id=1, source_target_pairs={{0,28},{4,0},{8,4},{12,8},{16,12},{20,16},{24,20},{28,24},{32,60},... | collective-permute-start | bytes 786440 | tf_op jit(solution)/shard_map/ppermute | solution.py:41
  35.6 9.5 %collective-permute-start.6 = (bf16[512,256]{1,0:T(8,128)(2,1)S(1)}, bf16[512,256]{1,0:T(8,128)(2,1)}, u32[]{:S(2)}, u32[]{:S(2)}) collective-permute-start(bf16[512,256]{1,0:T(8,128)(2,1)S(1)} %collective-permute-done.4.refs_5_), channel_id=1, source_target_pairs={{0,4},{4,8},{8,12},{12,16},{16,20},{20,24},{24,28},{28,0},{32,36},... | collective-permute-start | bytes 786440 | tf_op jit(solution)/shard_map/ppermute | solution.py:38
  45.0 0.7 copy-start.7
  69.1 22.4 %copy-start.1 = (bf16[256,256]{1,0:T(8,128)(2,1)S(1)}, bf16[256,256]{1,0:T(8,128)(2,1)}, u32[]{:S(2)}) copy-start(bf16[256,256]{1,0:T(8,128)(2,1)} %residual_ref.1) | copy-start | bytes 393220
  109.5 15.6 %copy-start.2 = (f32[1,2048]{1,0:T(1,128)S(1)}, f32[1,2048]{1,0:T(1,128)}, u32[]{:S(2)}) copy-start(f32[1,2048]{1,0:T(1,128)} %convert_element_type.35.ids_here_ref.ids_ref) | copy-start | bytes 24580
  109.6 15.6 %copy-start.4 = (bf16[256,16]{0,1:T(8,128)(2,1)S(1)}, bf16[256,16]{0,1:T(8,128)(2,1)}, u32[]{:S(2)}) copy-start(bf16[256,16]{0,1:T(8,128)(2,1)} %copy.27) | copy-start | bytes 24580
  125.1 12.6 %copy-start.3 = (f32[1,2048]{1,0:T(1,128)S(1)}, f32[1,2048]{1,0:T(1,128)}, u32[]{:S(2)}) copy-start(f32[1,2048]{1,0:T(1,128)} %reshape_reshape.3.leader_ref) | copy-start | bytes 24580
  125.1 12.6 %copy-start.6 = (s32[128]{0:T(128)S(1)}, s32[128]{0:T(128)}, u32[]{:S(2)}) copy-start(s32[128]{0:T(128)} %track_ref.1) | copy-start | bytes 1540
  132.1 1.3 collective-permute-start.7
  133.4 4.4 %collective-permute-start.8 = (bf16[16,2048]{1,0:T(8,128)(2,1)S(1)}, bf16[16,2048]{1,0:T(8,128)(2,1)S(1)}, u32[]{:S(2)}, u32[]{:S(2)}) collective-permute-start(bf16[16,2048]{1,0:T(8,128)(2,1)S(1)} %add_convert_fusion.part_ref), channel_id=1, source_target_pairs={{0,2},{2,0},{1,3},{3,1},{4,6},{6,4},{5,7},{7,5},{8,10},{10,8},{9,1... | collective-permute-start | bytes 196616 | tf_op jit(solution)/shard_map/ppermute | solution.py:417

commit v6 on v5

--- a/solution.py
+++ b/solution.py
@@ -13,6 +13,7 @@
 SIDE = 8
 LOG2E = 1.4426950408889634
 STAT = 16
+EARLIER = 32768.0
 VMEM_BYTES = 24 * 1024 * 1024
 
 GROUP_Z = [[g * SIDE + i for i in range(SIDE)] for g in range(SIDE)]
@@ -41,6 +42,54 @@
             down = lax.ppermute(down, "seq", ring(seq_count, -1))
             pieces.append(down)
     return pieces
+
+
+def prepare_kernel(row_count_ref, slot_ref, target_ref, carried_ref, sel_ref, count_ref):
+    here = slot_ref.shape[0]
+    slots = slot_ref[...]
+    sub = lax.broadcasted_iota(jnp.int32, (POOL, BLK), 0)
+    lane = lax.broadcasted_iota(jnp.int32, (POOL, BLK), 1)
+    zero = jnp.zeros((POOL, BLK), jnp.float32)
+    picks = []
+    for b in range(here):
+        hit = (slots[b : b + 1] == sub) & (lane < row_count_ref[b])
+        hit = jnp.where(hit, 1.0, 0.0)
+        picks.append(jnp.concatenate([hit if i == b else zero for i in range(here)], axis=1))
+    sel = jnp.concatenate(picks, axis=0)
+    sel_ref[...] = sel.astype(jnp.bfloat16)
+    counts = jnp.broadcast_to(jnp.sum(sel, axis=1, keepdims=True), (sel.shape[0], 128))
+    counts = jnp.concatenate(
+        [counts, jnp.zeros((128 - counts.shape[0], 128), jnp.float32)], axis=0
+    )
+    count_ref[...] = counts.T[:1]
+    rows = target_ref.shape[0]
+    blank = jnp.zeros((128 - rows, 128), jnp.float32)
+    for g in range(SIDE):
+        tile = target_ref[:, g * 128 : g * 128 + 128].astype(jnp.float32)
+        tile = jnp.concatenate([tile, blank], axis=0).T
+        eights = [
+            tile[z * 16 : z * 16 + 8] + pltpu.roll(tile[z * 16 + 8 : z * 16 + 16], 64, 1)
+            for z in range(SIDE)
+        ]
+        carried_ref[g] = jnp.concatenate(
+            [jnp.concatenate(eights[:4], axis=0), jnp.concatenate(eights[4:], axis=0)], axis=1
+        ).astype(jnp.bfloat16)
+
+
+def prepare(row_count, pool_slot, targets):
+    here = pool_slot.shape[0]
+    vmem = pl.BlockSpec(memory_space=pltpu.VMEM)
+    return pl.pallas_call(
+        prepare_kernel,
+        in_specs=[pl.BlockSpec(memory_space=pltpu.SMEM), vmem, vmem],
+        out_shape=[
+            jax.ShapeDtypeStruct((SIDE, 32, 256), jnp.bfloat16),
+            jax.ShapeDtypeStruct((here * POOL, here * BLK), jnp.bfloat16),
+            jax.ShapeDtypeStruct((1, 128), jnp.float32),
+        ],
+        compiler_params=pltpu.CompilerParams(vmem_limit_bytes=VMEM_BYTES),
+        name="prepare",
+    )(row_count, pool_slot, targets)
 
 
 def attend_kernel(q_ref, piece_ref, count_ref, *refs):
@@ -197,11 +246,22 @@
 
 
 def track_kernel(
-    ids_here_ref, ids_ref, every_ref, both_ref, weight_ref, mean_ref, part_ref, divisor_ref, count_buf
+    track_ref,
+    index_ref,
+    every_ref,
+    both_ref,
+    weight_ref,
+    mean_ref,
+    part_ref,
+    divisor_ref,
+    count_buf,
+    id_buf,
+    weight_buf,
 ):
     step = mean_ref.shape[0]
-
-    @pl.when(pl.program_id(0) == 0)
+    at = pl.program_id(0)
+
+    @pl.when(at == 0)
     def _():
         lane = lax.broadcasted_iota(jnp.int32, (1, 128), 1)
         rows = [
@@ -216,61 +276,83 @@
                     row = pltpu.roll(row, turn, 1) if turn else row
                     tile = jnp.where(lane // 32 == q, row, tile)
                 count_buf[g : g + 1, half * 128 : half * 128 + 128] = tile
-
-    here = column(ids_here_ref[...])
+                track = jnp.zeros((1, 128), jnp.int32)
+                for j in range(8):
+                    track = jnp.where(lane // POOL == j, track_ref[g * 16 + half * 8 + j], track)
+                id_buf[g : g + 1, half * 128 : half * 128 + 128] = (
+                    track * POOL + lane % POOL
+                ).astype(jnp.float32)
+        weight_buf[...] = weight_ref[...].T
+
+    here = column(id_buf[pl.ds(at, 1)])
     sums = jnp.zeros(mean_ref.shape, jnp.float32)
     counts = jnp.zeros((step, step), jnp.float32)
     for g in range(SIDE):
-        match = here == ids_ref[:, g * step : g * step + step]
+        match = here == id_buf[g : g + 1]
         sums = sums + jnp.dot(
             jnp.where(match, 1.0, 0.0).astype(jnp.bfloat16),
             every_ref[g],
             preferred_element_type=jnp.float32,
         )
-        counts = counts + jnp.where(match, count_buf[g : g + 1], 0.0)
-    divisor = jnp.maximum(jnp.sum(counts, axis=1, keepdims=True), 1.0)
+        seen = count_buf[g : g + 1] + jnp.where(g < at, EARLIER, 0.0)
+        counts = counts + jnp.where(match, seen, 0.0)
+    below = lax.broadcasted_iota(jnp.int32, (step, step), 1) < lax.broadcasted_iota(
+        jnp.int32, (step, step), 0
+    )
+    counts = counts + jnp.where((here == id_buf[pl.ds(at, 1)]) & below, EARLIER, 0.0)
+    total = jnp.sum(counts, axis=1, keepdims=True)
+    before = jnp.floor(total * (1.0 / EARLIER))
+    divisor = jnp.maximum(total - before * EARLIER, 1.0)
     divisor_ref[...] = jnp.broadcast_to(divisor, divisor_ref.shape)
-    mean = (sums / divisor).astype(jnp.bfloat16)
-    mean_ref[...] = mean
+    mean = sums / divisor
+    mean_ref[...] = jnp.where(before > 0.0, 0.0, mean).astype(jnp.bfloat16)
+    chunk = part_ref.shape[0]
+    start = pl.multiple_of(lax.rem(index_ref[0], 128 // chunk) * chunk, chunk)
     part_ref[...] = lax.dot_general(
-        weight_ref[...], mean, (((1,), (1,)), ((), ())), preferred_element_type=jnp.float32
+        weight_buf[pl.ds(start, chunk)],
+        mean.astype(jnp.bfloat16),
+        (((1,), (1,)), ((), ())),
+        preferred_element_type=jnp.float32,
     ).astype(jnp.bfloat16)
 
 
-def track_means(ids, every, both, weight):
-    width = every.shape[2]
-    rows = ids.shape[1]
-    chunk = weight.shape[0]
-    step = rows // SIDE
+def track_means(tracks, index, every, both, weight, chunk):
+    step, width = every.shape[1:]
+    rows = SIDE * step
     return pl.pallas_call(
         track_kernel,
-        grid=(SIDE,),
-        in_specs=[
-            pl.BlockSpec((1, step), lambda i: (0, i)),
-            pl.BlockSpec((1, rows), lambda i: (0, 0)),
-            pl.BlockSpec(every.shape, lambda i: (0, 0, 0)),
-            pl.BlockSpec(both.shape, lambda i: (0, 0, 0)),
-            pl.BlockSpec((chunk, width), lambda i: (0, 0)),
-        ],
-        out_specs=[
-            pl.BlockSpec((step, width), lambda i: (i, 0)),
-            pl.BlockSpec((chunk, step), lambda i: (0, i)),
-            pl.BlockSpec((step, 128), lambda i: (i, 0)),
-        ],
+        grid_spec=pltpu.PrefetchScalarGridSpec(
+            num_scalar_prefetch=2,
+            grid=(SIDE,),
+            in_specs=[
+                pl.BlockSpec(every.shape, lambda i, t, at: (0, 0, 0)),
+                pl.BlockSpec(both.shape, lambda i, t, at: (0, 0, 0)),
+                pl.BlockSpec((width, 128), lambda i, t, at: (0, at[0] // (128 // chunk))),
+            ],
+            out_specs=[
+                pl.BlockSpec((step, width), lambda i, t, at: (i, 0)),
+                pl.BlockSpec((chunk, step), lambda i, t, at: (0, i)),
+                pl.BlockSpec((step, 128), lambda i, t, at: (i, 0)),
+            ],
+            scratch_shapes=[
+                pltpu.VMEM((SIDE, step), jnp.float32),
+                pltpu.VMEM((SIDE, step), jnp.float32),
+                pltpu.VMEM((128, width), jnp.bfloat16),
+            ],
+        ),
         out_shape=[
             jax.ShapeDtypeStruct((rows, width), jnp.bfloat16),
             jax.ShapeDtypeStruct((chunk, rows), jnp.bfloat16),
             jax.ShapeDtypeStruct((rows, 128), jnp.float32),
         ],
-        scratch_shapes=[pltpu.VMEM((SIDE, step), jnp.float32)],
         compiler_params=pltpu.CompilerParams(vmem_limit_bytes=VMEM_BYTES),
         name="track_means",
-    )(ids, ids, every, both, weight)
-
-
-def error_kernel(track_ref, part_ref, other_ref, both_ref, leader_ref, mean_ref, out_ref, target_buf):
-    back = part_ref.shape[1] // out_ref.shape[0]
-    width = mean_ref.shape[1]
+    )(tracks, index, every, both, weight)
+
+
+def error_kernel(track_ref, part_ref, other_ref, both_ref, mean_ref, out_ref, target_buf):
+    chunk = part_ref.shape[0]
+    back = part_ref.shape[1] // target_buf.shape[0]
     for z in range(SIDE):
         carried = both_ref[z, back : back + 32].astype(jnp.float32)
         for g in range(SIDE):
@@ -294,30 +376,56 @@
     total = part_ref[...].astype(jnp.float32) + other_ref[...].astype(jnp.float32)
     error = (total - target).astype(jnp.bfloat16).astype(jnp.float32)
     grad = jnp.dot(
-        (error * leader_ref[...]).astype(jnp.bfloat16),
-        mean_ref[...],
-        preferred_element_type=jnp.float32,
+        error.astype(jnp.bfloat16), mean_ref[...], preferred_element_type=jnp.float32
     ).astype(jnp.bfloat16)
-    per = 128 // back
-    for s in range(out_ref.shape[0]):
-        tile = error[:, s // per * 128 : s // per * 128 + 128]
-        turn = s % per * back
-        rows = pltpu.roll(tile, 128 - turn, 1) if turn else tile
-        out_ref[s, :, :width] = grad
-        out_ref[s, :, width:] = rows.astype(jnp.bfloat16)
-
-
-def error_messages(tracks, partial, other, both, leader, mean, seq_count):
+    wide = lax.broadcasted_iota(jnp.int32, (chunk, 128), 1)
+    for z in range(SIDE):
+        out_ref[z, :chunk] = grad
+        for half in range(2):
+            tile = jnp.zeros((chunk, 128), jnp.float32)
+            for q in range(4):
+                source = (half * 4 + q) * 2 + z // 4
+                row = error[:, source * 128 : source * 128 + 128]
+                turn = (q - z % 4) % 4 * 32
+                row = pltpu.roll(row, turn, 1) if turn else row
+                tile = jnp.where(wide // 32 == q, row, tile)
+            out_ref[z, chunk:, half * 128 : half * 128 + 128] = tile.astype(jnp.bfloat16)
+
+
+def error_messages(tracks, partial, other, both, mean, seq_count):
     chunk = partial.shape[0]
     vmem = pl.BlockSpec(memory_space=pltpu.VMEM)
     return pl.pallas_call(
         error_kernel,
-        in_specs=[pl.BlockSpec(memory_space=pltpu.SMEM), vmem, vmem, vmem, vmem, vmem],
-        out_shape=jax.ShapeDtypeStruct((seq_count, chunk, mean.shape[1] + 128), jnp.bfloat16),
+        in_specs=[pl.BlockSpec(memory_space=pltpu.SMEM), vmem, vmem, vmem, vmem],
+        out_shape=jax.ShapeDtypeStruct((SIDE, 2 * chunk, mean.shape[1]), jnp.bfloat16),
         scratch_shapes=[pltpu.VMEM((seq_count, 8, 128), jnp.float32)],
         compiler_params=pltpu.CompilerParams(vmem_limit_bytes=VMEM_BYTES),
         name="error_messages",
-    )(tracks, partial, other, both, leader, mean)
+    )(tracks, partial, other, both, mean)
+
+
+def relay_kernel(in_ref, out_ref):
+    chunk, width = in_ref.shape[1] // 2, in_ref.shape[2]
+    for z in range(SIDE):
+        span = slice(z * chunk, z * chunk + chunk)
+        grad = in_ref[z, :chunk]
+        errors = in_ref[z, chunk:].astype(jnp.float32)
+        for g in range(SIDE):
+            tile = errors[:, g // 4 * 128 : g // 4 * 128 + 128]
+            tile = pltpu.roll(tile, 128 - g % 4 * 32, 1) if g % 4 else tile
+            out_ref[g, span, :width] = grad
+            out_ref[g, span, width:] = tile.astype(jnp.bfloat16)
+
+
+def relay(x):
+    chunk, width = x.shape[1] // 2, x.shape[2]
+    return pl.pallas_call(
+        relay_kernel,
+        out_shape=jax.ShapeDtypeStruct((SIDE, SIDE * chunk, width + 128), jnp.bfloat16),
+        compiler_params=pltpu.CompilerParams(vmem_limit_bytes=VMEM_BYTES),
+        name="relay",
+    )(x)
 
 
 def finish_kernel(index_ref, final_ref, weight_ref, sel_ref, divisor_ref, grad_ref, context_ref):
@@ -358,66 +466,39 @@
         ],
         compiler_params=pltpu.CompilerParams(vmem_limit_bytes=VMEM_BYTES),
         name="finish",
-    )(index.reshape(1).astype(jnp.int32), final, weight, sel, divisor)
+    )(index, final, weight, sel, divisor)
 
 
 def local(queries, keys, values, residual, reg_weight, targets, block_track, row_count, pool_slot):
     tok_rows, width = queries.shape
-    here = tok_rows // BLK
     seq_count = lax.axis_size("seq")
-    seq_index = lax.axis_index("seq")
-    blocks = here * seq_count
-    target_d = reg_weight.shape[1]
-    chunk = target_d // seq_count
-    owned = targets.shape[0]
-
-    own_kv = jnp.concatenate([keys, values], axis=0)
-    pieces = gather_ring(own_kv, seq_count)
+    index = lax.axis_index("seq").astype(jnp.int32).reshape(1)
+    owned, pool, target_d = targets.shape
+
+    pieces = gather_ring(jnp.concatenate([keys, values], axis=0), seq_count)
     query_all = spread(queries, GROUP_YX).reshape(SIDE * tok_rows, width)
-
-    valid = jnp.arange(BLK, dtype=jnp.int32)[None, :] < row_count[:, None]
-    match = pool_slot[:, None, :] == jnp.arange(POOL, dtype=jnp.int32)[None, :, None]
-    sel = match & valid[:, None, :]
-    same_block = jnp.arange(here)[:, None] == jnp.arange(here)[None, :]
-    selector = (
-        jnp.where(sel[:, :, None, :] & same_block[:, None, :, None], 1.0, 0.0)
-        .astype(jnp.bfloat16)
-        .reshape(here * POOL, tok_rows)
+    carried, selector, slot_rows = prepare(
+        row_count, pool_slot, targets.reshape(owned * pool, target_d)
     )
-    slot_rows = jnp.sum(jnp.where(sel, 1.0, 0.0), axis=2).reshape(1, here * POOL)
-    slot_rows = jnp.pad(slot_rows, ((0, 0), (0, 128 - here * POOL)))
-    turned = targets.reshape(owned * POOL, target_d).T
-    turned = turned.reshape(SIDE, SIDE, 2, chunk // 2, owned * POOL)
-    carried = jnp.concatenate([turned[:, :, 0], turned[:, :, 1]], axis=3)
-    carried = carried.reshape(SIDE, 2, SIDE * chunk // 4, 128)
-    carried = jnp.concatenate([carried[:, 0], carried[:, 1]], axis=2)
-    same = block_track[:, None] == block_track[None, :]
-    earlier = jnp.arange(blocks)[None, :] < jnp.arange(blocks)[:, None]
-    leader = jnp.where(jnp.any(same & earlier, axis=1), 0.0, 1.0)
-    leader = jnp.repeat(leader, POOL).reshape(1, blocks * POOL)
-    ids = (
-        (block_track[:, None] * POOL + jnp.arange(POOL, dtype=jnp.int32)[None, :])
-        .reshape(1, blocks * POOL)
-        .astype(jnp.float32)
-    )
-    chunk_weight = lax.dynamic_slice_in_dim(reg_weight, seq_index * chunk, chunk, axis=1).T
 
     part = attend(query_all, pieces, carried, slot_rows)
-    part, selector, leader, ids, chunk_weight = lax.optimization_barrier(
-        (part, selector, leader, ids, chunk_weight)
-    )
+    part, index = lax.optimization_barrier((part, index))
     part = lax.all_to_all(part, "seq", 0, 0, axis_index_groups=GROUP_YX)
     both = merge(part, residual, selector)
     both = lax.all_to_all(both, "seq", 0, 0, axis_index_groups=GROUP_Z)
-    pooled = both[:, : here * POOL].reshape(blocks * POOL // SIDE, width)
+    back = selector.shape[0]
+    pooled = both[:, :back].reshape(SIDE * back, width)
     every = spread(pooled, GROUP_YX)
-    mean, partial, divisor = track_means(ids, every, both, chunk_weight)
+    mean, partial, divisor = track_means(
+        block_track, index, every, both, reg_weight, target_d // seq_count
+    )
     core_mate = lax.ppermute(partial, "head", [(0, 1), (1, 0), (2, 3), (3, 2)])
     partial = (partial.astype(jnp.float32) + core_mate.astype(jnp.float32)).astype(jnp.bfloat16)
     other = lax.ppermute(partial, "head", [(0, 2), (2, 0), (1, 3), (3, 1)])
-    final = error_messages(block_track, partial, other, both, leader, mean, seq_count)
-    final = lax.all_to_all(final, "seq", 0, 0).reshape(target_d, width + 128)
-    return finish(seq_index, final, reg_weight, selector, divisor)
+    final = error_messages(block_track, partial, other, both, mean, seq_count)
+    final = lax.all_to_all(final, "seq", 0, 0, axis_index_groups=GROUP_Z)
+    final = lax.all_to_all(relay(final), "seq", 0, 0, axis_index_groups=GROUP_YX)
+    return finish(index, final.reshape(target_d, width + 128), reg_weight, selector, divisor)
 
 
 def solution(mesh):

time: 171 us -> 164 us (0.959); the launches traced: 168 us -> 163 us
  local copies, waits for them, and re-layouts: 14.5 us -> 3.89 us
  waiting for transfers between devices: 12.1 us -> 20.5 us
  other arithmetic: 3.25 us -> 0.02 us
  blocking collectives: 81.6 us -> 79.6 us
    ppermute x3, waiting for transfers between devices: 0.01 us -> 12 us  [gather_ring(): down = lax.ppermute(down, 'seq', ring(seq_count, -1))]
    ppermute x4, waiting for transfers between devices: 7.21 us -> 3.7 us  [gather_ring(): up = lax.ppermute(up, 'seq', ring(seq_count, 1))]
    unnamed x25 -> x13, local copies, waits for them, and re-layouts: 3.84 us -> 0.94 us
    pallas_call x1 -> x3, Pallas kernels: 6.96 us -> 9.32 us  [the longest x1 8.27 us: track_means(): pl.pallas_call(track_kernel, grid_spec=pltpu.PrefetchScalarGridSpec(num_s...]
    all_to_all x1 -> x2, blocking collectives: 27.3 us -> 26.6 us  [the longest x1 15.1 us: local(): lax.all_to_all(relay(final), 'seq', 0, 0, axis_index_groups=GROUP_YX)]
  transfers between devices with their start and end apart: 10 -> 10, of which waited for: 4 -> 6; matrix products, arithmetic and copies ran while one was open for 9% -> 1% of each run, Pallas kernels for 0% -> 1%
where the time goes in v6:
time: 164 us; the launch traced here: 163 us
  blocking collectives  79.6 us (49%)
  Pallas kernels  36.8 us (22%)
  starting transfers between devices  21.9 us (13%)
  waiting for transfers between devices  20.5 us (12%)
  local copies, waits for them, and re-layouts  3.89 us (2%)
    pallas_call x1, Pallas kernels, attend(): pl.pallas_call(attend_kernel, grid=(pairs, SIDE // 2), in_specs=[pl.Block...  22.6 us
    all_to_all x1, blocking collectives, local(): part = lax.all_to_all(part, 'seq', 0, 0, axis_index_groups=GROUP_YX)  21.5 us
    all_to_all x1, blocking collectives, local(): both = lax.all_to_all(both, 'seq', 0, 0, axis_index_groups=GROUP_Z)  15.8 us
    all_to_all x1, blocking collectives, spread(): return lax.all_to_all(wide, 'seq', 0, 0, axis_index_groups=groups)  15.7 us
    all_to_all x1, blocking collectives, local(): lax.all_to_all(relay(final), 'seq', 0, 0, axis_index_groups=GROUP_YX)  15.1 us
    ppermute x3, waiting for transfers between devices, gather_ring(): down = lax.ppermute(down, 'seq', ring(seq_count, -1))  12 us
    all_to_all x1, blocking collectives, local(): final = lax.all_to_all(final, 'seq', 0, 0, axis_index_groups=GROUP_Z)  11.5 us
    ppermute x3, starting transfers between devices, gather_ring(): down = lax.ppermute(down, 'seq', ring(seq_count, -1))  11.3 us
  transfers between devices with their start and end apart: 10, of which 6 were waited for; matrix products, arithmetic and copies ran while one was open for 1% of the time, Pallas kernels for 1%

profile of v6, /device:TPU:2, one launch (start us, length us, event | category | flops | bytes accessed | tf_op | source)
XLA Modules:
  0.0 163.5 jit_solution(6780768945058145864)
XLA Ops:
  0.6 0.9 constant_dynamic-update-slice_fusion.1
  1.5 0.9 constant_dynamic-update-slice_fusion.refs_0_
  2.5 2.0 %collective-permute-start = (bf16[512,256]{1,0:T(8,128)(2,1)S(1)}, bf16[512,256]{1,0:T(8,128)(2,1)S(1)}, u32[]{:S(2)}, u32[]{:S(2)}) collective-permute-start(bf16[512,256]{1,0:T(8,128)(2,1)S(1)} %constant_dynamic-update-slice_fusion.refs_0_), channel_id=1, source_target_pairs={{0,4},{4,8},{8,12},{12,16},{16,20},{20,24},{24,28},{28,0},{32,36},... | collective-permute-start | bytes 786440 | tf_op jit(solution)/shard_map/ppermute | solution.py:39
  4.5 2.0 %broadcast_in_dim.6 = bf16[8,256,256]{2,1,0:T(8,128)(2,1)} broadcast(bf16[256,256]{1,0:T(8,128)(2,1)} %param.9), dimensions={1,2} | broadcast | bytes 1179648 | tf_op jit(solution)/shard_map/broadcast_in_dim | solution.py:24
  6.4 7.6 %all-to-all-start = ((bf16[8,256,256]{2,1,0:T(8,128)(2,1)}), bf16[8,256,256]{2,1,0:T(8,128)(2,1)S(1)}, u32[]{:S(2)}, u32[]{:S(2)}) async-start(bf16[8,256,256]{2,1,0:T(8,128)(2,1)} %broadcast_in_dim.6), calls=%async_computation | async-start | bytes 2097152 | tf_op jit(solution)/shard_map/all_to_all | solution.py:25
  14.0 4.0 %collective-permute-start.1 = (bf16[512,256]{1,0:T(8,128)(2,1)S(1)}, bf16[512,256]{1,0:T(8,128)(2,1)S(1)}, u32[]{:S(2)}, u32[]{:S(2)}) collective-permute-start(bf16[512,256]{1,0:T(8,128)(2,1)S(1)} %constant_dynamic-update-slice_fusion.refs_0_), channel_id=1, source_target_pairs={{0,28},{4,0},{8,4},{12,8},{16,12},{20,16},{24,20},{28,24},{32,60},... | collective-permute-start | bytes 786440 | tf_op jit(solution)/shard_map/ppermute | solution.py:42
  18.0 5.0 %collective-permute-done.1.refs_2_ = bf16[512,256]{1,0:T(8,128)(2,1)S(1)} collective-permute-done((bf16[512,256]{1,0:T(8,128)(2,1)S(1)}, bf16[512,256]{1,0:T(8,128)(2,1)S(1)}, u32[]{:S(2)}, u32[]{:S(2)}) %collective-permute-start.1) | collective-permute-done | bytes 262176 | tf_op jit(solution)/shard_map/ppermute | solution.py:42
  23.0 3.7 %collective-permute-start.3 = (bf16[512,256]{1,0:T(8,128)(2,1)S(1)}, bf16[512,256]{1,0:T(8,128)(2,1)S(1)}, u32[]{:S(2)}, u32[]{:S(2)}) collective-permute-start(bf16[512,256]{1,0:T(8,128)(2,1)S(1)} %collective-permute-done.1.refs_2_), channel_id=1, source_target_pairs={{0,28},{4,0},{8,4},{12,8},{16,12},{20,16},{24,20},{28,24},{32,60},... | collective-permute-start | bytes 786440 | tf_op jit(solution)/shard_map/ppermute | solution.py:42
  26.7 4.1 %collective-permute-done.3.refs_4_ = bf16[512,256]{1,0:T(8,128)(2,1)S(1)} collective-permute-done((bf16[512,256]{1,0:T(8,128)(2,1)S(1)}, bf16[512,256]{1,0:T(8,128)(2,1)S(1)}, u32[]{:S(2)}, u32[]{:S(2)}) %collective-permute-start.3) | collective-permute-done | bytes 262176 | tf_op jit(solution)/shard_map/ppermute | solution.py:42
  30.7 3.7 %collective-permute-start.5 = (bf16[512,256]{1,0:T(8,128)(2,1)S(1)}, bf16[512,256]{1,0:T(8,128)(2,1)S(1)}, u32[]{:S(2)}, u32[]{:S(2)}) collective-permute-start(bf16[512,256]{1,0:T(8,128)(2,1)S(1)} %collective-permute-done.3.refs_4_), channel_id=1, source_target_pairs={{0,28},{4,0},{8,4},{12,8},{16,12},{20,16},{24,20},{28,24},{32,60},... | collective-permute-start | bytes 786440 | tf_op jit(solution)/shard_map/ppermute | solution.py:42
  34.5 0.9 prepare.1
  35.4 2.9 %collective-permute-done.5.refs_6_ = bf16[512,256]{1,0:T(8,128)(2,1)S(1)} collective-permute-done((bf16[512,256]{1,0:T(8,128)(2,1)S(1)}, bf16[512,256]{1,0:T(8,128)(2,1)S(1)}, u32[]{:S(2)}, u32[]{:S(2)}) %collective-permute-start.5) | collective-permute-done | bytes 262176 | tf_op jit(solution)/shard_map/ppermute | solution.py:42
  38.3 3.7 %collective-permute-done.6.refs_7_ = bf16[512,256]{1,0:T(8,128)(2,1)S(1)} collective-permute-done((bf16[512,256]{1,0:T(8,128)(2,1)S(1)}, bf16[512,256]{1,0:T(8,128)(2,1)S(1)}, u32[]{:S(2)}, u32[]{:S(2)}) %collective-permute-start.6) | collective-permute-done | bytes 262176 | tf_op jit(solution)/shard_map/ppermute | solution.py:39
  42.0 22.6 %attend.1 = bf16[8,304,256]{2,1,0:T(8,128)(2,1)S(1)} custom-call(bf16[2048,256]{1,0:T(8,128)(2,1)S(1)} %bitcast.5, bf16[8,32,256]{2,1,0:T(8,128)(2,1)S(1)} %get-tuple-element.10.piece_ref, f32[1,128]{1,0:T(1,128)S(1)} %get-tuple-element.11.count_ref, bf16[512,256]{1,0:T(8,128)(2,1)S(1)} %constant_dynamic-update-slice_fusion.refs_0_, ...), custom_call_target="tpu_custom_call" | custom-call | tf_op jit(solution)/shard_map/attend/pallas_call | solution.py:153
  64.6 0.0 copy-start.2
  64.6 21.5 %all_to_all.30.part_ref = bf16[8,304,256]{2,1,0:T(8,128)(2,1)S(1)} all-to-all(bf16[8,304,256]{2,1,0:T(8,128)(2,1)S(1)} %attend.1), channel_id=1, replica_groups={{0,32,64,96,128,160,192,224},{4,36,68,100,132,164,196,228},{8,40,72,104..., dimensions={0} | all-to-all | bytes 2490368 | tf_op jit(solution)/shard_map/all_to_all | solution.py:486
  86.1 1.5 merge.1
  87.6 15.8 %all_to_all.31.both_ref = bf16[8,80,256]{2,1,0:T(8,128)(2,1)S(1)} all-to-all(bf16[8,80,256]{2,1,0:T(8,128)(2,1)S(1)} %merge.1), channel_id=1, replica_groups={{0,4,8,12,16,20,24,28},{32,36,40,44,48,52,56,60},{64,68,72,76,80,84,88,..., dimensions={0} | all-to-all | bytes 655360 | tf_op jit(solution)/shard_map/all_to_all | solution.py:488
  103.4 0.1 broadcast_in_dim.15
  103.5 0.0 copy-start
  103.5 0.0 copy-start.3
  103.5 15.7 %all_to_all.32.every_ref = bf16[8,256,256]{2,1,0:T(8,128)(2,1)S(1)} all-to-all(bf16[8,256,256]{2,1,0:T(8,128)(2,1)S(1)} %broadcast_in_dim.15), channel_id=1, replica_groups={{0,32,64,96,128,160,192,224},{4,36,68,100,132,164,196,228},{8,40,72,104..., dimensions={0} | all-to-all | bytes 2097152 | tf_op jit(solution)/shard_map/all_to_all | solution.py:25
  119.2 8.3 %track_means.1 = (bf16[2048,256]{1,0:T(8,128)(2,1)S(1)}, bf16[16,2048]{1,0:T(8,128)(2,1)S(1)}, f32[2048,128]{1,0:T(8,128)S(1)}) custom-call(s32[128]{0:T(128)S(1)} %copy-done.3, s32[1]{0:T(128)} %bitcast.2.index_ref, bf16[8,256,256]{2,1,0:T(8,128)(2,1)S(1)} %all_to_all.32.every_ref, bf16[8,80,256]{2,1,0:T(8,128)(2,1)S(1)} %all_to_all.31.both_ref, ...), custom_call_target="tpu_custom_call" | custom-call | tf_op jit(solution)/shard_map/track_means/pallas_call | solution.py:322
  127.5 0.2 collective-permute-start.7
  127.7 1.2 collective-permute-done.7
  128.9 0.8 collective-permute-start.8
  129.7 3.6 %collective-permute-done.8.other_ref = bf16[16,2048]{1,0:T(8,128)(2,1)S(1)} collective-permute-done((bf16[16,2048]{1,0:T(8,128)(2,1)S(1)}, bf16[16,2048]{1,0:T(8,128)(2,1)S(1)}, u32[]{:S(2)}, u32[]{:S(2)}) %collective-permute-start.8) | collective-permute-done | bytes 65568 | tf_op jit(solution)/shard_map/ppermute | solution.py:497
  133.3 2.0 %error_messages.1 = bf16[8,32,256]{2,1,0:T(8,128)(2,1)S(1)} custom-call(s32[128]{0:T(128)S(1)} %copy-done.3, bf16[16,2048]{1,0:T(8,128)(2,1)S(1)} %add_convert_fusion.part_ref, bf16[16,2048]{1,0:T(8,128)(2,1)S(1)} %collective-permute-done.8.other_ref, bf16[8,80,256]{2,1,0:T(8,128)(2,1)S(1)} %all_to_all.31.both_ref, ...), custom_call_target="tpu_custom_call" | custom-call | tf_op jit(solution)/shard_map/error_messages/pallas_call | solution.py:398
  135.3 11.5 %all_to_all.33.in_ref = bf16[8,32,256]{2,1,0:T(8,128)(2,1)S(1)} all-to-all(bf16[8,32,256]{2,1,0:T(8,128)(2,1)S(1)} %error_messages.1), channel_id=1, replica_groups={{0,4,8,12,16,20,24,28},{32,36,40,44,48,52,56,60},{64,68,72,76,80,84,88,..., dimensions={0} | all-to-all | bytes 262144 | tf_op jit(solution)/shard_map/all_to_all | solution.py:499
  146.8 0.1 relay.1
  146.9 15.1 %all_to_all.34 = bf16[8,128,384]{2,1,0:T(8,128)(2,1)S(1)} all-to-all(bf16[8,128,384]{2,1,0:T(8,128)(2,1)S(1)} %relay.1), channel_id=1, replica_groups={{0,32,64,96,128,160,192,224},{4,36,68,100,132,164,196,228},{8,40,72,104..., dimensions={0} | all-to-all | bytes 1572864 | tf_op jit(solution)/shard_map/all_to_all | solution.py:500
  162.1 1.4 finish.1
  (18 shorter events, 0.1 us)
Async XLA Ops:
  2.5 15.5 %collective-permute-start = (bf16[512,256]{1,0:T(8,128)(2,1)S(1)}, bf16[512,256]{1,0:T(8,128)(2,1)S(1)}, u32[]{:S(2)}, u32[]{:S(2)}) collective-permute-start(bf16[512,256]{1,0:T(8,128)(2,1)S(1)} %constant_dynamic-update-slice_fusion.refs_0_), channel_id=1, source_target_pairs={{0,4},{4,8},{8,12},{12,16},{16,20},{20,24},{24,28},{28,0},{32,36},... | collective-permute-start | bytes 786440 | tf_op jit(solution)/shard_map/ppermute | solution.py:39
  6.4 28.0 %copy-start.1 = (bf16[4,16,1024]{2,1,0:T(8,128)(2,1)S(1)}, bf16[4,16,1024]{2,1,0:T(8,128)(2,1)}, u32[]{:S(2)}) copy-start(bf16[4,16,1024]{2,1,0:T(8,128)(2,1)} %param.14) | copy-start | bytes 393220
  6.4 28.0 %copy-start.4 = (s32[2,128]{1,0:T(2,128)S(1)}, s32[2,128]{1,0:T(2,128)}, u32[]{:S(2)}) copy-start(s32[2,128]{1,0:T(2,128)} %slot_ref.1) | copy-start | bytes 3076
  6.4 28.0 %copy-start.5 = (s32[2]{0:T(128)S(1)}, s32[2]{0:T(128)}, u32[]{:S(2)}) copy-start(s32[2]{0:T(128)} %row_count_ref.1) | copy-start | bytes 28
  6.4 31.9 %all-to-all-start = ((bf16[8,256,256]{2,1,0:T(8,128)(2,1)}), bf16[8,256,256]{2,1,0:T(8,128)(2,1)S(1)}, u32[]{:S(2)}, u32[]{:S(2)}) async-start(bf16[8,256,256]{2,1,0:T(8,128)(2,1)} %broadcast_in_dim.6), calls=%async_computation | async-start | bytes 2097152 | tf_op jit(solution)/shard_map/all_to_all | solution.py:25
  14.0 9.0 %collective-permute-start.1 = (bf16[512,256]{1,0:T(8,128)(2,1)S(1)}, bf16[512,256]{1,0:T(8,128)(2,1)S(1)}, u32[]{:S(2)}, u32[]{:S(2)}) collective-permute-start(bf16[512,256]{1,0:T(8,128)(2,1)S(1)} %constant_dynamic-update-slice_fusion.refs_0_), channel_id=1, source_target_pairs={{0,28},{4,0},{8,4},{12,8},{16,12},{20,16},{24,20},{28,24},{32,60},... | collective-permute-start | bytes 786440 | tf_op jit(solution)/shard_map/ppermute | solution.py:42
  18.0 8.7 %collective-permute-start.2 = (bf16[512,256]{1,0:T(8,128)(2,1)S(1)}, bf16[512,256]{1,0:T(8,128)(2,1)S(1)}, u32[]{:S(2)}, u32[]{:S(2)}) collective-permute-start(bf16[512,256]{1,0:T(8,128)(2,1)S(1)} %collective-permute-done.refs_1_), channel_id=1, source_target_pairs={{0,4},{4,8},{8,12},{12,16},{16,20},{20,24},{24,28},{28,0},{32,36},... | collective-permute-start | bytes 786440 | tf_op jit(solution)/shard_map/ppermute | solution.py:39
  23.0 7.8 %collective-permute-start.3 = (bf16[512,256]{1,0:T(8,128)(2,1)S(1)}, bf16[512,256]{1,0:T(8,128)(2,1)S(1)}, u32[]{:S(2)}, u32[]{:S(2)}) collective-permute-start(bf16[512,256]{1,0:T(8,128)(2,1)S(1)} %collective-permute-done.1.refs_2_), channel_id=1, source_target_pairs={{0,28},{4,0},{8,4},{12,8},{16,12},{20,16},{24,20},{28,24},{32,60},... | collective-permute-start | bytes 786440 | tf_op jit(solution)/shard_map/ppermute | solution.py:42
  26.7 7.8 %collective-permute-start.4 = (bf16[512,256]{1,0:T(8,128)(2,1)S(1)}, bf16[512,256]{1,0:T(8,128)(2,1)S(1)}, u32[]{:S(2)}, u32[]{:S(2)}) collective-permute-start(bf16[512,256]{1,0:T(8,128)(2,1)S(1)} %collective-permute-done.2.refs_3_), channel_id=1, source_target_pairs={{0,4},{4,8},{8,12},{12,16},{16,20},{20,24},{24,28},{28,0},{32,36},... | collective-permute-start | bytes 786440 | tf_op jit(solution)/shard_map/ppermute | solution.py:39
  30.7 7.6 %collective-permute-start.5 = (bf16[512,256]{1,0:T(8,128)(2,1)S(1)}, bf16[512,256]{1,0:T(8,128)(2,1)S(1)}, u32[]{:S(2)}, u32[]{:S(2)}) collective-permute-start(bf16[512,256]{1,0:T(8,128)(2,1)S(1)} %collective-permute-done.3.refs_4_), channel_id=1, source_target_pairs={{0,28},{4,0},{8,4},{12,8},{16,12},{20,16},{24,20},{28,24},{32,60},... | collective-permute-start | bytes 786440 | tf_op jit(solution)/shard_map/ppermute | solution.py:42
  34.4 7.6 %collective-permute-start.6 = (bf16[512,256]{1,0:T(8,128)(2,1)S(1)}, bf16[512,256]{1,0:T(8,128)(2,1)S(1)}, u32[]{:S(2)}, u32[]{:S(2)}) collective-permute-start(bf16[512,256]{1,0:T(8,128)(2,1)S(1)} %collective-permute-done.4.refs_5_), channel_id=1, source_target_pairs={{0,4},{4,8},{8,12},{12,16},{16,20},{20,24},{24,28},{28,0},{32,36},... | collective-permute-start | bytes 786440 | tf_op jit(solution)/shard_map/ppermute | solution.py:39
  64.6 21.5 %copy-start.2 = (bf16[256,256]{1,0:T(8,128)(2,1)S(1)}, bf16[256,256]{1,0:T(8,128)(2,1)}, u32[]{:S(2)}) copy-start(bf16[256,256]{1,0:T(8,128)(2,1)} %residual_ref.1) | copy-start | bytes 393220
  103.5 15.7 %copy-start = (bf16[256,1024]{1,0:T(8,128)(2,1)S(1)}, bf16[256,1024]{1,0:T(8,128)(2,1)}, u32[]{:S(2)}) copy-start(bf16[256,1024]{1,0:T(8,128)(2,1)} %weight_ref.3) | copy-start | bytes 1572868
  103.5 15.7 %copy-start.3 = (s32[128]{0:T(128)S(1)}, s32[128]{0:T(128)}, u32[]{:S(2)}) copy-start(s32[128]{0:T(128)} %track_ref.3) | copy-start | bytes 1540
  127.5 1.4 collective-permute-start.7
  128.9 4.4 %collective-permute-start.8 = (bf16[16,2048]{1,0:T(8,128)(2,1)S(1)}, bf16[16,2048]{1,0:T(8,128)(2,1)S(1)}, u32[]{:S(2)}, u32[]{:S(2)}) collective-permute-start(bf16[16,2048]{1,0:T(8,128)(2,1)S(1)} %add_convert_fusion.part_ref), channel_id=1, source_target_pairs={{0,2},{2,0},{1,3},{3,1},{4,6},{6,4},{5,7},{7,5},{8,10},{10,8},{9,1... | collective-permute-start | bytes 196616 | tf_op jit(solution)/shard_map/ppermute | solution.py:497

commit v7 on v6

--- a/solution.py
+++ b/solution.py
@@ -35,13 +35,14 @@
 
 def gather_ring(x, seq_count):
     pieces, up, down = [x], x, x
-    for i in range(SIDE // 2):
+    for _ in range(SIDE // 2 - 1):
         up = lax.ppermute(up, "seq", ring(seq_count, 1))
-        pieces.append(up)
-        if i + 1 < SIDE // 2:
-            down = lax.ppermute(down, "seq", ring(seq_count, -1))
-            pieces.append(down)
-    return pieces
+        down = lax.ppermute(down, "seq", ring(seq_count, -1))
+        pieces += [up, down]
+    half = x.shape[0] // 2
+    far_keys = lax.ppermute(up[:half], "seq", ring(seq_count, 1))
+    far_values = lax.ppermute(down[half:], "seq", ring(seq_count, -1))
+    return pieces + [far_keys, far_values]
 
 
 def prepare_kernel(row_count_ref, slot_ref, target_ref, carried_ref, sel_ref, count_ref):
@@ -102,11 +103,10 @@
     def _():
         zero = jnp.zeros((), jnp.bfloat16)
         one = jnp.ones((), jnp.bfloat16)
-        for i, kv_ref in enumerate(kv_refs):
-            n = kv_ref.shape[0] // 2
+        n = kv_refs[-1].shape[0]
+        pairs = [(ref[:n], ref[n:]) for ref in kv_refs[:-2]]
+        for i, (k, v) in enumerate(pairs + [(kv_refs[-2][...], kv_refs[-1][...])]):
             span = pl.ds(i * n, n)
-            k = kv_ref[:n]
-            v = kv_ref[n:]
             k_own[0, :, span] = jnp.where(first, k, zero).T
             k_own[1, :, span] = jnp.where(first, zero, k).T
             v_own[0, span] = jnp.where(first, v, one)
@@ -258,8 +258,8 @@
     id_buf,
     weight_buf,
 ):
-    step = mean_ref.shape[0]
-    at = pl.program_id(0)
+    step = every_ref.shape[1]
+    at = pl.program_id(0) * 2
 
     @pl.when(at == 0)
     def _():
@@ -284,9 +284,9 @@
                 ).astype(jnp.float32)
         weight_buf[...] = weight_ref[...].T
 
-    here = column(id_buf[pl.ds(at, 1)])
+    here = jnp.concatenate([column(id_buf[pl.ds(at + i, 1)]) for i in range(2)], axis=0)
     sums = jnp.zeros(mean_ref.shape, jnp.float32)
-    counts = jnp.zeros((step, step), jnp.float32)
+    counts = jnp.zeros((2 * step, step), jnp.float32)
     for g in range(SIDE):
         match = here == id_buf[g : g + 1]
         sums = sums + jnp.dot(
@@ -296,10 +296,12 @@
         )
         seen = count_buf[g : g + 1] + jnp.where(g < at, EARLIER, 0.0)
         counts = counts + jnp.where(match, seen, 0.0)
-    below = lax.broadcasted_iota(jnp.int32, (step, step), 1) < lax.broadcasted_iota(
-        jnp.int32, (step, step), 0
+    below = lax.broadcasted_iota(jnp.int32, (2 * step, step), 0) - lax.broadcasted_iota(
+        jnp.int32, (2 * step, step), 1
     )
-    counts = counts + jnp.where((here == id_buf[pl.ds(at, 1)]) & below, EARLIER, 0.0)
+    for i in range(2):
+        match = (here == id_buf[pl.ds(at + i, 1)]) & (below > i * step)
+        counts = counts + jnp.where(match, EARLIER, 0.0)
     total = jnp.sum(counts, axis=1, keepdims=True)
     before = jnp.floor(total * (1.0 / EARLIER))
     divisor = jnp.maximum(total - before * EARLIER, 1.0)
@@ -323,16 +325,16 @@
         track_kernel,
         grid_spec=pltpu.PrefetchScalarGridSpec(
             num_scalar_prefetch=2,
-            grid=(SIDE,),
+            grid=(SIDE // 2,),
             in_specs=[
                 pl.BlockSpec(every.shape, lambda i, t, at: (0, 0, 0)),
                 pl.BlockSpec(both.shape, lambda i, t, at: (0, 0, 0)),
                 pl.BlockSpec((width, 128), lambda i, t, at: (0, at[0] // (128 // chunk))),
             ],
             out_specs=[
-                pl.BlockSpec((step, width), lambda i, t, at: (i, 0)),
-                pl.BlockSpec((chunk, step), lambda i, t, at: (0, i)),
-                pl.BlockSpec((step, 128), lambda i, t, at: (i, 0)),
+                pl.BlockSpec((2 * step, width), lambda i, t, at: (i, 0)),
+                pl.BlockSpec((chunk, 2 * step), lambda i, t, at: (0, i)),
+                pl.BlockSpec((2 * step, 128), lambda i, t, at: (i, 0)),
             ],
             scratch_shapes=[
                 pltpu.VMEM((SIDE, step), jnp.float32),

time: 164 us -> 163 us (level)
  waiting for transfers between devices: 20.5 us -> 16.3 us
  starting transfers between devices: 21.9 us -> 24.1 us
    ppermute x3, waiting for transfers between devices: 12 us -> 0.01 us  [gather_ring(): down = lax.ppermute(down, 'seq', ring(seq_count, -1))]
    ppermute x4 -> x3, waiting for transfers between devices: 3.7 us -> 9.52 us  [gather_ring(): up = lax.ppermute(up, 'seq', ring(seq_count, 1))]
    ppermute x0 -> x2, starting transfers between devices: none -> 3.24 us  [the longest x1 3.23 us: gather_ring(): far_values = lax.ppermute(down[half:], 'seq', ring(seq_count, -1))]
    ppermute x0 -> x2, waiting for transfers between devices: none -> 1.9 us  [the longest x1 1.55 us: gather_ring(): far_keys = lax.ppermute(up[:half], 'seq', ring(seq_count, 1))]
  transfers between devices with their start and end apart: 10 -> 11, of which waited for: 6 -> 6; matrix products, arithmetic and copies ran while one was open for 1% -> 2% of each run, Pallas kernels for 1% -> 1%
where the time goes in v7:
time: 163 us; the launch traced here: 162 us
  blocking collectives  80.3 us (49%)
  Pallas kernels  35.6 us (22%)
  starting transfers between devices  24.1 us (15%)
  waiting for transfers between devices  16.3 us (10%)
  local copies, waits for them, and re-layouts  5.22 us (3%)
    pallas_call x1, Pallas kernels, attend(): pl.pallas_call(attend_kernel, grid=(pairs, SIDE // 2), in_specs=[pl.Block...  22.7 us
    all_to_all x1, blocking collectives, local(): part = lax.all_to_all(part, 'seq', 0, 0, axis_index_groups=GROUP_YX)  21.3 us
    all_to_all x1, blocking collectives, local(): both = lax.all_to_all(both, 'seq', 0, 0, axis_index_groups=GROUP_Z)  16.7 us
    all_to_all x1, blocking collectives, spread(): return lax.all_to_all(wide, 'seq', 0, 0, axis_index_groups=groups)  15.7 us
    all_to_all x1, blocking collectives, local(): lax.all_to_all(relay(final), 'seq', 0, 0, axis_index_groups=GROUP_YX)  15.1 us
    all_to_all x1, blocking collectives, local(): final = lax.all_to_all(final, 'seq', 0, 0, axis_index_groups=GROUP_Z)  11.5 us
    ppermute x3, starting transfers between devices, gather_ring(): down = lax.ppermute(down, 'seq', ring(seq_count, -1))  10.5 us
    ppermute x3, waiting for transfers between devices, gather_ring(): up = lax.ppermute(up, 'seq', ring(seq_count, 1))  9.52 us
  transfers between devices with their start and end apart: 11, of which 6 were waited for; matrix products, arithmetic and copies ran while one was open for 2% of the time, Pallas kernels for 1%

profile of v7, /device:TPU:2, one launch (start us, length us, event | category | flops | bytes accessed | tf_op | source)
XLA Modules:
  0.0 162.2 jit_solution(12249779892875071915)
XLA Ops:
  0.6 0.9 constant_dynamic-update-slice_fusion.1
  1.5 0.9 constant_dynamic-update-slice_fusion.refs_0_
  2.5 2.0 %collective-permute-start = (bf16[512,256]{1,0:T(8,128)(2,1)S(1)}, bf16[512,256]{1,0:T(8,128)(2,1)S(1)}, u32[]{:S(2)}, u32[]{:S(2)}) collective-permute-start(bf16[512,256]{1,0:T(8,128)(2,1)S(1)} %constant_dynamic-update-slice_fusion.refs_0_), channel_id=1, source_target_pairs={{0,4},{4,8},{8,12},{12,16},{16,20},{20,24},{24,28},{28,0},{32,36},... | collective-permute-start | bytes 786440 | tf_op jit(solution)/shard_map/ppermute | solution.py:39
  4.5 4.0 %collective-permute-start.1 = (bf16[512,256]{1,0:T(8,128)(2,1)S(1)}, bf16[512,256]{1,0:T(8,128)(2,1)S(1)}, u32[]{:S(2)}, u32[]{:S(2)}) collective-permute-start(bf16[512,256]{1,0:T(8,128)(2,1)S(1)} %constant_dynamic-update-slice_fusion.refs_0_), channel_id=1, source_target_pairs={{0,28},{4,0},{8,4},{12,8},{16,12},{20,16},{24,20},{28,24},{32,60},... | collective-permute-start | bytes 786440 | tf_op jit(solution)/shard_map/ppermute | solution.py:40
  8.5 1.9 %broadcast_in_dim.6 = bf16[8,256,256]{2,1,0:T(8,128)(2,1)} broadcast(bf16[256,256]{1,0:T(8,128)(2,1)} %param.9), dimensions={1,2} | broadcast | bytes 1179648 | tf_op jit(solution)/shard_map/broadcast_in_dim | solution.py:24
  10.4 7.6 %all-to-all-start = ((bf16[8,256,256]{2,1,0:T(8,128)(2,1)}), bf16[8,256,256]{2,1,0:T(8,128)(2,1)S(1)}, u32[]{:S(2)}, u32[]{:S(2)}) async-start(bf16[8,256,256]{2,1,0:T(8,128)(2,1)} %broadcast_in_dim.6), calls=%async_computation | async-start | bytes 2097152 | tf_op jit(solution)/shard_map/all_to_all | solution.py:25
  18.1 3.2 %collective-permute-start.3 = (bf16[512,256]{1,0:T(8,128)(2,1)S(1)}, bf16[512,256]{1,0:T(8,128)(2,1)S(1)}, u32[]{:S(2)}, u32[]{:S(2)}) collective-permute-start(bf16[512,256]{1,0:T(8,128)(2,1)S(1)} %collective-permute-done.1.refs_2_), channel_id=1, source_target_pairs={{0,28},{4,0},{8,4},{12,8},{16,12},{20,16},{24,20},{28,24},{32,60},... | collective-permute-start | bytes 786440 | tf_op jit(solution)/shard_map/ppermute | solution.py:40
  21.3 5.2 %collective-permute-done.2.refs_3_ = bf16[512,256]{1,0:T(8,128)(2,1)S(1)} collective-permute-done((bf16[512,256]{1,0:T(8,128)(2,1)S(1)}, bf16[512,256]{1,0:T(8,128)(2,1)S(1)}, u32[]{:S(2)}, u32[]{:S(2)}) %collective-permute-start.2) | collective-permute-done | bytes 262176 | tf_op jit(solution)/shard_map/ppermute | solution.py:39
  26.5 3.2 %collective-permute-start.5 = (bf16[512,256]{1,0:T(8,128)(2,1)S(1)}, bf16[512,256]{1,0:T(8,128)(2,1)S(1)}, u32[]{:S(2)}, u32[]{:S(2)}) collective-permute-start(bf16[512,256]{1,0:T(8,128)(2,1)S(1)} %collective-permute-done.3.refs_4_), channel_id=1, source_target_pairs={{0,28},{4,0},{8,4},{12,8},{16,12},{20,16},{24,20},{28,24},{32,60},... | collective-permute-start | bytes 786440 | tf_op jit(solution)/shard_map/ppermute | solution.py:40
  29.7 4.3 %collective-permute-done.4.refs_5_ = bf16[512,256]{1,0:T(8,128)(2,1)S(1)} collective-permute-done((bf16[512,256]{1,0:T(8,128)(2,1)S(1)}, bf16[512,256]{1,0:T(8,128)(2,1)S(1)}, u32[]{:S(2)}, u32[]{:S(2)}) %collective-permute-start.4) | collective-permute-done | bytes 262176 | tf_op jit(solution)/shard_map/ppermute | solution.py:39
  34.0 0.7 slice.12
  34.7 0.7 slice.13
  35.4 3.2 %collective-permute-start.7 = (bf16[256,256]{1,0:T(8,128)(2,1)}, bf16[256,256]{1,0:T(8,128)(2,1)S(1)}, u32[]{:S(2)}, u32[]{:S(2)}) collective-permute-start(bf16[256,256]{1,0:T(8,128)(2,1)} %slice.13), channel_id=1, source_target_pairs={{0,28},{4,0},{8,4},{12,8},{16,12},{20,16},{24,20},{28,24},{32,60},... | collective-permute-start | bytes 393224 | tf_op jit(solution)/shard_map/ppermute | solution.py:44
  38.6 0.9 prepare.1
  39.5 1.5 collective-permute-done.6.refs_7_
  41.1 0.4 collective-permute-done.7.refs_8_
  41.5 22.7 %attend.1 = bf16[8,304,256]{2,1,0:T(8,128)(2,1)S(1)} custom-call(bf16[2048,256]{1,0:T(8,128)(2,1)S(1)} %bitcast.5, bf16[8,32,256]{2,1,0:T(8,128)(2,1)S(1)} %get-tuple-element.10.piece_ref, f32[1,128]{1,0:T(1,128)S(1)} %get-tuple-element.11.count_ref, bf16[512,256]{1,0:T(8,128)(2,1)S(1)} %constant_dynamic-update-slice_fusion.refs_0_, ...), custom_call_target="tpu_custom_call" | custom-call | tf_op jit(solution)/shard_map/attend/pallas_call | solution.py:153
  64.2 21.3 %all_to_all.30.part_ref = bf16[8,304,256]{2,1,0:T(8,128)(2,1)S(1)} all-to-all(bf16[8,304,256]{2,1,0:T(8,128)(2,1)S(1)} %attend.1), channel_id=1, replica_groups={{0,32,64,96,128,160,192,224},{4,36,68,100,132,164,196,228},{8,40,72,104..., dimensions={0} | all-to-all | bytes 2490368 | tf_op jit(solution)/shard_map/all_to_all | solution.py:488
  85.5 1.5 merge.1
  87.0 16.7 %all_to_all.31.both_ref = bf16[8,80,256]{2,1,0:T(8,128)(2,1)S(1)} all-to-all(bf16[8,80,256]{2,1,0:T(8,128)(2,1)S(1)} %merge.1), channel_id=1, replica_groups={{0,4,8,12,16,20,24,28},{32,36,40,44,48,52,56,60},{64,68,72,76,80,84,88,..., dimensions={0} | all-to-all | bytes 655360 | tf_op jit(solution)/shard_map/all_to_all | solution.py:490
  103.7 0.1 broadcast_in_dim.15
  103.8 15.7 %all_to_all.32.every_ref = bf16[8,256,256]{2,1,0:T(8,128)(2,1)S(1)} all-to-all(bf16[8,256,256]{2,1,0:T(8,128)(2,1)S(1)} %broadcast_in_dim.15), channel_id=1, replica_groups={{0,32,64,96,128,160,192,224},{4,36,68,100,132,164,196,228},{8,40,72,104..., dimensions={0} | all-to-all | bytes 2097152 | tf_op jit(solution)/shard_map/all_to_all | solution.py:25
  119.5 6.9 %track_means.1 = (bf16[2048,256]{1,0:T(8,128)(2,1)S(1)}, bf16[16,2048]{1,0:T(8,128)(2,1)S(1)}, f32[2048,128]{1,0:T(8,128)S(1)}) custom-call(s32[128]{0:T(128)S(1)} %copy-done.3, s32[1]{0:T(128)} %bitcast.2.index_ref, bf16[8,256,256]{2,1,0:T(8,128)(2,1)S(1)} %all_to_all.32.every_ref, bf16[8,80,256]{2,1,0:T(8,128)(2,1)S(1)} %all_to_all.31.both_ref, ...), custom_call_target="tpu_custom_call" | custom-call | tf_op jit(solution)/shard_map/track_means/pallas_call | solution.py:324
  126.4 0.1 collective-permute-start.8
  126.4 1.2 collective-permute-done.8
  127.7 0.8 collective-permute-start.9
  128.5 3.6 %collective-permute-done.9.other_ref = bf16[16,2048]{1,0:T(8,128)(2,1)S(1)} collective-permute-done((bf16[16,2048]{1,0:T(8,128)(2,1)S(1)}, bf16[16,2048]{1,0:T(8,128)(2,1)S(1)}, u32[]{:S(2)}, u32[]{:S(2)}) %collective-permute-start.9) | collective-permute-done | bytes 65568 | tf_op jit(solution)/shard_map/ppermute | solution.py:499
  132.1 2.0 %error_messages.1 = bf16[8,32,256]{2,1,0:T(8,128)(2,1)S(1)} custom-call(s32[128]{0:T(128)S(1)} %copy-done.3, bf16[16,2048]{1,0:T(8,128)(2,1)S(1)} %add_convert_fusion.part_ref, bf16[16,2048]{1,0:T(8,128)(2,1)S(1)} %collective-permute-done.9.other_ref, bf16[8,80,256]{2,1,0:T(8,128)(2,1)S(1)} %all_to_all.31.both_ref, ...), custom_call_target="tpu_custom_call" | custom-call | tf_op jit(solution)/shard_map/error_messages/pallas_call | solution.py:400
  134.1 11.5 %all_to_all.33.in_ref = bf16[8,32,256]{2,1,0:T(8,128)(2,1)S(1)} all-to-all(bf16[8,32,256]{2,1,0:T(8,128)(2,1)S(1)} %error_messages.1), channel_id=1, replica_groups={{0,4,8,12,16,20,24,28},{32,36,40,44,48,52,56,60},{64,68,72,76,80,84,88,..., dimensions={0} | all-to-all | bytes 262144 | tf_op jit(solution)/shard_map/all_to_all | solution.py:501
  145.6 0.1 relay.1
  145.7 15.1 %all_to_all.34 = bf16[8,128,384]{2,1,0:T(8,128)(2,1)S(1)} all-to-all(bf16[8,128,384]{2,1,0:T(8,128)(2,1)S(1)} %relay.1), channel_id=1, replica_groups={{0,32,64,96,128,160,192,224},{4,36,68,100,132,164,196,228},{8,40,72,104..., dimensions={0} | all-to-all | bytes 1572864 | tf_op jit(solution)/shard_map/all_to_all | solution.py:502
  160.9 1.4 finish.1
  (22 shorter events, 0.1 us)
Async XLA Ops:
  2.5 15.6 %collective-permute-start = (bf16[512,256]{1,0:T(8,128)(2,1)S(1)}, bf16[512,256]{1,0:T(8,128)(2,1)S(1)}, u32[]{:S(2)}, u32[]{:S(2)}) collective-permute-start(bf16[512,256]{1,0:T(8,128)(2,1)S(1)} %constant_dynamic-update-slice_fusion.refs_0_), channel_id=1, source_target_pairs={{0,4},{4,8},{8,12},{12,16},{16,20},{20,24},{24,28},{28,0},{32,36},... | collective-permute-start | bytes 786440 | tf_op jit(solution)/shard_map/ppermute | solution.py:39
  4.5 13.6 %collective-permute-start.1 = (bf16[512,256]{1,0:T(8,128)(2,1)S(1)}, bf16[512,256]{1,0:T(8,128)(2,1)S(1)}, u32[]{:S(2)}, u32[]{:S(2)}) collective-permute-start(bf16[512,256]{1,0:T(8,128)(2,1)S(1)} %constant_dynamic-update-slice_fusion.refs_0_), channel_id=1, source_target_pairs={{0,28},{4,0},{8,4},{12,8},{16,12},{20,16},{24,20},{28,24},{32,60},... | collective-permute-start | bytes 786440 | tf_op jit(solution)/shard_map/ppermute | solution.py:40
  10.4 28.2 %copy-start.1 = (bf16[4,16,1024]{2,1,0:T(8,128)(2,1)S(1)}, bf16[4,16,1024]{2,1,0:T(8,128)(2,1)}, u32[]{:S(2)}) copy-start(bf16[4,16,1024]{2,1,0:T(8,128)(2,1)} %param.14) | copy-start | bytes 393220
  10.4 28.2 %copy-start.4 = (s32[2,128]{1,0:T(2,128)S(1)}, s32[2,128]{1,0:T(2,128)}, u32[]{:S(2)}) copy-start(s32[2,128]{1,0:T(2,128)} %slot_ref.1) | copy-start | bytes 3076
  10.4 28.2 %copy-start.5 = (s32[2]{0:T(128)S(1)}, s32[2]{0:T(128)}, u32[]{:S(2)}) copy-start(s32[2]{0:T(128)} %row_count_ref.1) | copy-start | bytes 28
  10.4 31.0 %all-to-all-start = ((bf16[8,256,256]{2,1,0:T(8,128)(2,1)}), bf16[8,256,256]{2,1,0:T(8,128)(2,1)S(1)}, u32[]{:S(2)}, u32[]{:S(2)}) async-start(bf16[8,256,256]{2,1,0:T(8,128)(2,1)} %broadcast_in_dim.6), calls=%async_computation | async-start | bytes 2097152 | tf_op jit(solution)/shard_map/all_to_all | solution.py:25
  18.0 8.4 %collective-permute-start.2 = (bf16[512,256]{1,0:T(8,128)(2,1)S(1)}, bf16[512,256]{1,0:T(8,128)(2,1)S(1)}, u32[]{:S(2)}, u32[]{:S(2)}) collective-permute-start(bf16[512,256]{1,0:T(8,128)(2,1)S(1)} %collective-permute-done.refs_1_), channel_id=1, source_target_pairs={{0,4},{4,8},{8,12},{12,16},{16,20},{20,24},{24,28},{28,0},{32,36},... | collective-permute-start | bytes 786440 | tf_op jit(solution)/shard_map/ppermute | solution.py:39
  18.1 8.4 %collective-permute-start.3 = (bf16[512,256]{1,0:T(8,128)(2,1)S(1)}, bf16[512,256]{1,0:T(8,128)(2,1)S(1)}, u32[]{:S(2)}, u32[]{:S(2)}) collective-permute-start(bf16[512,256]{1,0:T(8,128)(2,1)S(1)} %collective-permute-done.1.refs_2_), channel_id=1, source_target_pairs={{0,28},{4,0},{8,4},{12,8},{16,12},{20,16},{24,20},{28,24},{32,60},... | collective-permute-start | bytes 786440 | tf_op jit(solution)/shard_map/ppermute | solution.py:40
  26.5 7.6 %collective-permute-start.4 = (bf16[512,256]{1,0:T(8,128)(2,1)S(1)}, bf16[512,256]{1,0:T(8,128)(2,1)S(1)}, u32[]{:S(2)}, u32[]{:S(2)}) collective-permute-start(bf16[512,256]{1,0:T(8,128)(2,1)S(1)} %collective-permute-done.2.refs_3_), channel_id=1, source_target_pairs={{0,4},{4,8},{8,12},{12,16},{16,20},{20,24},{24,28},{28,0},{32,36},... | collective-permute-start | bytes 786440 | tf_op jit(solution)/shard_map/ppermute | solution.py:39
  26.5 8.2 %collective-permute-start.5 = (bf16[512,256]{1,0:T(8,128)(2,1)S(1)}, bf16[512,256]{1,0:T(8,128)(2,1)S(1)}, u32[]{:S(2)}, u32[]{:S(2)}) collective-permute-start(bf16[512,256]{1,0:T(8,128)(2,1)S(1)} %collective-permute-done.3.refs_4_), channel_id=1, source_target_pairs={{0,28},{4,0},{8,4},{12,8},{16,12},{20,16},{24,20},{28,24},{32,60},... | collective-permute-start | bytes 786440 | tf_op jit(solution)/shard_map/ppermute | solution.py:40
  34.7 6.4 %collective-permute-start.6 = (bf16[256,256]{1,0:T(8,128)(2,1)}, bf16[256,256]{1,0:T(8,128)(2,1)S(1)}, u32[]{:S(2)}, u32[]{:S(2)}) collective-permute-start(bf16[256,256]{1,0:T(8,128)(2,1)} %slice.12), channel_id=1, source_target_pairs={{0,4},{4,8},{8,12},{12,16},{16,20},{20,24},{24,28},{28,0},{32,36},... | collective-permute-start | bytes 393224 | tf_op jit(solution)/shard_map/ppermute | solution.py:43
  35.4 6.1 %collective-permute-start.7 = (bf16[256,256]{1,0:T(8,128)(2,1)}, bf16[256,256]{1,0:T(8,128)(2,1)S(1)}, u32[]{:S(2)}, u32[]{:S(2)}) collective-permute-start(bf16[256,256]{1,0:T(8,128)(2,1)} %slice.13), channel_id=1, source_target_pairs={{0,28},{4,0},{8,4},{12,8},{16,12},{20,16},{24,20},{28,24},{32,60},... | collective-permute-start | bytes 393224 | tf_op jit(solution)/shard_map/ppermute | solution.py:44
  64.2 21.3 %copy-start.2 = (bf16[256,256]{1,0:T(8,128)(2,1)S(1)}, bf16[256,256]{1,0:T(8,128)(2,1)}, u32[]{:S(2)}) copy-start(bf16[256,256]{1,0:T(8,128)(2,1)} %residual_ref.1) | copy-start | bytes 393220
  103.8 15.7 %copy-start = (bf16[256,1024]{1,0:T(8,128)(2,1)S(1)}, bf16[256,1024]{1,0:T(8,128)(2,1)}, u32[]{:S(2)}) copy-start(bf16[256,1024]{1,0:T(8,128)(2,1)} %weight_ref.3) | copy-start | bytes 1572868
  103.8 15.7 %copy-start.3 = (s32[128]{0:T(128)S(1)}, s32[128]{0:T(128)}, u32[]{:S(2)}) copy-start(s32[128]{0:T(128)} %track_ref.3) | copy-start | bytes 1540
  126.4 1.3 collective-permute-start.8
  127.7 4.4 %collective-permute-start.9 = (bf16[16,2048]{1,0:T(8,128)(2,1)S(1)}, bf16[16,2048]{1,0:T(8,128)(2,1)S(1)}, u32[]{:S(2)}, u32[]{:S(2)}) collective-permute-start(bf16[16,2048]{1,0:T(8,128)(2,1)S(1)} %add_convert_fusion.part_ref), channel_id=1, source_target_pairs={{0,2},{2,0},{1,3},{3,1},{4,6},{6,4},{5,7},{7,5},{8,10},{10,8},{9,1... | collective-permute-start | bytes 196616 | tf_op jit(solution)/shard_map/ppermute | solution.py:499

commit v8 on v7

--- a/solution.py
+++ b/solution.py
@@ -43,6 +43,37 @@
     far_keys = lax.ppermute(up[:half], "seq", ring(seq_count, 1))
     far_values = lax.ppermute(down[half:], "seq", ring(seq_count, -1))
     return pieces + [far_keys, far_values]
+
+
+def lay_out_kernel(k_ref, v_ref, q_ref, kv_ref, wide_ref, sems):
+    n = k_ref.shape[0]
+    copies = [
+        pltpu.make_async_copy(k_ref, kv_ref.at[pl.ds(0, n)], sems.at[0]),
+        pltpu.make_async_copy(v_ref, kv_ref.at[pl.ds(n, n)], sems.at[1]),
+    ]
+    for i in range(SIDE):
+        copies.append(pltpu.make_async_copy(q_ref, wide_ref.at[i], sems.at[2 + i]))
+    for copy in copies:
+        copy.start()
+    for copy in copies:
+        copy.wait()
+
+
+def lay_out(keys, values, queries):
+    n, width = keys.shape
+    anywhere = pl.BlockSpec(memory_space=pl.ANY)
+    return pl.pallas_call(
+        lay_out_kernel,
+        in_specs=[anywhere] * 3,
+        out_specs=[anywhere] * 2,
+        out_shape=[
+            jax.ShapeDtypeStruct((2 * n, width), keys.dtype),
+            jax.ShapeDtypeStruct((SIDE, n, width), queries.dtype),
+        ],
+        scratch_shapes=[pltpu.SemaphoreType.DMA((2 + SIDE,))],
+        compiler_params=pltpu.CompilerParams(vmem_limit_bytes=60 * 1024 * 1024),
+        name="lay_out",
+    )(keys, values, queries)
 
 
 def prepare_kernel(row_count_ref, slot_ref, target_ref, carried_ref, sel_ref, count_ref):
@@ -477,8 +508,10 @@
     index = lax.axis_index("seq").astype(jnp.int32).reshape(1)
     owned, pool, target_d = targets.shape
 
-    pieces = gather_ring(jnp.concatenate([keys, values], axis=0), seq_count)
-    query_all = spread(queries, GROUP_YX).reshape(SIDE * tok_rows, width)
+    own_kv, wide = lay_out(keys, values, queries)
+    pieces = gather_ring(own_kv, seq_count)
+    query_all = lax.all_to_all(wide, "seq", 0, 0, axis_index_groups=GROUP_YX)
+    query_all = query_all.reshape(SIDE * tok_rows, width)
     carried, selector, slot_rows = prepare(
         row_count, pool_slot, targets.reshape(owned * pool, target_d)
     )

time: 163 us -> 200 us (1.23)
  Pallas kernels: 35.6 us -> 76.5 us
  local copies, waits for them, and re-layouts: 5.22 us -> 1.44 us
    pallas_call x0 -> x1, Pallas kernels: none -> 40.9 us  [lay_out(): pl.pallas_call(lay_out_kernel, in_specs=[anywhere] * 3, out_specs=[anywhe...]
  transfers between devices with their start and end apart: 11 -> 11, of which waited for: 6 -> 6; matrix products, arithmetic and copies ran while one was open for 2% -> 1% of each run, Pallas kernels for 1% -> 0%
where the time goes in v8:
time: 200 us; the launch traced here: 199 us
  blocking collectives  80.3 us (40%)
  Pallas kernels  76.5 us (38%)
  starting transfers between devices  24.1 us (12%)
  waiting for transfers between devices  16.3 us (8%)
    pallas_call x1, Pallas kernels, lay_out(): pl.pallas_call(lay_out_kernel, in_specs=[anywhere] * 3, out_specs=[anywhe...  40.9 us
    pallas_call x1, Pallas kernels, attend(): pl.pallas_call(attend_kernel, grid=(pairs, SIDE // 2), in_specs=[pl.Block...  22.7 us
    all_to_all x1, blocking collectives, local(): part = lax.all_to_all(part, 'seq', 0, 0, axis_index_groups=GROUP_YX)  21.3 us
    all_to_all x1, blocking collectives, local(): both = lax.all_to_all(both, 'seq', 0, 0, axis_index_groups=GROUP_Z)  16.7 us
    all_to_all x1, blocking collectives, spread(): return lax.all_to_all(wide, 'seq', 0, 0, axis_index_groups=groups)  15.7 us
    all_to_all x1, blocking collectives, local(): lax.all_to_all(relay(final), 'seq', 0, 0, axis_index_groups=GROUP_YX)  15.1 us
    all_to_all x1, blocking collectives, local(): final = lax.all_to_all(final, 'seq', 0, 0, axis_index_groups=GROUP_Z)  11.5 us
    ppermute x3, starting transfers between devices, gather_ring(): down = lax.ppermute(down, 'seq', ring(seq_count, -1))  10.5 us
  transfers between devices with their start and end apart: 11, of which 6 were waited for; matrix products, arithmetic and copies ran while one was open for 1% of the time, Pallas kernels for 0%

profile of v8, /device:TPU:2, one launch (start us, length us, event | category | flops | bytes accessed | tf_op | source)
XLA Modules:
  0.0 199.4 jit_solution(1215887930087262349)
XLA Ops:
  0.6 40.9 %lay_out.1 = (bf16[512,256]{1,0:T(8,128)(2,1)}, bf16[8,256,256]{2,1,0:T(8,128)(2,1)}) custom-call(bf16[256,256]{1,0:T(8,128)(2,1)} %k_ref.1, bf16[256,256]{1,0:T(8,128)(2,1)} %v_ref.1, bf16[256,256]{1,0:T(8,128)(2,1)} %q_ref.1), custom_call_target="tpu_custom_call" | custom-call | tf_op jit(solution)/shard_map/lay_out/pallas_call | solution.py:65
  41.5 2.0 %collective-permute-start = (bf16[512,256]{1,0:T(8,128)(2,1)}, bf16[512,256]{1,0:T(8,128)(2,1)S(1)}, u32[]{:S(2)}, u32[]{:S(2)}) collective-permute-start(bf16[512,256]{1,0:T(8,128)(2,1)} %get-tuple-element.15.refs_0_), channel_id=1, source_target_pairs={{0,4},{4,8},{8,12},{12,16},{16,20},{20,24},{24,28},{28,0},{32,36},... | collective-permute-start | bytes 786440 | tf_op jit(solution)/shard_map/ppermute | solution.py:39
  43.5 4.0 %collective-permute-start.1 = (bf16[512,256]{1,0:T(8,128)(2,1)}, bf16[512,256]{1,0:T(8,128)(2,1)S(1)}, u32[]{:S(2)}, u32[]{:S(2)}) collective-permute-start(bf16[512,256]{1,0:T(8,128)(2,1)} %get-tuple-element.15.refs_0_), channel_id=1, source_target_pairs={{0,28},{4,0},{8,4},{12,8},{16,12},{20,16},{24,20},{28,24},{32,60},... | collective-permute-start | bytes 786440 | tf_op jit(solution)/shard_map/ppermute | solution.py:40
  47.6 7.6 %all-to-all-start = ((bf16[8,256,256]{2,1,0:T(8,128)(2,1)}), bf16[8,256,256]{2,1,0:T(8,128)(2,1)S(1)}, u32[]{:S(2)}, u32[]{:S(2)}) async-start(bf16[8,256,256]{2,1,0:T(8,128)(2,1)} %get-tuple-element.12), calls=%async_computation | async-start | bytes 2097152 | tf_op jit(solution)/shard_map/all_to_all | solution.py:513
  55.2 3.2 %collective-permute-start.3 = (bf16[512,256]{1,0:T(8,128)(2,1)S(1)}, bf16[512,256]{1,0:T(8,128)(2,1)S(1)}, u32[]{:S(2)}, u32[]{:S(2)}) collective-permute-start(bf16[512,256]{1,0:T(8,128)(2,1)S(1)} %collective-permute-done.1.refs_2_), channel_id=1, source_target_pairs={{0,28},{4,0},{8,4},{12,8},{16,12},{20,16},{24,20},{28,24},{32,60},... | collective-permute-start | bytes 786440 | tf_op jit(solution)/shard_map/ppermute | solution.py:40
  58.4 5.2 %collective-permute-done.2.refs_3_ = bf16[512,256]{1,0:T(8,128)(2,1)S(1)} collective-permute-done((bf16[512,256]{1,0:T(8,128)(2,1)S(1)}, bf16[512,256]{1,0:T(8,128)(2,1)S(1)}, u32[]{:S(2)}, u32[]{:S(2)}) %collective-permute-start.2) | collective-permute-done | bytes 262176 | tf_op jit(solution)/shard_map/ppermute | solution.py:39
  63.6 3.2 %collective-permute-start.5 = (bf16[512,256]{1,0:T(8,128)(2,1)S(1)}, bf16[512,256]{1,0:T(8,128)(2,1)S(1)}, u32[]{:S(2)}, u32[]{:S(2)}) collective-permute-start(bf16[512,256]{1,0:T(8,128)(2,1)S(1)} %collective-permute-done.3.refs_4_), channel_id=1, source_target_pairs={{0,28},{4,0},{8,4},{12,8},{16,12},{20,16},{24,20},{28,24},{32,60},... | collective-permute-start | bytes 786440 | tf_op jit(solution)/shard_map/ppermute | solution.py:40
  66.8 4.3 %collective-permute-done.4.refs_5_ = bf16[512,256]{1,0:T(8,128)(2,1)S(1)} collective-permute-done((bf16[512,256]{1,0:T(8,128)(2,1)S(1)}, bf16[512,256]{1,0:T(8,128)(2,1)S(1)}, u32[]{:S(2)}, u32[]{:S(2)}) %collective-permute-start.4) | collective-permute-done | bytes 262176 | tf_op jit(solution)/shard_map/ppermute | solution.py:39
  71.2 0.7 slice.12
  71.8 0.7 slice.13
  72.5 3.2 %collective-permute-start.7 = (bf16[256,256]{1,0:T(8,128)(2,1)}, bf16[256,256]{1,0:T(8,128)(2,1)S(1)}, u32[]{:S(2)}, u32[]{:S(2)}) collective-permute-start(bf16[256,256]{1,0:T(8,128)(2,1)} %slice.13), channel_id=1, source_target_pairs={{0,28},{4,0},{8,4},{12,8},{16,12},{20,16},{24,20},{28,24},{32,60},... | collective-permute-start | bytes 393224 | tf_op jit(solution)/shard_map/ppermute | solution.py:44
  75.7 0.9 prepare.1
  76.7 1.6 collective-permute-done.6.refs_7_
  78.2 0.3 collective-permute-done.7.refs_8_
  78.6 22.7 %attend.1 = bf16[8,304,256]{2,1,0:T(8,128)(2,1)S(1)} custom-call(bf16[2048,256]{1,0:T(8,128)(2,1)S(1)} %bitcast.5, bf16[8,32,256]{2,1,0:T(8,128)(2,1)S(1)} %get-tuple-element.13.piece_ref, f32[1,128]{1,0:T(1,128)S(1)} %get-tuple-element.14.count_ref, bf16[512,256]{1,0:T(8,128)(2,1)S(1)} %copy-done.1, bf16[512,256]{1,0:T(8,128)(2,1)S(1)} %collective-permute-done.refs_1_, ...), custom_call_target="tpu_custom_call" | custom-call | tf_op jit(solution)/shard_map/attend/pallas_call | solution.py:184
  101.3 0.0 copy-start.3
  101.3 21.3 %all_to_all.30.part_ref = bf16[8,304,256]{2,1,0:T(8,128)(2,1)S(1)} all-to-all(bf16[8,304,256]{2,1,0:T(8,128)(2,1)S(1)} %attend.1), channel_id=1, replica_groups={{0,32,64,96,128,160,192,224},{4,36,68,100,132,164,196,228},{8,40,72,104..., dimensions={0} | all-to-all | bytes 2490368 | tf_op jit(solution)/shard_map/all_to_all | solution.py:521
  122.6 1.5 merge.1
  124.2 16.7 %all_to_all.31.both_ref = bf16[8,80,256]{2,1,0:T(8,128)(2,1)S(1)} all-to-all(bf16[8,80,256]{2,1,0:T(8,128)(2,1)S(1)} %merge.1), channel_id=1, replica_groups={{0,4,8,12,16,20,24,28},{32,36,40,44,48,52,56,60},{64,68,72,76,80,84,88,..., dimensions={0} | all-to-all | bytes 655360 | tf_op jit(solution)/shard_map/all_to_all | solution.py:523
  140.9 0.1 broadcast_in_dim.8
  141.0 0.0 copy-start
  141.0 15.7 %all_to_all.32.every_ref = bf16[8,256,256]{2,1,0:T(8,128)(2,1)S(1)} all-to-all(bf16[8,256,256]{2,1,0:T(8,128)(2,1)S(1)} %broadcast_in_dim.8), channel_id=1, replica_groups={{0,32,64,96,128,160,192,224},{4,36,68,100,132,164,196,228},{8,40,72,104..., dimensions={0} | all-to-all | bytes 2097152 | tf_op jit(solution)/shard_map/all_to_all | solution.py:25
  156.7 6.9 %track_means.1 = (bf16[2048,256]{1,0:T(8,128)(2,1)S(1)}, bf16[16,2048]{1,0:T(8,128)(2,1)S(1)}, f32[2048,128]{1,0:T(8,128)S(1)}) custom-call(s32[128]{0:T(128)S(1)} %copy-done.4, s32[1]{0:T(128)} %bitcast.2.index_ref, bf16[8,256,256]{2,1,0:T(8,128)(2,1)S(1)} %all_to_all.32.every_ref, bf16[8,80,256]{2,1,0:T(8,128)(2,1)S(1)} %all_to_all.31.both_ref, ...), custom_call_target="tpu_custom_call" | custom-call | tf_op jit(solution)/shard_map/track_means/pallas_call | solution.py:355
  163.5 0.1 collective-permute-start.8
  163.6 1.2 collective-permute-done.8
  164.8 0.8 collective-permute-start.9
  165.6 3.6 %collective-permute-done.9.other_ref = bf16[16,2048]{1,0:T(8,128)(2,1)S(1)} collective-permute-done((bf16[16,2048]{1,0:T(8,128)(2,1)S(1)}, bf16[16,2048]{1,0:T(8,128)(2,1)S(1)}, u32[]{:S(2)}, u32[]{:S(2)}) %collective-permute-start.9) | collective-permute-done | bytes 65568 | tf_op jit(solution)/shard_map/ppermute | solution.py:532
  169.2 2.0 %error_messages.1 = bf16[8,32,256]{2,1,0:T(8,128)(2,1)S(1)} custom-call(s32[128]{0:T(128)S(1)} %copy-done.4, bf16[16,2048]{1,0:T(8,128)(2,1)S(1)} %add_convert_fusion.part_ref, bf16[16,2048]{1,0:T(8,128)(2,1)S(1)} %collective-permute-done.9.other_ref, bf16[8,80,256]{2,1,0:T(8,128)(2,1)S(1)} %all_to_all.31.both_ref, ...), custom_call_target="tpu_custom_call" | custom-call | tf_op jit(solution)/shard_map/error_messages/pallas_call | solution.py:431
  171.2 11.5 %all_to_all.33.in_ref = bf16[8,32,256]{2,1,0:T(8,128)(2,1)S(1)} all-to-all(bf16[8,32,256]{2,1,0:T(8,128)(2,1)S(1)} %error_messages.1), channel_id=1, replica_groups={{0,4,8,12,16,20,24,28},{32,36,40,44,48,52,56,60},{64,68,72,76,80,84,88,..., dimensions={0} | all-to-all | bytes 262144 | tf_op jit(solution)/shard_map/all_to_all | solution.py:534
  182.7 0.1 relay.1
  182.8 15.1 %all_to_all.34 = bf16[8,128,384]{2,1,0:T(8,128)(2,1)S(1)} all-to-all(bf16[8,128,384]{2,1,0:T(8,128)(2,1)S(1)} %relay.1), channel_id=1, replica_groups={{0,32,64,96,128,160,192,224},{4,36,68,100,132,164,196,228},{8,40,72,104..., dimensions={0} | all-to-all | bytes 1572864 | tf_op jit(solution)/shard_map/all_to_all | solution.py:535
  198.0 1.4 finish.1
  (22 shorter events, 0.1 us)
Async XLA Ops:
  41.5 13.6 %collective-permute-start = (bf16[512,256]{1,0:T(8,128)(2,1)}, bf16[512,256]{1,0:T(8,128)(2,1)S(1)}, u32[]{:S(2)}, u32[]{:S(2)}) collective-permute-start(bf16[512,256]{1,0:T(8,128)(2,1)} %get-tuple-element.15.refs_0_), channel_id=1, source_target_pairs={{0,4},{4,8},{8,12},{12,16},{16,20},{20,24},{24,28},{28,0},{32,36},... | collective-permute-start | bytes 786440 | tf_op jit(solution)/shard_map/ppermute | solution.py:39
  43.5 11.7 %collective-permute-start.1 = (bf16[512,256]{1,0:T(8,128)(2,1)}, bf16[512,256]{1,0:T(8,128)(2,1)S(1)}, u32[]{:S(2)}, u32[]{:S(2)}) collective-permute-start(bf16[512,256]{1,0:T(8,128)(2,1)} %get-tuple-element.15.refs_0_), channel_id=1, source_target_pairs={{0,28},{4,0},{8,4},{12,8},{16,12},{20,16},{24,20},{28,24},{32,60},... | collective-permute-start | bytes 786440 | tf_op jit(solution)/shard_map/ppermute | solution.py:40
  47.6 28.2 %copy-start.2 = (bf16[4,16,1024]{2,1,0:T(8,128)(2,1)S(1)}, bf16[4,16,1024]{2,1,0:T(8,128)(2,1)}, u32[]{:S(2)}) copy-start(bf16[4,16,1024]{2,1,0:T(8,128)(2,1)} %param.14) | copy-start | bytes 393220
  47.6 28.2 %copy-start.5 = (s32[2,128]{1,0:T(2,128)S(1)}, s32[2,128]{1,0:T(2,128)}, u32[]{:S(2)}) copy-start(s32[2,128]{1,0:T(2,128)} %slot_ref.1) | copy-start | bytes 3076
  47.6 28.2 %copy-start.6 = (s32[2]{0:T(128)S(1)}, s32[2]{0:T(128)}, u32[]{:S(2)}) copy-start(s32[2]{0:T(128)} %row_count_ref.1) | copy-start | bytes 28
  47.6 31.0 %copy-start.1 = (bf16[512,256]{1,0:T(8,128)(2,1)S(1)}, bf16[512,256]{1,0:T(8,128)(2,1)}, u32[]{:S(2)}) copy-start(bf16[512,256]{1,0:T(8,128)(2,1)} %get-tuple-element.15.refs_0_) | copy-start | bytes 786436
  47.6 31.0 %all-to-all-start = ((bf16[8,256,256]{2,1,0:T(8,128)(2,1)}), bf16[8,256,256]{2,1,0:T(8,128)(2,1)S(1)}, u32[]{:S(2)}, u32[]{:S(2)}) async-start(bf16[8,256,256]{2,1,0:T(8,128)(2,1)} %get-tuple-element.12), calls=%async_computation | async-start | bytes 2097152 | tf_op jit(solution)/shard_map/all_to_all | solution.py:513
  55.2 8.4 %collective-permute-start.2 = (bf16[512,256]{1,0:T(8,128)(2,1)S(1)}, bf16[512,256]{1,0:T(8,128)(2,1)S(1)}, u32[]{:S(2)}, u32[]{:S(2)}) collective-permute-start(bf16[512,256]{1,0:T(8,128)(2,1)S(1)} %collective-permute-done.refs_1_), channel_id=1, source_target_pairs={{0,4},{4,8},{8,12},{12,16},{16,20},{20,24},{24,28},{28,0},{32,36},... | collective-permute-start | bytes 786440 | tf_op jit(solution)/shard_map/ppermute | solution.py:39
  55.2 8.4 %collective-permute-start.3 = (bf16[512,256]{1,0:T(8,128)(2,1)S(1)}, bf16[512,256]{1,0:T(8,128)(2,1)S(1)}, u32[]{:S(2)}, u32[]{:S(2)}) collective-permute-start(bf16[512,256]{1,0:T(8,128)(2,1)S(1)} %collective-permute-done.1.refs_2_), channel_id=1, source_target_pairs={{0,28},{4,0},{8,4},{12,8},{16,12},{20,16},{24,20},{28,24},{32,60},... | collective-permute-start | bytes 786440 | tf_op jit(solution)/shard_map/ppermute | solution.py:40
  63.6 7.6 %collective-permute-start.4 = (bf16[512,256]{1,0:T(8,128)(2,1)S(1)}, bf16[512,256]{1,0:T(8,128)(2,1)S(1)}, u32[]{:S(2)}, u32[]{:S(2)}) collective-permute-start(bf16[512,256]{1,0:T(8,128)(2,1)S(1)} %collective-permute-done.2.refs_3_), channel_id=1, source_target_pairs={{0,4},{4,8},{8,12},{12,16},{16,20},{20,24},{24,28},{28,0},{32,36},... | collective-permute-start | bytes 786440 | tf_op jit(solution)/shard_map/ppermute | solution.py:39
  63.6 8.2 %collective-permute-start.5 = (bf16[512,256]{1,0:T(8,128)(2,1)S(1)}, bf16[512,256]{1,0:T(8,128)(2,1)S(1)}, u32[]{:S(2)}, u32[]{:S(2)}) collective-permute-start(bf16[512,256]{1,0:T(8,128)(2,1)S(1)} %collective-permute-done.3.refs_4_), channel_id=1, source_target_pairs={{0,28},{4,0},{8,4},{12,8},{16,12},{20,16},{24,20},{28,24},{32,60},... | collective-permute-start | bytes 786440 | tf_op jit(solution)/shard_map/ppermute | solution.py:40
  71.8 6.4 %collective-permute-start.6 = (bf16[256,256]{1,0:T(8,128)(2,1)}, bf16[256,256]{1,0:T(8,128)(2,1)S(1)}, u32[]{:S(2)}, u32[]{:S(2)}) collective-permute-start(bf16[256,256]{1,0:T(8,128)(2,1)} %slice.12), channel_id=1, source_target_pairs={{0,4},{4,8},{8,12},{12,16},{16,20},{20,24},{24,28},{28,0},{32,36},... | collective-permute-start | bytes 393224 | tf_op jit(solution)/shard_map/ppermute | solution.py:43
  72.5 6.1 %collective-permute-start.7 = (bf16[256,256]{1,0:T(8,128)(2,1)}, bf16[256,256]{1,0:T(8,128)(2,1)S(1)}, u32[]{:S(2)}, u32[]{:S(2)}) collective-permute-start(bf16[256,256]{1,0:T(8,128)(2,1)} %slice.13), channel_id=1, source_target_pairs={{0,28},{4,0},{8,4},{12,8},{16,12},{20,16},{24,20},{28,24},{32,60},... | collective-permute-start | bytes 393224 | tf_op jit(solution)/shard_map/ppermute | solution.py:44
  101.3 21.3 %copy-start.3 = (bf16[256,256]{1,0:T(8,128)(2,1)S(1)}, bf16[256,256]{1,0:T(8,128)(2,1)}, u32[]{:S(2)}) copy-start(bf16[256,256]{1,0:T(8,128)(2,1)} %residual_ref.1) | copy-start | bytes 393220
  141.0 15.7 %copy-start = (bf16[256,1024]{1,0:T(8,128)(2,1)S(1)}, bf16[256,1024]{1,0:T(8,128)(2,1)}, u32[]{:S(2)}) copy-start(bf16[256,1024]{1,0:T(8,128)(2,1)} %weight_ref.3) | copy-start | bytes 1572868
  141.0 15.7 %copy-start.4 = (s32[128]{0:T(128)S(1)}, s32[128]{0:T(128)}, u32[]{:S(2)}) copy-start(s32[128]{0:T(128)} %track_ref.3) | copy-start | bytes 1540
  163.5 1.3 collective-permute-start.8
  164.8 4.4 %collective-permute-start.9 = (bf16[16,2048]{1,0:T(8,128)(2,1)S(1)}, bf16[16,2048]{1,0:T(8,128)(2,1)S(1)}, u32[]{:S(2)}, u32[]{:S(2)}) collective-permute-start(bf16[16,2048]{1,0:T(8,128)(2,1)S(1)} %add_convert_fusion.part_ref), channel_id=1, source_target_pairs={{0,2},{2,0},{1,3},{3,1},{4,6},{6,4},{5,7},{7,5},{8,10},{10,8},{9,1... | collective-permute-start | bytes 196616 | tf_op jit(solution)/shard_map/ppermute | solution.py:532

commit v9 on v8

--- a/solution.py
+++ b/solution.py
@@ -64,7 +64,7 @@
     anywhere = pl.BlockSpec(memory_space=pl.ANY)
     return pl.pallas_call(
         lay_out_kernel,
-        in_specs=[anywhere] * 3,
+        in_specs=[pl.BlockSpec(memory_space=pltpu.VMEM)] * 3,
         out_specs=[anywhere] * 2,
         out_shape=[
             jax.ShapeDtypeStruct((2 * n, width), keys.dtype),

time: 200 us -> 161 us (0.81)
  Pallas kernels: 76.5 us -> 37.7 us
    pallas_call x1, Pallas kernels: 40.9 us -> 2.15 us  [lay_out(): pl.pallas_call(lay_out_kernel, in_specs=[pl.BlockSpec(memory_space=pltpu....]
  transfers between devices with their start and end apart: 11 -> 11, of which waited for: 6 -> 6; matrix products, arithmetic and copies ran while one was open for 1% -> 1% of each run, Pallas kernels for 0% -> 1%
where the time goes in v9:
time: 161 us
  blocking collectives  80.3 us (50%)
  Pallas kernels  37.7 us (23%)
  starting transfers between devices  24.1 us (15%)
  waiting for transfers between devices  16.3 us (10%)
    pallas_call x1, Pallas kernels, attend(): pl.pallas_call(attend_kernel, grid=(pairs, SIDE // 2), in_specs=[pl.Block...  22.7 us
    all_to_all x1, blocking collectives, local(): part = lax.all_to_all(part, 'seq', 0, 0, axis_index_groups=GROUP_YX)  21.3 us
    all_to_all x1, blocking collectives, local(): both = lax.all_to_all(both, 'seq', 0, 0, axis_index_groups=GROUP_Z)  16.7 us
    all_to_all x1, blocking collectives, spread(): return lax.all_to_all(wide, 'seq', 0, 0, axis_index_groups=groups)  15.7 us
    all_to_all x1, blocking collectives, local(): lax.all_to_all(relay(final), 'seq', 0, 0, axis_index_groups=GROUP_YX)  15.1 us
    all_to_all x1, blocking collectives, local(): final = lax.all_to_all(final, 'seq', 0, 0, axis_index_groups=GROUP_Z)  11.5 us
    ppermute x3, starting transfers between devices, gather_ring(): down = lax.ppermute(down, 'seq', ring(seq_count, -1))  10.5 us
    ppermute x3, waiting for transfers between devices, gather_ring(): up = lax.ppermute(up, 'seq', ring(seq_count, 1))  9.52 us
  transfers between devices with their start and end apart: 11, of which 6 were waited for; matrix products, arithmetic and copies ran while one was open for 1% of the time, Pallas kernels for 1%

profile of v9, /device:TPU:2, one launch (start us, length us, event | category | flops | bytes accessed | tf_op | source)
XLA Modules:
  0.0 160.6 jit_solution(3463991691962372612)
XLA Ops:
  0.6 2.1 %lay_out.1 = (bf16[512,256]{1,0:T(8,128)(2,1)}, bf16[8,256,256]{2,1,0:T(8,128)(2,1)}) custom-call(bf16[256,256]{1,0:T(8,128)(2,1)} %k_ref.1, bf16[256,256]{1,0:T(8,128)(2,1)} %v_ref.1, bf16[256,256]{1,0:T(8,128)(2,1)} %q_ref.1), custom_call_target="tpu_custom_call" | custom-call | tf_op jit(solution)/shard_map/lay_out/pallas_call | solution.py:65
  2.8 2.0 %collective-permute-start = (bf16[512,256]{1,0:T(8,128)(2,1)}, bf16[512,256]{1,0:T(8,128)(2,1)S(1)}, u32[]{:S(2)}, u32[]{:S(2)}) collective-permute-start(bf16[512,256]{1,0:T(8,128)(2,1)} %get-tuple-element.15.refs_0_), channel_id=1, source_target_pairs={{0,4},{4,8},{8,12},{12,16},{16,20},{20,24},{24,28},{28,0},{32,36},... | collective-permute-start | bytes 786440 | tf_op jit(solution)/shard_map/ppermute | solution.py:39
  4.8 4.0 %collective-permute-start.1 = (bf16[512,256]{1,0:T(8,128)(2,1)}, bf16[512,256]{1,0:T(8,128)(2,1)S(1)}, u32[]{:S(2)}, u32[]{:S(2)}) collective-permute-start(bf16[512,256]{1,0:T(8,128)(2,1)} %get-tuple-element.15.refs_0_), channel_id=1, source_target_pairs={{0,28},{4,0},{8,4},{12,8},{16,12},{20,16},{24,20},{28,24},{32,60},... | collective-permute-start | bytes 786440 | tf_op jit(solution)/shard_map/ppermute | solution.py:40
  8.8 7.6 %all-to-all-start = ((bf16[8,256,256]{2,1,0:T(8,128)(2,1)}), bf16[8,256,256]{2,1,0:T(8,128)(2,1)S(1)}, u32[]{:S(2)}, u32[]{:S(2)}) async-start(bf16[8,256,256]{2,1,0:T(8,128)(2,1)} %get-tuple-element.12), calls=%async_computation | async-start | bytes 2097152 | tf_op jit(solution)/shard_map/all_to_all | solution.py:513
  16.4 3.2 %collective-permute-start.3 = (bf16[512,256]{1,0:T(8,128)(2,1)S(1)}, bf16[512,256]{1,0:T(8,128)(2,1)S(1)}, u32[]{:S(2)}, u32[]{:S(2)}) collective-permute-start(bf16[512,256]{1,0:T(8,128)(2,1)S(1)} %collective-permute-done.1.refs_2_), channel_id=1, source_target_pairs={{0,28},{4,0},{8,4},{12,8},{16,12},{20,16},{24,20},{28,24},{32,60},... | collective-permute-start | bytes 786440 | tf_op jit(solution)/shard_map/ppermute | solution.py:40
  19.7 5.2 %collective-permute-done.2.refs_3_ = bf16[512,256]{1,0:T(8,128)(2,1)S(1)} collective-permute-done((bf16[512,256]{1,0:T(8,128)(2,1)S(1)}, bf16[512,256]{1,0:T(8,128)(2,1)S(1)}, u32[]{:S(2)}, u32[]{:S(2)}) %collective-permute-start.2) | collective-permute-done | bytes 262176 | tf_op jit(solution)/shard_map/ppermute | solution.py:39
  24.9 3.2 %collective-permute-start.5 = (bf16[512,256]{1,0:T(8,128)(2,1)S(1)}, bf16[512,256]{1,0:T(8,128)(2,1)S(1)}, u32[]{:S(2)}, u32[]{:S(2)}) collective-permute-start(bf16[512,256]{1,0:T(8,128)(2,1)S(1)} %collective-permute-done.3.refs_4_), channel_id=1, source_target_pairs={{0,28},{4,0},{8,4},{12,8},{16,12},{20,16},{24,20},{28,24},{32,60},... | collective-permute-start | bytes 786440 | tf_op jit(solution)/shard_map/ppermute | solution.py:40
  28.1 4.3 %collective-permute-done.4.refs_5_ = bf16[512,256]{1,0:T(8,128)(2,1)S(1)} collective-permute-done((bf16[512,256]{1,0:T(8,128)(2,1)S(1)}, bf16[512,256]{1,0:T(8,128)(2,1)S(1)}, u32[]{:S(2)}, u32[]{:S(2)}) %collective-permute-start.4) | collective-permute-done | bytes 262176 | tf_op jit(solution)/shard_map/ppermute | solution.py:39
  32.4 0.7 slice.12
  33.1 0.7 slice.13
  33.8 3.2 %collective-permute-start.7 = (bf16[256,256]{1,0:T(8,128)(2,1)}, bf16[256,256]{1,0:T(8,128)(2,1)S(1)}, u32[]{:S(2)}, u32[]{:S(2)}) collective-permute-start(bf16[256,256]{1,0:T(8,128)(2,1)} %slice.13), channel_id=1, source_target_pairs={{0,28},{4,0},{8,4},{12,8},{16,12},{20,16},{24,20},{28,24},{32,60},... | collective-permute-start | bytes 393224 | tf_op jit(solution)/shard_map/ppermute | solution.py:44
  37.0 0.9 prepare.1
  37.9 1.6 collective-permute-done.6.refs_7_
  39.5 0.3 collective-permute-done.7.refs_8_
  39.8 22.7 %attend.1 = bf16[8,304,256]{2,1,0:T(8,128)(2,1)S(1)} custom-call(bf16[2048,256]{1,0:T(8,128)(2,1)S(1)} %bitcast.5, bf16[8,32,256]{2,1,0:T(8,128)(2,1)S(1)} %get-tuple-element.13.piece_ref, f32[1,128]{1,0:T(1,128)S(1)} %get-tuple-element.14.count_ref, bf16[512,256]{1,0:T(8,128)(2,1)S(1)} %copy-done.1, bf16[512,256]{1,0:T(8,128)(2,1)S(1)} %collective-permute-done.refs_1_, ...), custom_call_target="tpu_custom_call" | custom-call | tf_op jit(solution)/shard_map/attend/pallas_call | solution.py:184
  62.6 0.0 copy-start.3
  62.6 21.3 %all_to_all.30.part_ref = bf16[8,304,256]{2,1,0:T(8,128)(2,1)S(1)} all-to-all(bf16[8,304,256]{2,1,0:T(8,128)(2,1)S(1)} %attend.1), channel_id=1, replica_groups={{0,32,64,96,128,160,192,224},{4,36,68,100,132,164,196,228},{8,40,72,104..., dimensions={0} | all-to-all | bytes 2490368 | tf_op jit(solution)/shard_map/all_to_all | solution.py:521
  83.9 1.5 merge.1
  85.4 16.7 %all_to_all.31.both_ref = bf16[8,80,256]{2,1,0:T(8,128)(2,1)S(1)} all-to-all(bf16[8,80,256]{2,1,0:T(8,128)(2,1)S(1)} %merge.1), channel_id=1, replica_groups={{0,4,8,12,16,20,24,28},{32,36,40,44,48,52,56,60},{64,68,72,76,80,84,88,..., dimensions={0} | all-to-all | bytes 655360 | tf_op jit(solution)/shard_map/all_to_all | solution.py:523
  102.1 0.1 broadcast_in_dim.8
  102.2 0.0 copy-start
  102.2 15.7 %all_to_all.32.every_ref = bf16[8,256,256]{2,1,0:T(8,128)(2,1)S(1)} all-to-all(bf16[8,256,256]{2,1,0:T(8,128)(2,1)S(1)} %broadcast_in_dim.8), channel_id=1, replica_groups={{0,32,64,96,128,160,192,224},{4,36,68,100,132,164,196,228},{8,40,72,104..., dimensions={0} | all-to-all | bytes 2097152 | tf_op jit(solution)/shard_map/all_to_all | solution.py:25
  117.9 6.9 %track_means.1 = (bf16[2048,256]{1,0:T(8,128)(2,1)S(1)}, bf16[16,2048]{1,0:T(8,128)(2,1)S(1)}, f32[2048,128]{1,0:T(8,128)S(1)}) custom-call(s32[128]{0:T(128)S(1)} %copy-done.4, s32[1]{0:T(128)} %bitcast.2.index_ref, bf16[8,256,256]{2,1,0:T(8,128)(2,1)S(1)} %all_to_all.32.every_ref, bf16[8,80,256]{2,1,0:T(8,128)(2,1)S(1)} %all_to_all.31.both_ref, ...), custom_call_target="tpu_custom_call" | custom-call | tf_op jit(solution)/shard_map/track_means/pallas_call | solution.py:355
  124.8 0.1 collective-permute-start.8
  124.8 1.2 collective-permute-done.8
  126.1 0.8 collective-permute-start.9
  126.9 3.6 %collective-permute-done.9.other_ref = bf16[16,2048]{1,0:T(8,128)(2,1)S(1)} collective-permute-done((bf16[16,2048]{1,0:T(8,128)(2,1)S(1)}, bf16[16,2048]{1,0:T(8,128)(2,1)S(1)}, u32[]{:S(2)}, u32[]{:S(2)}) %collective-permute-start.9) | collective-permute-done | bytes 65568 | tf_op jit(solution)/shard_map/ppermute | solution.py:532
  130.5 2.0 %error_messages.1 = bf16[8,32,256]{2,1,0:T(8,128)(2,1)S(1)} custom-call(s32[128]{0:T(128)S(1)} %copy-done.4, bf16[16,2048]{1,0:T(8,128)(2,1)S(1)} %add_convert_fusion.part_ref, bf16[16,2048]{1,0:T(8,128)(2,1)S(1)} %collective-permute-done.9.other_ref, bf16[8,80,256]{2,1,0:T(8,128)(2,1)S(1)} %all_to_all.31.both_ref, ...), custom_call_target="tpu_custom_call" | custom-call | tf_op jit(solution)/shard_map/error_messages/pallas_call | solution.py:431
  132.5 11.5 %all_to_all.33.in_ref = bf16[8,32,256]{2,1,0:T(8,128)(2,1)S(1)} all-to-all(bf16[8,32,256]{2,1,0:T(8,128)(2,1)S(1)} %error_messages.1), channel_id=1, replica_groups={{0,4,8,12,16,20,24,28},{32,36,40,44,48,52,56,60},{64,68,72,76,80,84,88,..., dimensions={0} | all-to-all | bytes 262144 | tf_op jit(solution)/shard_map/all_to_all | solution.py:534
  144.0 0.1 relay.1
  144.1 15.1 %all_to_all.34 = bf16[8,128,384]{2,1,0:T(8,128)(2,1)S(1)} all-to-all(bf16[8,128,384]{2,1,0:T(8,128)(2,1)S(1)} %relay.1), channel_id=1, replica_groups={{0,32,64,96,128,160,192,224},{4,36,68,100,132,164,196,228},{8,40,72,104..., dimensions={0} | all-to-all | bytes 1572864 | tf_op jit(solution)/shard_map/all_to_all | solution.py:535
  159.2 1.4 finish.1
  (22 shorter events, 0.1 us)
Async XLA Ops:
  2.8 13.6 %collective-permute-start = (bf16[512,256]{1,0:T(8,128)(2,1)}, bf16[512,256]{1,0:T(8,128)(2,1)S(1)}, u32[]{:S(2)}, u32[]{:S(2)}) collective-permute-start(bf16[512,256]{1,0:T(8,128)(2,1)} %get-tuple-element.15.refs_0_), channel_id=1, source_target_pairs={{0,4},{4,8},{8,12},{12,16},{16,20},{20,24},{24,28},{28,0},{32,36},... | collective-permute-start | bytes 786440 | tf_op jit(solution)/shard_map/ppermute | solution.py:39
  4.8 11.7 %collective-permute-start.1 = (bf16[512,256]{1,0:T(8,128)(2,1)}, bf16[512,256]{1,0:T(8,128)(2,1)S(1)}, u32[]{:S(2)}, u32[]{:S(2)}) collective-permute-start(bf16[512,256]{1,0:T(8,128)(2,1)} %get-tuple-element.15.refs_0_), channel_id=1, source_target_pairs={{0,28},{4,0},{8,4},{12,8},{16,12},{20,16},{24,20},{28,24},{32,60},... | collective-permute-start | bytes 786440 | tf_op jit(solution)/shard_map/ppermute | solution.py:40
  8.8 28.2 %copy-start.2 = (bf16[4,16,1024]{2,1,0:T(8,128)(2,1)S(1)}, bf16[4,16,1024]{2,1,0:T(8,128)(2,1)}, u32[]{:S(2)}) copy-start(bf16[4,16,1024]{2,1,0:T(8,128)(2,1)} %param.14) | copy-start | bytes 393220
  8.8 28.2 %copy-start.5 = (s32[2,128]{1,0:T(2,128)S(1)}, s32[2,128]{1,0:T(2,128)}, u32[]{:S(2)}) copy-start(s32[2,128]{1,0:T(2,128)} %slot_ref.1) | copy-start | bytes 3076
  8.8 28.2 %copy-start.6 = (s32[2]{0:T(128)S(1)}, s32[2]{0:T(128)}, u32[]{:S(2)}) copy-start(s32[2]{0:T(128)} %row_count_ref.1) | copy-start | bytes 28
  8.8 31.0 %copy-start.1 = (bf16[512,256]{1,0:T(8,128)(2,1)S(1)}, bf16[512,256]{1,0:T(8,128)(2,1)}, u32[]{:S(2)}) copy-start(bf16[512,256]{1,0:T(8,128)(2,1)} %get-tuple-element.15.refs_0_) | copy-start | bytes 786436
  8.8 31.0 %all-to-all-start = ((bf16[8,256,256]{2,1,0:T(8,128)(2,1)}), bf16[8,256,256]{2,1,0:T(8,128)(2,1)S(1)}, u32[]{:S(2)}, u32[]{:S(2)}) async-start(bf16[8,256,256]{2,1,0:T(8,128)(2,1)} %get-tuple-element.12), calls=%async_computation | async-start | bytes 2097152 | tf_op jit(solution)/shard_map/all_to_all | solution.py:513
  16.4 8.4 %collective-permute-start.2 = (bf16[512,256]{1,0:T(8,128)(2,1)S(1)}, bf16[512,256]{1,0:T(8,128)(2,1)S(1)}, u32[]{:S(2)}, u32[]{:S(2)}) collective-permute-start(bf16[512,256]{1,0:T(8,128)(2,1)S(1)} %collective-permute-done.refs_1_), channel_id=1, source_target_pairs={{0,4},{4,8},{8,12},{12,16},{16,20},{20,24},{24,28},{28,0},{32,36},... | collective-permute-start | bytes 786440 | tf_op jit(solution)/shard_map/ppermute | solution.py:39
  16.4 8.4 %collective-permute-start.3 = (bf16[512,256]{1,0:T(8,128)(2,1)S(1)}, bf16[512,256]{1,0:T(8,128)(2,1)S(1)}, u32[]{:S(2)}, u32[]{:S(2)}) collective-permute-start(bf16[512,256]{1,0:T(8,128)(2,1)S(1)} %collective-permute-done.1.refs_2_), channel_id=1, source_target_pairs={{0,28},{4,0},{8,4},{12,8},{16,12},{20,16},{24,20},{28,24},{32,60},... | collective-permute-start | bytes 786440 | tf_op jit(solution)/shard_map/ppermute | solution.py:40
  24.8 7.6 %collective-permute-start.4 = (bf16[512,256]{1,0:T(8,128)(2,1)S(1)}, bf16[512,256]{1,0:T(8,128)(2,1)S(1)}, u32[]{:S(2)}, u32[]{:S(2)}) collective-permute-start(bf16[512,256]{1,0:T(8,128)(2,1)S(1)} %collective-permute-done.2.refs_3_), channel_id=1, source_target_pairs={{0,4},{4,8},{8,12},{12,16},{16,20},{20,24},{24,28},{28,0},{32,36},... | collective-permute-start | bytes 786440 | tf_op jit(solution)/shard_map/ppermute | solution.py:39
  24.9 8.2 %collective-permute-start.5 = (bf16[512,256]{1,0:T(8,128)(2,1)S(1)}, bf16[512,256]{1,0:T(8,128)(2,1)S(1)}, u32[]{:S(2)}, u32[]{:S(2)}) collective-permute-start(bf16[512,256]{1,0:T(8,128)(2,1)S(1)} %collective-permute-done.3.refs_4_), channel_id=1, source_target_pairs={{0,28},{4,0},{8,4},{12,8},{16,12},{20,16},{24,20},{28,24},{32,60},... | collective-permute-start | bytes 786440 | tf_op jit(solution)/shard_map/ppermute | solution.py:40
  33.1 6.4 %collective-permute-start.6 = (bf16[256,256]{1,0:T(8,128)(2,1)}, bf16[256,256]{1,0:T(8,128)(2,1)S(1)}, u32[]{:S(2)}, u32[]{:S(2)}) collective-permute-start(bf16[256,256]{1,0:T(8,128)(2,1)} %slice.12), channel_id=1, source_target_pairs={{0,4},{4,8},{8,12},{12,16},{16,20},{20,24},{24,28},{28,0},{32,36},... | collective-permute-start | bytes 393224 | tf_op jit(solution)/shard_map/ppermute | solution.py:43
  33.8 6.1 %collective-permute-start.7 = (bf16[256,256]{1,0:T(8,128)(2,1)}, bf16[256,256]{1,0:T(8,128)(2,1)S(1)}, u32[]{:S(2)}, u32[]{:S(2)}) collective-permute-start(bf16[256,256]{1,0:T(8,128)(2,1)} %slice.13), channel_id=1, source_target_pairs={{0,28},{4,0},{8,4},{12,8},{16,12},{20,16},{24,20},{28,24},{32,60},... | collective-permute-start | bytes 393224 | tf_op jit(solution)/shard_map/ppermute | solution.py:44
  62.6 21.3 %copy-start.3 = (bf16[256,256]{1,0:T(8,128)(2,1)S(1)}, bf16[256,256]{1,0:T(8,128)(2,1)}, u32[]{:S(2)}) copy-start(bf16[256,256]{1,0:T(8,128)(2,1)} %residual_ref.1) | copy-start | bytes 393220
  102.2 15.7 %copy-start = (bf16[256,1024]{1,0:T(8,128)(2,1)S(1)}, bf16[256,1024]{1,0:T(8,128)(2,1)}, u32[]{:S(2)}) copy-start(bf16[256,1024]{1,0:T(8,128)(2,1)} %weight_ref.3) | copy-start | bytes 1572868
  102.2 15.7 %copy-start.4 = (s32[128]{0:T(128)S(1)}, s32[128]{0:T(128)}, u32[]{:S(2)}) copy-start(s32[128]{0:T(128)} %track_ref.3) | copy-start | bytes 1540
  124.8 1.3 collective-permute-start.8
  126.1 4.4 %collective-permute-start.9 = (bf16[16,2048]{1,0:T(8,128)(2,1)S(1)}, bf16[16,2048]{1,0:T(8,128)(2,1)S(1)}, u32[]{:S(2)}, u32[]{:S(2)}) collective-permute-start(bf16[16,2048]{1,0:T(8,128)(2,1)S(1)} %add_convert_fusion.part_ref), channel_id=1, source_target_pairs={{0,2},{2,0},{1,3},{3,1},{4,6},{6,4},{5,7},{7,5},{8,10},{10,8},{9,1... | collective-permute-start | bytes 196616 | tf_op jit(solution)/shard_map/ppermute | solution.py:532

commit v10 on v9

--- a/solution.py
+++ b/solution.py
@@ -439,36 +439,46 @@
 
 
 def relay_kernel(in_ref, out_ref):
-    chunk, width = in_ref.shape[1] // 2, in_ref.shape[2]
-    for z in range(SIDE):
-        span = slice(z * chunk, z * chunk + chunk)
-        grad = in_ref[z, :chunk]
-        errors = in_ref[z, chunk:].astype(jnp.float32)
-        for g in range(SIDE):
-            tile = errors[:, g // 4 * 128 : g // 4 * 128 + 128]
-            tile = pltpu.roll(tile, 128 - g % 4 * 32, 1) if g % 4 else tile
-            out_ref[g, span, :width] = grad
-            out_ref[g, span, width:] = tile.astype(jnp.bfloat16)
+    chunk = in_ref.shape[1] // 2
+    lane = lax.broadcasted_iota(jnp.int32, (chunk, 128), 1)
+    errors = [in_ref[z, chunk:].astype(jnp.float32) for z in range(SIDE)]
+    for g in range(SIDE):
+        for z in range(SIDE):
+            out_ref[g, z * chunk : z * chunk + chunk] = in_ref[z, :chunk]
+        for half in range(2):
+            tile = jnp.zeros((chunk, 128), jnp.float32)
+            for q in range(4):
+                row = errors[half * 4 + q][:, g // 4 * 128 : g // 4 * 128 + 128]
+                turn = (q - g % 4) % 4 * 32
+                row = pltpu.roll(row, turn, 1) if turn else row
+                tile = jnp.where(lane // 32 == q, row, tile)
+            out_ref[g, SIDE * chunk :, half * 128 : half * 128 + 128] = tile.astype(jnp.bfloat16)
 
 
 def relay(x):
     chunk, width = x.shape[1] // 2, x.shape[2]
     return pl.pallas_call(
         relay_kernel,
-        out_shape=jax.ShapeDtypeStruct((SIDE, SIDE * chunk, width + 128), jnp.bfloat16),
+        out_shape=jax.ShapeDtypeStruct((SIDE, (SIDE + 1) * chunk, width), jnp.bfloat16),
         compiler_params=pltpu.CompilerParams(vmem_limit_bytes=VMEM_BYTES),
         name="relay",
     )(x)
 
 
 def finish_kernel(index_ref, final_ref, weight_ref, sel_ref, divisor_ref, grad_ref, context_ref):
-    width = weight_ref.shape[0]
     back = sel_ref.shape[0]
-    for i in range(final_ref.shape[0] // width):
-        span = slice(i * width, i * width + width)
-        grad_ref[:, span] = final_ref[span, :width].T
+    chunk = final_ref.shape[1] // (SIDE + 1)
+    rows = SIDE * chunk
+    tiles = []
+    for g in range(SIDE):
+        grad_ref[:, g * rows : g * rows + rows] = final_ref[g, :rows].T
+        errors = final_ref[g, rows:].astype(jnp.float32)
+        for z in range(SIDE):
+            tile = errors[:, z // 4 * 128 : z // 4 * 128 + 128]
+            tile = pltpu.roll(tile, 128 - z % 4 * 32, 1) if z % 4 else tile
+            tiles.append(tile.astype(jnp.bfloat16))
     mean_grad = jnp.dot(
-        weight_ref[...], final_ref[:, width:], preferred_element_type=jnp.float32
+        weight_ref[...], jnp.concatenate(tiles, axis=0), preferred_element_type=jnp.float32
     ).T[:back]
     track_grad = (mean_grad / divisor_ref[:, :1]).astype(jnp.bfloat16)
     context_ref[...] = lax.dot_general(
@@ -486,7 +496,7 @@
             num_scalar_prefetch=1,
             grid=(1,),
             in_specs=[
-                whole(*final.shape),
+                pl.BlockSpec(final.shape, lambda i, at: (0, 0, 0)),
                 whole(*weight.shape),
                 whole(*sel.shape),
                 pl.BlockSpec((back, 128), lambda i, at: (at[0], 0)),
@@ -533,7 +543,7 @@
     final = error_messages(block_track, partial, other, both, mean, seq_count)
     final = lax.all_to_all(final, "seq", 0, 0, axis_index_groups=GROUP_Z)
     final = lax.all_to_all(relay(final), "seq", 0, 0, axis_index_groups=GROUP_YX)
-    return finish(index, final.reshape(target_d, width + 128), reg_weight, selector, divisor)
+    return finish(index, final, reg_weight, selector, divisor)
 
 
 def solution(mesh):

time: 161 us -> 159 us (0.988)
  blocking collectives: 80.3 us -> 78.2 us
    all_to_all x1, blocking collectives: 15.1 us -> 13.1 us  [local(): lax.all_to_all(relay(final), 'seq', 0, 0, axis_index_groups=GROUP_YX)]
where the time goes in v10:
time: 159 us
  blocking collectives  78.2 us (49%)
  Pallas kernels  37.8 us (24%)
  starting transfers between devices  24.1 us (15%)
  waiting for transfers between devices  16.3 us (10%)
    pallas_call x1, Pallas kernels, attend(): pl.pallas_call(attend_kernel, grid=(pairs, SIDE // 2), in_specs=[pl.Block...  22.7 us
    all_to_all x1, blocking collectives, local(): part = lax.all_to_all(part, 'seq', 0, 0, axis_index_groups=GROUP_YX)  21.3 us
    all_to_all x1, blocking collectives, local(): both = lax.all_to_all(both, 'seq', 0, 0, axis_index_groups=GROUP_Z)  16.7 us
    all_to_all x1, blocking collectives, spread(): return lax.all_to_all(wide, 'seq', 0, 0, axis_index_groups=groups)  15.7 us
    all_to_all x1, blocking collectives, local(): lax.all_to_all(relay(final), 'seq', 0, 0, axis_index_groups=GROUP_YX)  13.1 us
    all_to_all x1, blocking collectives, local(): final = lax.all_to_all(final, 'seq', 0, 0, axis_index_groups=GROUP_Z)  11.5 us
    ppermute x3, starting transfers between devices, gather_ring(): down = lax.ppermute(down, 'seq', ring(seq_count, -1))  10.5 us
    ppermute x3, waiting for transfers between devices, gather_ring(): up = lax.ppermute(up, 'seq', ring(seq_count, 1))  9.52 us
  transfers between devices with their start and end apart: 11, of which 6 were waited for; matrix products, arithmetic and copies ran while one was open for 1% of the time, Pallas kernels for 1%

profile of v10, /device:TPU:2, one launch (start us, length us, event | category | flops | bytes accessed | tf_op | source)
XLA Modules:
  0.0 158.6 jit_solution(13302792196309241984)
XLA Ops:
  0.6 2.1 %lay_out.1 = (bf16[512,256]{1,0:T(8,128)(2,1)}, bf16[8,256,256]{2,1,0:T(8,128)(2,1)}) custom-call(bf16[256,256]{1,0:T(8,128)(2,1)} %k_ref.1, bf16[256,256]{1,0:T(8,128)(2,1)} %v_ref.1, bf16[256,256]{1,0:T(8,128)(2,1)} %q_ref.1), custom_call_target="tpu_custom_call" | custom-call | tf_op jit(solution)/shard_map/lay_out/pallas_call | solution.py:65
  2.8 2.0 %collective-permute-start = (bf16[512,256]{1,0:T(8,128)(2,1)}, bf16[512,256]{1,0:T(8,128)(2,1)S(1)}, u32[]{:S(2)}, u32[]{:S(2)}) collective-permute-start(bf16[512,256]{1,0:T(8,128)(2,1)} %get-tuple-element.15.refs_0_), channel_id=1, source_target_pairs={{0,4},{4,8},{8,12},{12,16},{16,20},{20,24},{24,28},{28,0},{32,36},... | collective-permute-start | bytes 786440 | tf_op jit(solution)/shard_map/ppermute | solution.py:39
  4.8 4.0 %collective-permute-start.1 = (bf16[512,256]{1,0:T(8,128)(2,1)}, bf16[512,256]{1,0:T(8,128)(2,1)S(1)}, u32[]{:S(2)}, u32[]{:S(2)}) collective-permute-start(bf16[512,256]{1,0:T(8,128)(2,1)} %get-tuple-element.15.refs_0_), channel_id=1, source_target_pairs={{0,28},{4,0},{8,4},{12,8},{16,12},{20,16},{24,20},{28,24},{32,60},... | collective-permute-start | bytes 786440 | tf_op jit(solution)/shard_map/ppermute | solution.py:40
  8.8 7.6 %all-to-all-start = ((bf16[8,256,256]{2,1,0:T(8,128)(2,1)}), bf16[8,256,256]{2,1,0:T(8,128)(2,1)S(1)}, u32[]{:S(2)}, u32[]{:S(2)}) async-start(bf16[8,256,256]{2,1,0:T(8,128)(2,1)} %get-tuple-element.12), calls=%async_computation | async-start | bytes 2097152 | tf_op jit(solution)/shard_map/all_to_all | solution.py:523
  16.4 3.2 %collective-permute-start.3 = (bf16[512,256]{1,0:T(8,128)(2,1)S(1)}, bf16[512,256]{1,0:T(8,128)(2,1)S(1)}, u32[]{:S(2)}, u32[]{:S(2)}) collective-permute-start(bf16[512,256]{1,0:T(8,128)(2,1)S(1)} %collective-permute-done.1.refs_2_), channel_id=1, source_target_pairs={{0,28},{4,0},{8,4},{12,8},{16,12},{20,16},{24,20},{28,24},{32,60},... | collective-permute-start | bytes 786440 | tf_op jit(solution)/shard_map/ppermute | solution.py:40
  19.7 5.2 %collective-permute-done.2.refs_3_ = bf16[512,256]{1,0:T(8,128)(2,1)S(1)} collective-permute-done((bf16[512,256]{1,0:T(8,128)(2,1)S(1)}, bf16[512,256]{1,0:T(8,128)(2,1)S(1)}, u32[]{:S(2)}, u32[]{:S(2)}) %collective-permute-start.2) | collective-permute-done | bytes 262176 | tf_op jit(solution)/shard_map/ppermute | solution.py:39
  24.9 3.2 %collective-permute-start.5 = (bf16[512,256]{1,0:T(8,128)(2,1)S(1)}, bf16[512,256]{1,0:T(8,128)(2,1)S(1)}, u32[]{:S(2)}, u32[]{:S(2)}) collective-permute-start(bf16[512,256]{1,0:T(8,128)(2,1)S(1)} %collective-permute-done.3.refs_4_), channel_id=1, source_target_pairs={{0,28},{4,0},{8,4},{12,8},{16,12},{20,16},{24,20},{28,24},{32,60},... | collective-permute-start | bytes 786440 | tf_op jit(solution)/shard_map/ppermute | solution.py:40
  28.1 4.3 %collective-permute-done.4.refs_5_ = bf16[512,256]{1,0:T(8,128)(2,1)S(1)} collective-permute-done((bf16[512,256]{1,0:T(8,128)(2,1)S(1)}, bf16[512,256]{1,0:T(8,128)(2,1)S(1)}, u32[]{:S(2)}, u32[]{:S(2)}) %collective-permute-start.4) | collective-permute-done | bytes 262176 | tf_op jit(solution)/shard_map/ppermute | solution.py:39
  32.4 0.7 slice.12
  33.1 0.7 slice.13
  33.8 3.2 %collective-permute-start.7 = (bf16[256,256]{1,0:T(8,128)(2,1)}, bf16[256,256]{1,0:T(8,128)(2,1)S(1)}, u32[]{:S(2)}, u32[]{:S(2)}) collective-permute-start(bf16[256,256]{1,0:T(8,128)(2,1)} %slice.13), channel_id=1, source_target_pairs={{0,28},{4,0},{8,4},{12,8},{16,12},{20,16},{24,20},{28,24},{32,60},... | collective-permute-start | bytes 393224 | tf_op jit(solution)/shard_map/ppermute | solution.py:44
  37.0 0.9 prepare.1
  37.9 1.6 collective-permute-done.6.refs_7_
  39.5 0.3 collective-permute-done.7.refs_8_
  39.8 22.7 %attend.1 = bf16[8,304,256]{2,1,0:T(8,128)(2,1)S(1)} custom-call(bf16[2048,256]{1,0:T(8,128)(2,1)S(1)} %bitcast.4, bf16[8,32,256]{2,1,0:T(8,128)(2,1)S(1)} %get-tuple-element.13.piece_ref, f32[1,128]{1,0:T(1,128)S(1)} %get-tuple-element.14.count_ref, bf16[512,256]{1,0:T(8,128)(2,1)S(1)} %copy-done.1, bf16[512,256]{1,0:T(8,128)(2,1)S(1)} %collective-permute-done.refs_1_, ...), custom_call_target="tpu_custom_call" | custom-call | tf_op jit(solution)/shard_map/attend/pallas_call | solution.py:184
  62.6 0.0 copy-start.3
  62.6 21.3 %all_to_all.30.part_ref = bf16[8,304,256]{2,1,0:T(8,128)(2,1)S(1)} all-to-all(bf16[8,304,256]{2,1,0:T(8,128)(2,1)S(1)} %attend.1), channel_id=1, replica_groups={{0,32,64,96,128,160,192,224},{4,36,68,100,132,164,196,228},{8,40,72,104..., dimensions={0} | all-to-all | bytes 2490368 | tf_op jit(solution)/shard_map/all_to_all | solution.py:531
  83.9 1.5 merge.1
  85.4 16.7 %all_to_all.31.both_ref = bf16[8,80,256]{2,1,0:T(8,128)(2,1)S(1)} all-to-all(bf16[8,80,256]{2,1,0:T(8,128)(2,1)S(1)} %merge.1), channel_id=1, replica_groups={{0,4,8,12,16,20,24,28},{32,36,40,44,48,52,56,60},{64,68,72,76,80,84,88,..., dimensions={0} | all-to-all | bytes 655360 | tf_op jit(solution)/shard_map/all_to_all | solution.py:533
  102.1 0.1 broadcast_in_dim.8
  102.2 0.0 copy-start.4
  102.2 15.7 %all_to_all.32.every_ref = bf16[8,256,256]{2,1,0:T(8,128)(2,1)S(1)} all-to-all(bf16[8,256,256]{2,1,0:T(8,128)(2,1)S(1)} %broadcast_in_dim.8), channel_id=1, replica_groups={{0,32,64,96,128,160,192,224},{4,36,68,100,132,164,196,228},{8,40,72,104..., dimensions={0} | all-to-all | bytes 2097152 | tf_op jit(solution)/shard_map/all_to_all | solution.py:25
  117.9 6.9 %track_means.1 = (bf16[2048,256]{1,0:T(8,128)(2,1)S(1)}, bf16[16,2048]{1,0:T(8,128)(2,1)S(1)}, f32[2048,128]{1,0:T(8,128)S(1)}) custom-call(s32[128]{0:T(128)S(1)} %copy-done.4, s32[1]{0:T(128)} %bitcast.2.index_ref, bf16[8,256,256]{2,1,0:T(8,128)(2,1)S(1)} %all_to_all.32.every_ref, bf16[8,80,256]{2,1,0:T(8,128)(2,1)S(1)} %all_to_all.31.both_ref, ...), custom_call_target="tpu_custom_call" | custom-call | tf_op jit(solution)/shard_map/track_means/pallas_call | solution.py:355
  124.8 0.1 collective-permute-start.8
  124.8 1.2 collective-permute-done.8
  126.1 0.8 collective-permute-start.9
  126.9 3.6 %collective-permute-done.9.other_ref = bf16[16,2048]{1,0:T(8,128)(2,1)S(1)} collective-permute-done((bf16[16,2048]{1,0:T(8,128)(2,1)S(1)}, bf16[16,2048]{1,0:T(8,128)(2,1)S(1)}, u32[]{:S(2)}, u32[]{:S(2)}) %collective-permute-start.9) | collective-permute-done | bytes 65568 | tf_op jit(solution)/shard_map/ppermute | solution.py:542
  130.5 2.0 %error_messages.1 = bf16[8,32,256]{2,1,0:T(8,128)(2,1)S(1)} custom-call(s32[128]{0:T(128)S(1)} %copy-done.4, bf16[16,2048]{1,0:T(8,128)(2,1)S(1)} %add_convert_fusion.part_ref, bf16[16,2048]{1,0:T(8,128)(2,1)S(1)} %collective-permute-done.9.other_ref, bf16[8,80,256]{2,1,0:T(8,128)(2,1)S(1)} %all_to_all.31.both_ref, ...), custom_call_target="tpu_custom_call" | custom-call | tf_op jit(solution)/shard_map/error_messages/pallas_call | solution.py:431
  132.5 11.5 %all_to_all.33.in_ref = bf16[8,32,256]{2,1,0:T(8,128)(2,1)S(1)} all-to-all(bf16[8,32,256]{2,1,0:T(8,128)(2,1)S(1)} %error_messages.1), channel_id=1, replica_groups={{0,4,8,12,16,20,24,28},{32,36,40,44,48,52,56,60},{64,68,72,76,80,84,88,..., dimensions={0} | all-to-all | bytes 262144 | tf_op jit(solution)/shard_map/all_to_all | solution.py:544
  144.0 0.1 relay.1
  144.1 13.1 %all_to_all.34.final_ref = bf16[8,144,256]{2,1,0:T(8,128)(2,1)S(1)} all-to-all(bf16[8,144,256]{2,1,0:T(8,128)(2,1)S(1)} %relay.1), channel_id=1, replica_groups={{0,32,64,96,128,160,192,224},{4,36,68,100,132,164,196,228},{8,40,72,104..., dimensions={0} | all-to-all | bytes 1179648 | tf_op jit(solution)/shard_map/all_to_all | solution.py:545
  157.2 1.4 finish.1
  (22 shorter events, 0.1 us)
Async XLA Ops:
  2.8 13.6 %collective-permute-start = (bf16[512,256]{1,0:T(8,128)(2,1)}, bf16[512,256]{1,0:T(8,128)(2,1)S(1)}, u32[]{:S(2)}, u32[]{:S(2)}) collective-permute-start(bf16[512,256]{1,0:T(8,128)(2,1)} %get-tuple-element.15.refs_0_), channel_id=1, source_target_pairs={{0,4},{4,8},{8,12},{12,16},{16,20},{20,24},{24,28},{28,0},{32,36},... | collective-permute-start | bytes 786440 | tf_op jit(solution)/shard_map/ppermute | solution.py:39
  4.8 11.7 %collective-permute-start.1 = (bf16[512,256]{1,0:T(8,128)(2,1)}, bf16[512,256]{1,0:T(8,128)(2,1)S(1)}, u32[]{:S(2)}, u32[]{:S(2)}) collective-permute-start(bf16[512,256]{1,0:T(8,128)(2,1)} %get-tuple-element.15.refs_0_), channel_id=1, source_target_pairs={{0,28},{4,0},{8,4},{12,8},{16,12},{20,16},{24,20},{28,24},{32,60},... | collective-permute-start | bytes 786440 | tf_op jit(solution)/shard_map/ppermute | solution.py:40
  8.8 28.2 %copy-start.2 = (bf16[4,16,1024]{2,1,0:T(8,128)(2,1)S(1)}, bf16[4,16,1024]{2,1,0:T(8,128)(2,1)}, u32[]{:S(2)}) copy-start(bf16[4,16,1024]{2,1,0:T(8,128)(2,1)} %param.14) | copy-start | bytes 393220
  8.8 28.2 %copy-start.5 = (s32[2,128]{1,0:T(2,128)S(1)}, s32[2,128]{1,0:T(2,128)}, u32[]{:S(2)}) copy-start(s32[2,128]{1,0:T(2,128)} %slot_ref.1) | copy-start | bytes 3076
  8.8 28.2 %copy-start.6 = (s32[2]{0:T(128)S(1)}, s32[2]{0:T(128)}, u32[]{:S(2)}) copy-start(s32[2]{0:T(128)} %row_count_ref.1) | copy-start | bytes 28
  8.8 31.0 %copy-start.1 = (bf16[512,256]{1,0:T(8,128)(2,1)S(1)}, bf16[512,256]{1,0:T(8,128)(2,1)}, u32[]{:S(2)}) copy-start(bf16[512,256]{1,0:T(8,128)(2,1)} %get-tuple-element.15.refs_0_) | copy-start | bytes 786436
  8.8 31.0 %all-to-all-start = ((bf16[8,256,256]{2,1,0:T(8,128)(2,1)}), bf16[8,256,256]{2,1,0:T(8,128)(2,1)S(1)}, u32[]{:S(2)}, u32[]{:S(2)}) async-start(bf16[8,256,256]{2,1,0:T(8,128)(2,1)} %get-tuple-element.12), calls=%async_computation | async-start | bytes 2097152 | tf_op jit(solution)/shard_map/all_to_all | solution.py:523
  16.4 8.4 %collective-permute-start.2 = (bf16[512,256]{1,0:T(8,128)(2,1)S(1)}, bf16[512,256]{1,0:T(8,128)(2,1)S(1)}, u32[]{:S(2)}, u32[]{:S(2)}) collective-permute-start(bf16[512,256]{1,0:T(8,128)(2,1)S(1)} %collective-permute-done.refs_1_), channel_id=1, source_target_pairs={{0,4},{4,8},{8,12},{12,16},{16,20},{20,24},{24,28},{28,0},{32,36},... | collective-permute-start | bytes 786440 | tf_op jit(solution)/shard_map/ppermute | solution.py:39
  16.4 8.4 %collective-permute-start.3 = (bf16[512,256]{1,0:T(8,128)(2,1)S(1)}, bf16[512,256]{1,0:T(8,128)(2,1)S(1)}, u32[]{:S(2)}, u32[]{:S(2)}) collective-permute-start(bf16[512,256]{1,0:T(8,128)(2,1)S(1)} %collective-permute-done.1.refs_2_), channel_id=1, source_target_pairs={{0,28},{4,0},{8,4},{12,8},{16,12},{20,16},{24,20},{28,24},{32,60},... | collective-permute-start | bytes 786440 | tf_op jit(solution)/shard_map/ppermute | solution.py:40
  24.8 7.6 %collective-permute-start.4 = (bf16[512,256]{1,0:T(8,128)(2,1)S(1)}, bf16[512,256]{1,0:T(8,128)(2,1)S(1)}, u32[]{:S(2)}, u32[]{:S(2)}) collective-permute-start(bf16[512,256]{1,0:T(8,128)(2,1)S(1)} %collective-permute-done.2.refs_3_), channel_id=1, source_target_pairs={{0,4},{4,8},{8,12},{12,16},{16,20},{20,24},{24,28},{28,0},{32,36},... | collective-permute-start | bytes 786440 | tf_op jit(solution)/shard_map/ppermute | solution.py:39
  24.9 8.2 %collective-permute-start.5 = (bf16[512,256]{1,0:T(8,128)(2,1)S(1)}, bf16[512,256]{1,0:T(8,128)(2,1)S(1)}, u32[]{:S(2)}, u32[]{:S(2)}) collective-permute-start(bf16[512,256]{1,0:T(8,128)(2,1)S(1)} %collective-permute-done.3.refs_4_), channel_id=1, source_target_pairs={{0,28},{4,0},{8,4},{12,8},{16,12},{20,16},{24,20},{28,24},{32,60},... | collective-permute-start | bytes 786440 | tf_op jit(solution)/shard_map/ppermute | solution.py:40
  33.1 6.4 %collective-permute-start.6 = (bf16[256,256]{1,0:T(8,128)(2,1)}, bf16[256,256]{1,0:T(8,128)(2,1)S(1)}, u32[]{:S(2)}, u32[]{:S(2)}) collective-permute-start(bf16[256,256]{1,0:T(8,128)(2,1)} %slice.12), channel_id=1, source_target_pairs={{0,4},{4,8},{8,12},{12,16},{16,20},{20,24},{24,28},{28,0},{32,36},... | collective-permute-start | bytes 393224 | tf_op jit(solution)/shard_map/ppermute | solution.py:43
  33.8 6.1 %collective-permute-start.7 = (bf16[256,256]{1,0:T(8,128)(2,1)}, bf16[256,256]{1,0:T(8,128)(2,1)S(1)}, u32[]{:S(2)}, u32[]{:S(2)}) collective-permute-start(bf16[256,256]{1,0:T(8,128)(2,1)} %slice.13), channel_id=1, source_target_pairs={{0,28},{4,0},{8,4},{12,8},{16,12},{20,16},{24,20},{28,24},{32,60},... | collective-permute-start | bytes 393224 | tf_op jit(solution)/shard_map/ppermute | solution.py:44
  62.6 21.3 %copy-start.3 = (bf16[256,256]{1,0:T(8,128)(2,1)S(1)}, bf16[256,256]{1,0:T(8,128)(2,1)}, u32[]{:S(2)}) copy-start(bf16[256,256]{1,0:T(8,128)(2,1)} %residual_ref.1) | copy-start | bytes 393220
  102.2 15.7 %copy-start = (bf16[256,1024]{1,0:T(8,128)(2,1)S(1)}, bf16[256,1024]{1,0:T(8,128)(2,1)}, u32[]{:S(2)}) copy-start(bf16[256,1024]{1,0:T(8,128)(2,1)} %weight_ref.3) | copy-start | bytes 1572868
  102.2 15.7 %copy-start.4 = (s32[128]{0:T(128)S(1)}, s32[128]{0:T(128)}, u32[]{:S(2)}) copy-start(s32[128]{0:T(128)} %track_ref.3) | copy-start | bytes 1540
  124.8 1.3 collective-permute-start.8
  126.1 4.4 %collective-permute-start.9 = (bf16[16,2048]{1,0:T(8,128)(2,1)S(1)}, bf16[16,2048]{1,0:T(8,128)(2,1)S(1)}, u32[]{:S(2)}, u32[]{:S(2)}) collective-permute-start(bf16[16,2048]{1,0:T(8,128)(2,1)S(1)} %add_convert_fusion.part_ref), channel_id=1, source_target_pairs={{0,2},{2,0},{1,3},{3,1},{4,6},{6,4},{5,7},{7,5},{8,10},{10,8},{9,1... | collective-permute-start | bytes 196616 | tf_op jit(solution)/shard_map/ppermute | solution.py:542

commit v11 on v10

--- a/solution.py
+++ b/solution.py
@@ -290,7 +290,7 @@
     weight_buf,
 ):
     step = every_ref.shape[1]
-    at = pl.program_id(0) * 2
+    at = pl.program_id(0) * 4
 
     @pl.when(at == 0)
     def _():
@@ -315,9 +315,9 @@
                 ).astype(jnp.float32)
         weight_buf[...] = weight_ref[...].T
 
-    here = jnp.concatenate([column(id_buf[pl.ds(at + i, 1)]) for i in range(2)], axis=0)
+    here = jnp.concatenate([column(id_buf[pl.ds(at + i, 1)]) for i in range(4)], axis=0)
     sums = jnp.zeros(mean_ref.shape, jnp.float32)
-    counts = jnp.zeros((2 * step, step), jnp.float32)
+    counts = jnp.zeros((4 * step, step), jnp.float32)
     for g in range(SIDE):
         match = here == id_buf[g : g + 1]
         sums = sums + jnp.dot(
@@ -327,10 +327,10 @@
         )
         seen = count_buf[g : g + 1] + jnp.where(g < at, EARLIER, 0.0)
         counts = counts + jnp.where(match, seen, 0.0)
-    below = lax.broadcasted_iota(jnp.int32, (2 * step, step), 0) - lax.broadcasted_iota(
-        jnp.int32, (2 * step, step), 1
+    below = lax.broadcasted_iota(jnp.int32, (4 * step, step), 0) - lax.broadcasted_iota(
+        jnp.int32, (4 * step, step), 1
     )
-    for i in range(2):
+    for i in range(4):
         match = (here == id_buf[pl.ds(at + i, 1)]) & (below > i * step)
         counts = counts + jnp.where(match, EARLIER, 0.0)
     total = jnp.sum(counts, axis=1, keepdims=True)
@@ -356,16 +356,16 @@
         track_kernel,
         grid_spec=pltpu.PrefetchScalarGridSpec(
             num_scalar_prefetch=2,
-            grid=(SIDE // 2,),
+            grid=(SIDE // 4,),
             in_specs=[
                 pl.BlockSpec(every.shape, lambda i, t, at: (0, 0, 0)),
                 pl.BlockSpec(both.shape, lambda i, t, at: (0, 0, 0)),
                 pl.BlockSpec((width, 128), lambda i, t, at: (0, at[0] // (128 // chunk))),
             ],
             out_specs=[
-                pl.BlockSpec((2 * step, width), lambda i, t, at: (i, 0)),
-                pl.BlockSpec((chunk, 2 * step), lambda i, t, at: (0, i)),
-                pl.BlockSpec((2 * step, 128), lambda i, t, at: (i, 0)),
+                pl.BlockSpec((4 * step, width), lambda i, t, at: (i, 0)),
+                pl.BlockSpec((chunk, 4 * step), lambda i, t, at: (0, i)),
+                pl.BlockSpec((4 * step, 128), lambda i, t, at: (i, 0)),
             ],
             scratch_shapes=[
                 pltpu.VMEM((SIDE, step), jnp.float32),

time: 159 us -> 158 us (level)
  no operation moved by 1% of the time
where the time goes in v11:
time: 158 us
  blocking collectives  78.2 us (49%)
  Pallas kernels  37.1 us (23%)
  starting transfers between devices  24.1 us (15%)
  waiting for transfers between devices  16.3 us (10%)
    pallas_call x1, Pallas kernels, attend(): pl.pallas_call(attend_kernel, grid=(pairs, SIDE // 2), in_specs=[pl.Block...  22.7 us
    all_to_all x1, blocking collectives, local(): part = lax.all_to_all(part, 'seq', 0, 0, axis_index_groups=GROUP_YX)  21.3 us
    all_to_all x1, blocking collectives, local(): both = lax.all_to_all(both, 'seq', 0, 0, axis_index_groups=GROUP_Z)  16.7 us
    all_to_all x1, blocking collectives, spread(): return lax.all_to_all(wide, 'seq', 0, 0, axis_index_groups=groups)  15.7 us
    all_to_all x1, blocking collectives, local(): lax.all_to_all(relay(final), 'seq', 0, 0, axis_index_groups=GROUP_YX)  13.1 us
    all_to_all x1, blocking collectives, local(): final = lax.all_to_all(final, 'seq', 0, 0, axis_index_groups=GROUP_Z)  11.5 us
    ppermute x3, starting transfers between devices, gather_ring(): down = lax.ppermute(down, 'seq', ring(seq_count, -1))  10.5 us
    ppermute x3, waiting for transfers between devices, gather_ring(): up = lax.ppermute(up, 'seq', ring(seq_count, 1))  9.52 us
  transfers between devices with their start and end apart: 11, of which 6 were waited for; matrix products, arithmetic and copies ran while one was open for 1% of the time, Pallas kernels for 1%

profile of v11, /device:TPU:2, one launch (start us, length us, event | category | flops | bytes accessed | tf_op | source)
XLA Modules:
  0.0 157.9 jit_solution(7973174883214383691)
XLA Ops:
  0.6 2.1 %lay_out.1 = (bf16[512,256]{1,0:T(8,128)(2,1)}, bf16[8,256,256]{2,1,0:T(8,128)(2,1)}) custom-call(bf16[256,256]{1,0:T(8,128)(2,1)} %k_ref.1, bf16[256,256]{1,0:T(8,128)(2,1)} %v_ref.1, bf16[256,256]{1,0:T(8,128)(2,1)} %q_ref.1), custom_call_target="tpu_custom_call" | custom-call | tf_op jit(solution)/shard_map/lay_out/pallas_call | solution.py:65
  2.8 2.0 %collective-permute-start = (bf16[512,256]{1,0:T(8,128)(2,1)}, bf16[512,256]{1,0:T(8,128)(2,1)S(1)}, u32[]{:S(2)}, u32[]{:S(2)}) collective-permute-start(bf16[512,256]{1,0:T(8,128)(2,1)} %get-tuple-element.15.refs_0_), channel_id=1, source_target_pairs={{0,4},{4,8},{8,12},{12,16},{16,20},{20,24},{24,28},{28,0},{32,36},... | collective-permute-start | bytes 786440 | tf_op jit(solution)/shard_map/ppermute | solution.py:39
  4.8 4.0 %collective-permute-start.1 = (bf16[512,256]{1,0:T(8,128)(2,1)}, bf16[512,256]{1,0:T(8,128)(2,1)S(1)}, u32[]{:S(2)}, u32[]{:S(2)}) collective-permute-start(bf16[512,256]{1,0:T(8,128)(2,1)} %get-tuple-element.15.refs_0_), channel_id=1, source_target_pairs={{0,28},{4,0},{8,4},{12,8},{16,12},{20,16},{24,20},{28,24},{32,60},... | collective-permute-start | bytes 786440 | tf_op jit(solution)/shard_map/ppermute | solution.py:40
  8.8 7.6 %all-to-all-start = ((bf16[8,256,256]{2,1,0:T(8,128)(2,1)}), bf16[8,256,256]{2,1,0:T(8,128)(2,1)S(1)}, u32[]{:S(2)}, u32[]{:S(2)}) async-start(bf16[8,256,256]{2,1,0:T(8,128)(2,1)} %get-tuple-element.12), calls=%async_computation | async-start | bytes 2097152 | tf_op jit(solution)/shard_map/all_to_all | solution.py:523
  16.4 3.2 %collective-permute-start.3 = (bf16[512,256]{1,0:T(8,128)(2,1)S(1)}, bf16[512,256]{1,0:T(8,128)(2,1)S(1)}, u32[]{:S(2)}, u32[]{:S(2)}) collective-permute-start(bf16[512,256]{1,0:T(8,128)(2,1)S(1)} %collective-permute-done.1.refs_2_), channel_id=1, source_target_pairs={{0,28},{4,0},{8,4},{12,8},{16,12},{20,16},{24,20},{28,24},{32,60},... | collective-permute-start | bytes 786440 | tf_op jit(solution)/shard_map/ppermute | solution.py:40
  19.7 5.2 %collective-permute-done.2.refs_3_ = bf16[512,256]{1,0:T(8,128)(2,1)S(1)} collective-permute-done((bf16[512,256]{1,0:T(8,128)(2,1)S(1)}, bf16[512,256]{1,0:T(8,128)(2,1)S(1)}, u32[]{:S(2)}, u32[]{:S(2)}) %collective-permute-start.2) | collective-permute-done | bytes 262176 | tf_op jit(solution)/shard_map/ppermute | solution.py:39
  24.9 3.2 %collective-permute-start.5 = (bf16[512,256]{1,0:T(8,128)(2,1)S(1)}, bf16[512,256]{1,0:T(8,128)(2,1)S(1)}, u32[]{:S(2)}, u32[]{:S(2)}) collective-permute-start(bf16[512,256]{1,0:T(8,128)(2,1)S(1)} %collective-permute-done.3.refs_4_), channel_id=1, source_target_pairs={{0,28},{4,0},{8,4},{12,8},{16,12},{20,16},{24,20},{28,24},{32,60},... | collective-permute-start | bytes 786440 | tf_op jit(solution)/shard_map/ppermute | solution.py:40
  28.1 4.3 %collective-permute-done.4.refs_5_ = bf16[512,256]{1,0:T(8,128)(2,1)S(1)} collective-permute-done((bf16[512,256]{1,0:T(8,128)(2,1)S(1)}, bf16[512,256]{1,0:T(8,128)(2,1)S(1)}, u32[]{:S(2)}, u32[]{:S(2)}) %collective-permute-start.4) | collective-permute-done | bytes 262176 | tf_op jit(solution)/shard_map/ppermute | solution.py:39
  32.4 0.7 slice.12
  33.1 0.7 slice.13
  33.8 3.2 %collective-permute-start.7 = (bf16[256,256]{1,0:T(8,128)(2,1)}, bf16[256,256]{1,0:T(8,128)(2,1)S(1)}, u32[]{:S(2)}, u32[]{:S(2)}) collective-permute-start(bf16[256,256]{1,0:T(8,128)(2,1)} %slice.13), channel_id=1, source_target_pairs={{0,28},{4,0},{8,4},{12,8},{16,12},{20,16},{24,20},{28,24},{32,60},... | collective-permute-start | bytes 393224 | tf_op jit(solution)/shard_map/ppermute | solution.py:44
  37.0 0.9 prepare.1
  37.9 1.6 collective-permute-done.6.refs_7_
  39.5 0.3 collective-permute-done.7.refs_8_
  39.8 22.7 %attend.1 = bf16[8,304,256]{2,1,0:T(8,128)(2,1)S(1)} custom-call(bf16[2048,256]{1,0:T(8,128)(2,1)S(1)} %bitcast.4, bf16[8,32,256]{2,1,0:T(8,128)(2,1)S(1)} %get-tuple-element.13.piece_ref, f32[1,128]{1,0:T(1,128)S(1)} %get-tuple-element.14.count_ref, bf16[512,256]{1,0:T(8,128)(2,1)S(1)} %copy-done.1, bf16[512,256]{1,0:T(8,128)(2,1)S(1)} %collective-permute-done.refs_1_, ...), custom_call_target="tpu_custom_call" | custom-call | tf_op jit(solution)/shard_map/attend/pallas_call | solution.py:184
  62.6 21.3 %all_to_all.30.part_ref = bf16[8,304,256]{2,1,0:T(8,128)(2,1)S(1)} all-to-all(bf16[8,304,256]{2,1,0:T(8,128)(2,1)S(1)} %attend.1), channel_id=1, replica_groups={{0,32,64,96,128,160,192,224},{4,36,68,100,132,164,196,228},{8,40,72,104..., dimensions={0} | all-to-all | bytes 2490368 | tf_op jit(solution)/shard_map/all_to_all | solution.py:531
  83.9 1.5 merge.1
  85.4 16.7 %all_to_all.31.both_ref = bf16[8,80,256]{2,1,0:T(8,128)(2,1)S(1)} all-to-all(bf16[8,80,256]{2,1,0:T(8,128)(2,1)S(1)} %merge.1), channel_id=1, replica_groups={{0,4,8,12,16,20,24,28},{32,36,40,44,48,52,56,60},{64,68,72,76,80,84,88,..., dimensions={0} | all-to-all | bytes 655360 | tf_op jit(solution)/shard_map/all_to_all | solution.py:533
  102.1 0.1 broadcast_in_dim.8
  102.2 0.0 copy-start
  102.2 0.0 copy-start.4
  102.2 15.7 %all_to_all.32.every_ref = bf16[8,256,256]{2,1,0:T(8,128)(2,1)S(1)} all-to-all(bf16[8,256,256]{2,1,0:T(8,128)(2,1)S(1)} %broadcast_in_dim.8), channel_id=1, replica_groups={{0,32,64,96,128,160,192,224},{4,36,68,100,132,164,196,228},{8,40,72,104..., dimensions={0} | all-to-all | bytes 2097152 | tf_op jit(solution)/shard_map/all_to_all | solution.py:25
  117.9 6.2 %track_means.1 = (bf16[2048,256]{1,0:T(8,128)(2,1)S(1)}, bf16[16,2048]{1,0:T(8,128)(2,1)S(1)}, f32[2048,128]{1,0:T(8,128)S(1)}) custom-call(s32[128]{0:T(128)S(1)} %copy-done.4, s32[1]{0:T(128)} %bitcast.2.index_ref, bf16[8,256,256]{2,1,0:T(8,128)(2,1)S(1)} %all_to_all.32.every_ref, bf16[8,80,256]{2,1,0:T(8,128)(2,1)S(1)} %all_to_all.31.both_ref, ...), custom_call_target="tpu_custom_call" | custom-call | tf_op jit(solution)/shard_map/track_means/pallas_call | solution.py:355
  124.1 0.1 collective-permute-start.8
  124.1 1.2 collective-permute-done.8
  125.4 0.8 collective-permute-start.9
  126.2 3.6 %collective-permute-done.9.other_ref = bf16[16,2048]{1,0:T(8,128)(2,1)S(1)} collective-permute-done((bf16[16,2048]{1,0:T(8,128)(2,1)S(1)}, bf16[16,2048]{1,0:T(8,128)(2,1)S(1)}, u32[]{:S(2)}, u32[]{:S(2)}) %collective-permute-start.9) | collective-permute-done | bytes 65568 | tf_op jit(solution)/shard_map/ppermute | solution.py:542
  129.8 2.0 %error_messages.1 = bf16[8,32,256]{2,1,0:T(8,128)(2,1)S(1)} custom-call(s32[128]{0:T(128)S(1)} %copy-done.4, bf16[16,2048]{1,0:T(8,128)(2,1)S(1)} %add_convert_fusion.part_ref, bf16[16,2048]{1,0:T(8,128)(2,1)S(1)} %collective-permute-done.9.other_ref, bf16[8,80,256]{2,1,0:T(8,128)(2,1)S(1)} %all_to_all.31.both_ref, ...), custom_call_target="tpu_custom_call" | custom-call | tf_op jit(solution)/shard_map/error_messages/pallas_call | solution.py:431
  131.8 11.5 %all_to_all.33.in_ref = bf16[8,32,256]{2,1,0:T(8,128)(2,1)S(1)} all-to-all(bf16[8,32,256]{2,1,0:T(8,128)(2,1)S(1)} %error_messages.1), channel_id=1, replica_groups={{0,4,8,12,16,20,24,28},{32,36,40,44,48,52,56,60},{64,68,72,76,80,84,88,..., dimensions={0} | all-to-all | bytes 262144 | tf_op jit(solution)/shard_map/all_to_all | solution.py:544
  143.3 0.1 relay.1
  143.4 13.1 %all_to_all.34.final_ref = bf16[8,144,256]{2,1,0:T(8,128)(2,1)S(1)} all-to-all(bf16[8,144,256]{2,1,0:T(8,128)(2,1)S(1)} %relay.1), channel_id=1, replica_groups={{0,32,64,96,128,160,192,224},{4,36,68,100,132,164,196,228},{8,40,72,104..., dimensions={0} | all-to-all | bytes 1179648 | tf_op jit(solution)/shard_map/all_to_all | solution.py:545
  156.5 1.4 finish.1
  (22 shorter events, 0.1 us)
Async XLA Ops:
  2.8 13.6 %collective-permute-start = (bf16[512,256]{1,0:T(8,128)(2,1)}, bf16[512,256]{1,0:T(8,128)(2,1)S(1)}, u32[]{:S(2)}, u32[]{:S(2)}) collective-permute-start(bf16[512,256]{1,0:T(8,128)(2,1)} %get-tuple-element.15.refs_0_), channel_id=1, source_target_pairs={{0,4},{4,8},{8,12},{12,16},{16,20},{20,24},{24,28},{28,0},{32,36},... | collective-permute-start | bytes 786440 | tf_op jit(solution)/shard_map/ppermute | solution.py:39
  4.8 11.7 %collective-permute-start.1 = (bf16[512,256]{1,0:T(8,128)(2,1)}, bf16[512,256]{1,0:T(8,128)(2,1)S(1)}, u32[]{:S(2)}, u32[]{:S(2)}) collective-permute-start(bf16[512,256]{1,0:T(8,128)(2,1)} %get-tuple-element.15.refs_0_), channel_id=1, source_target_pairs={{0,28},{4,0},{8,4},{12,8},{16,12},{20,16},{24,20},{28,24},{32,60},... | collective-permute-start | bytes 786440 | tf_op jit(solution)/shard_map/ppermute | solution.py:40
  8.8 28.2 %copy-start.2 = (bf16[4,16,1024]{2,1,0:T(8,128)(2,1)S(1)}, bf16[4,16,1024]{2,1,0:T(8,128)(2,1)}, u32[]{:S(2)}) copy-start(bf16[4,16,1024]{2,1,0:T(8,128)(2,1)} %param.14) | copy-start | bytes 393220
  8.8 28.2 %copy-start.5 = (s32[2,128]{1,0:T(2,128)S(1)}, s32[2,128]{1,0:T(2,128)}, u32[]{:S(2)}) copy-start(s32[2,128]{1,0:T(2,128)} %slot_ref.1) | copy-start | bytes 3076
  8.8 28.2 %copy-start.6 = (s32[2]{0:T(128)S(1)}, s32[2]{0:T(128)}, u32[]{:S(2)}) copy-start(s32[2]{0:T(128)} %row_count_ref.1) | copy-start | bytes 28
  8.8 31.0 %copy-start.1 = (bf16[512,256]{1,0:T(8,128)(2,1)S(1)}, bf16[512,256]{1,0:T(8,128)(2,1)}, u32[]{:S(2)}) copy-start(bf16[512,256]{1,0:T(8,128)(2,1)} %get-tuple-element.15.refs_0_) | copy-start | bytes 786436
  8.8 31.0 %all-to-all-start = ((bf16[8,256,256]{2,1,0:T(8,128)(2,1)}), bf16[8,256,256]{2,1,0:T(8,128)(2,1)S(1)}, u32[]{:S(2)}, u32[]{:S(2)}) async-start(bf16[8,256,256]{2,1,0:T(8,128)(2,1)} %get-tuple-element.12), calls=%async_computation | async-start | bytes 2097152 | tf_op jit(solution)/shard_map/all_to_all | solution.py:523
  16.4 8.4 %collective-permute-start.2 = (bf16[512,256]{1,0:T(8,128)(2,1)S(1)}, bf16[512,256]{1,0:T(8,128)(2,1)S(1)}, u32[]{:S(2)}, u32[]{:S(2)}) collective-permute-start(bf16[512,256]{1,0:T(8,128)(2,1)S(1)} %collective-permute-done.refs_1_), channel_id=1, source_target_pairs={{0,4},{4,8},{8,12},{12,16},{16,20},{20,24},{24,28},{28,0},{32,36},... | collective-permute-start | bytes 786440 | tf_op jit(solution)/shard_map/ppermute | solution.py:39
  16.4 8.4 %collective-permute-start.3 = (bf16[512,256]{1,0:T(8,128)(2,1)S(1)}, bf16[512,256]{1,0:T(8,128)(2,1)S(1)}, u32[]{:S(2)}, u32[]{:S(2)}) collective-permute-start(bf16[512,256]{1,0:T(8,128)(2,1)S(1)} %collective-permute-done.1.refs_2_), channel_id=1, source_target_pairs={{0,28},{4,0},{8,4},{12,8},{16,12},{20,16},{24,20},{28,24},{32,60},... | collective-permute-start | bytes 786440 | tf_op jit(solution)/shard_map/ppermute | solution.py:40
  24.8 7.6 %collective-permute-start.4 = (bf16[512,256]{1,0:T(8,128)(2,1)S(1)}, bf16[512,256]{1,0:T(8,128)(2,1)S(1)}, u32[]{:S(2)}, u32[]{:S(2)}) collective-permute-start(bf16[512,256]{1,0:T(8,128)(2,1)S(1)} %collective-permute-done.2.refs_3_), channel_id=1, source_target_pairs={{0,4},{4,8},{8,12},{12,16},{16,20},{20,24},{24,28},{28,0},{32,36},... | collective-permute-start | bytes 786440 | tf_op jit(solution)/shard_map/ppermute | solution.py:39
  24.9 8.2 %collective-permute-start.5 = (bf16[512,256]{1,0:T(8,128)(2,1)S(1)}, bf16[512,256]{1,0:T(8,128)(2,1)S(1)}, u32[]{:S(2)}, u32[]{:S(2)}) collective-permute-start(bf16[512,256]{1,0:T(8,128)(2,1)S(1)} %collective-permute-done.3.refs_4_), channel_id=1, source_target_pairs={{0,28},{4,0},{8,4},{12,8},{16,12},{20,16},{24,20},{28,24},{32,60},... | collective-permute-start | bytes 786440 | tf_op jit(solution)/shard_map/ppermute | solution.py:40
  33.1 6.4 %collective-permute-start.6 = (bf16[256,256]{1,0:T(8,128)(2,1)}, bf16[256,256]{1,0:T(8,128)(2,1)S(1)}, u32[]{:S(2)}, u32[]{:S(2)}) collective-permute-start(bf16[256,256]{1,0:T(8,128)(2,1)} %slice.12), channel_id=1, source_target_pairs={{0,4},{4,8},{8,12},{12,16},{16,20},{20,24},{24,28},{28,0},{32,36},... | collective-permute-start | bytes 393224 | tf_op jit(solution)/shard_map/ppermute | solution.py:43
  33.8 6.1 %collective-permute-start.7 = (bf16[256,256]{1,0:T(8,128)(2,1)}, bf16[256,256]{1,0:T(8,128)(2,1)S(1)}, u32[]{:S(2)}, u32[]{:S(2)}) collective-permute-start(bf16[256,256]{1,0:T(8,128)(2,1)} %slice.13), channel_id=1, source_target_pairs={{0,28},{4,0},{8,4},{12,8},{16,12},{20,16},{24,20},{28,24},{32,60},... | collective-permute-start | bytes 393224 | tf_op jit(solution)/shard_map/ppermute | solution.py:44
  62.6 21.3 %copy-start.3 = (bf16[256,256]{1,0:T(8,128)(2,1)S(1)}, bf16[256,256]{1,0:T(8,128)(2,1)}, u32[]{:S(2)}) copy-start(bf16[256,256]{1,0:T(8,128)(2,1)} %residual_ref.1) | copy-start | bytes 393220
  102.2 15.7 %copy-start = (bf16[256,1024]{1,0:T(8,128)(2,1)S(1)}, bf16[256,1024]{1,0:T(8,128)(2,1)}, u32[]{:S(2)}) copy-start(bf16[256,1024]{1,0:T(8,128)(2,1)} %weight_ref.3) | copy-start | bytes 1572868
  102.2 15.7 %copy-start.4 = (s32[128]{0:T(128)S(1)}, s32[128]{0:T(128)}, u32[]{:S(2)}) copy-start(s32[128]{0:T(128)} %track_ref.3) | copy-start | bytes 1540
  124.1 1.3 collective-permute-start.8
  125.4 4.4 %collective-permute-start.9 = (bf16[16,2048]{1,0:T(8,128)(2,1)S(1)}, bf16[16,2048]{1,0:T(8,128)(2,1)S(1)}, u32[]{:S(2)}, u32[]{:S(2)}) collective-permute-start(bf16[16,2048]{1,0:T(8,128)(2,1)S(1)} %add_convert_fusion.part_ref), channel_id=1, source_target_pairs={{0,2},{2,0},{1,3},{3,1},{4,6},{6,4},{5,7},{7,5},{8,10},{10,8},{9,1... | collective-permute-start | bytes 196616 | tf_op jit(solution)/shard_map/ppermute | solution.py:542
